TPU v7x, 32 devices: a whole 2x2x4 slice. The times are simulated.
32 devices in a mesh: row: 8 (over y, x, core), col: 4 (over z).
Axes of the slice: x: 2, y: 2, z: 4, core: 2. Of those that a mesh axis runs over, the one named last changes fastest.
Arguments:
- tokens: bfloat16 [8192, 2048], P(('row', 'col')), may hold values from -6 to 6
- out_grad: bfloat16 [8192, 2048], P(('row', 'col')), may hold values from -6 to 6
- segments: int32 [8, 1024], P('row'), may hold values from 0 to 2, as said below
- routes: int32 [8192, 8], P(('row', 'col')), may hold values from 0 to 63, all different within a row; in each aligned block of 256 rows (0 to 255, 256 to 511, ...) at most 48 rows name the same one
- attn_gain: float32 [2048], replicated, may hold values from 0.25 to 1.75
- ffn_gain: float32 [2048], replicated, may hold values from 0.25 to 1.75
- query_gain: float32 [2048], P('col'), may hold values from 0.25 to 1.75
- key_gain: float32 [2048], P('col'), may hold values from 0.25 to 1.75
- w_query: bfloat16 [2048, 2048], P('row', 'col'), may hold values from -0.125 to 0.125
- w_key: bfloat16 [2048, 2048], P('row', 'col'), may hold values from -0.125 to 0.125
- w_value: bfloat16 [2048, 2048], P('row', 'col'), may hold values from -0.125 to 0.125
- w_out: bfloat16 [2048, 2048], P('col', 'row'), may hold values from -0.75 to 0.75
- router: bfloat16 [2048, 64], replicated, may hold values from -0.0625 to 0.0625
- w_gate: bfloat16 [2048, 65536], P(None, ('row', 'col')), may hold values from -0.125 to 0.125
- w_up: bfloat16 [2048, 65536], P(None, ('row', 'col')), may hold values from -0.125 to 0.125
- w_down: bfloat16 [65536, 2048], P(('row', 'col')), may hold values from -4 to 4
Outputs:
- output: bfloat16 [8192, 2048], P(('row', 'col'))
- input_grad: float32 [8192, 2048], P(('row', 'col'))
- attn_gain_grad: float32 [2048], replicated
- ffn_gain_grad: float32 [2048], replicated
- query_gain_grad: float32 [2048], P('col')
- key_gain_grad: float32 [2048], P('col')
- query_grad: float32 [2048, 2048], P('row', 'col')
- key_grad: float32 [2048, 2048], P('row', 'col')
- value_grad: float32 [2048, 2048], P('row', 'col')
- out_proj_grad: float32 [2048, 2048], P('col', 'row')
- router_grad: float32 [2048, 64], replicated
- gate_grad: float32 [2048, 65536], P(None, ('row', 'col'))
- up_grad: float32 [2048, 65536], P(None, ('row', 'col'))
- down_grad: float32 [65536, 2048], P(('row', 'col'))
Inputs may be any that keep to these rules, and one draw needn't show every extreme that they name: `routes`: each token names 8 different experts; among the 256 tokens of one device (aligned blocks of 256 rows) no expert is named by more than 48 tokens, a bound that some block reaches. `segments`: never falling along a sequence.
All inputs are finite; a program needn't handle non-finite values.
Results may differ from a plain program's by a relative error of at most 0.02.
Values may be sent and summed in bfloat16 or wider, within the bound.
No kernel may reach another device: no remote copies, remote signals or barrier semaphores. Data moves between devices by JAX's collectives and lax.ppermute only.
A program may use at most 384 MiB of HBM per device.

v0:
```python
import jax
import jax.numpy as jnp
from jax import lax
from jax.sharding import PartitionSpec as P

D = 2048
HEAD_DIM = 128
FF = 1024


EPSILON = 1e-05
ROPE_BASE = 10000.0
MASKED = -1e30


def rms_scale(values):
    return lax.rsqrt(jnp.mean(values * values, -1, keepdims=True) + EPSILON)


def norm_back(values, scale, gain, grad_in):
    scaled_grad = grad_in * gain
    gain_grad = jnp.sum(grad_in * values * scale, 0)
    value_grad = scale * scaled_grad - values * scale * scale * scale * jnp.mean(
        scaled_grad * values, -1, keepdims=True
    )
    return (value_grad, gain_grad)


def times_t(left, right):
    return lax.dot_general(
        left, right, (((1,), (1,)), ((), ())), preferred_element_type=jnp.float32
    )


def rope_tables(length, head_size):
    half = head_size // 2
    freq = jnp.exp(jnp.arange(half, dtype=jnp.float32) * (-2.0 * jnp.log(ROPE_BASE) / head_size))
    angles = jnp.arange(length, dtype=jnp.float32)[:, None] * freq[None, :]
    return (jnp.cos(angles)[:, None, :], jnp.sin(angles)[:, None, :])


def rotate(values, cosines, sine_table):
    half = values.shape[-1] // 2
    first, second = (values[..., :half], values[..., half:])
    return jnp.concatenate(
        [first * cosines - second * sine_table, second * cosines + first * sine_table], -1
    )


def rotate_back(grads, cosines, sine_table):
    half = grads.shape[-1] // 2
    first, second = (grads[..., :half], grads[..., half:])
    return jnp.concatenate(
        [first * cosines + second * sine_table, second * cosines - first * sine_table], -1
    )


def score_block(query_heads, key_heads, doc_ids, row_start, row_stop, factor):
    scores = (
        jnp.einsum(
            "qhd,khd->hqk",
            query_heads[row_start:row_stop],
            key_heads[:row_stop],
            preferred_element_type=jnp.float32,
        )
        * factor
    )
    query_pos = row_start + jnp.arange(row_stop - row_start)[:, None]
    key_pos = jnp.arange(row_stop)[None, :]
    allowed = (key_pos <= query_pos) & (
        doc_ids[row_start:row_stop][:, None] == doc_ids[:row_stop][None, :]
    )
    return jnp.where(allowed[None], scores, MASKED)


def to_owners(table, experts, devices, capacity):
    width = table.shape[-1]
    if devices <= experts:
        return table.reshape(devices, experts // devices, capacity, width)
    grouped = table.reshape(experts, 1, capacity, width)
    return jnp.broadcast_to(grouped, (experts, devices // experts, capacity, width)).reshape(
        devices, 1, capacity, width
    )


def from_owners(returned, experts, capacity):
    devices = returned.shape[0]
    width = returned.shape[-1]
    widened = returned.astype(jnp.float32)
    if devices <= experts:
        return widened.reshape(experts * capacity, width)
    return jnp.sum(widened.reshape(experts, devices // experts, capacity, width), 1).reshape(
        experts * capacity, width
    )


def local(
    tokens,
    out_grad,
    segments,
    routes,
    attn_gain,
    ffn_gain,
    query_gain,
    key_gain,
    w_query,
    w_key,
    w_value,
    w_out,
    router,
    w_gate,
    w_up,
    w_down,
):
    rows_total = lax.axis_size("row")
    devices = rows_total * lax.axis_size("col")
    tok_count, width = tokens.shape
    top_count = routes.shape[1]
    expert_count = router.shape[1]
    capacity = tok_count * top_count * 3 // (expert_count * 2)
    local_units = w_gate.shape[1]
    piece_width = min(local_units, FF)
    owned = local_units // piece_width
    head_cols = w_query.shape[1]
    heads_here = head_cols // HEAD_DIM
    doc_ids = segments[0]
    length = doc_ids.shape[0]
    block = min(length, 512)
    factor = 1.0 / HEAD_DIM**0.5
    inputs_f = tokens.astype(jnp.float32)
    inv_first = rms_scale(inputs_f)
    normal_a = (inputs_f * inv_first * attn_gain).astype(jnp.bfloat16)
    seq_rows = lax.all_gather(normal_a, "col", axis=0, tiled=True)
    wq_full, wk_full, wv_full, wo_full = (
        lax.all_gather(w_query, "row", axis=0, tiled=True),
        lax.all_gather(w_key, "row", axis=0, tiled=True),
        lax.all_gather(w_value, "row", axis=0, tiled=True),
        lax.all_gather(w_out, "row", axis=1, tiled=True),
    )
    query_raw = jnp.dot(seq_rows, wq_full, preferred_element_type=jnp.float32)
    key_raw = jnp.dot(seq_rows, wk_full, preferred_element_type=jnp.float32)
    value_heads = (
        jnp.dot(seq_rows, wv_full, preferred_element_type=jnp.float32)
        .astype(jnp.bfloat16)
        .reshape(length, heads_here, HEAD_DIM)
    )
    query_sq, key_sq = lax.psum(
        (jnp.sum(query_raw * query_raw, -1), jnp.sum(key_raw * key_raw, -1)), "col"
    )
    inv_query = lax.rsqrt(query_sq / D + EPSILON)[:, None]
    inv_key = lax.rsqrt(key_sq / D + EPSILON)[:, None]
    cosines, sine_table = rope_tables(length, HEAD_DIM)
    query_heads = rotate(
        (query_raw * inv_query * query_gain).reshape(length, heads_here, HEAD_DIM),
        cosines,
        sine_table,
    ).astype(jnp.bfloat16)
    key_heads = rotate(
        (key_raw * inv_key * key_gain).reshape(length, heads_here, HEAD_DIM), cosines, sine_table
    ).astype(jnp.bfloat16)
    attended_parts = []
    log_totals = []
    for row_start in range(0, length, block):
        row_stop = row_start + block
        scores = score_block(query_heads, key_heads, doc_ids, row_start, row_stop, factor)
        peak = jnp.max(scores, -1, keepdims=True)
        exps = jnp.exp(scores - peak)
        totals = jnp.sum(exps, -1, keepdims=True)
        log_totals.append(peak + jnp.log(totals))
        weights = (exps / totals).astype(jnp.bfloat16)
        attended_parts.append(
            jnp.einsum(
                "hqk,khd->qhd", weights, value_heads[:row_stop], preferred_element_type=jnp.float32
            )
        )
    attended = jnp.concatenate(attended_parts, 0).reshape(length, head_cols).astype(jnp.bfloat16)
    attn = lax.psum_scatter(
        jnp.dot(attended, wo_full, preferred_element_type=jnp.float32),
        "col",
        scatter_dimension=0,
        tiled=True,
    )
    residual = inputs_f + attn
    inv_second = rms_scale(residual)
    normal_b = (residual * inv_second * ffn_gain).astype(jnp.bfloat16)
    expert_probs = jax.nn.softmax(
        jnp.dot(normal_b, router, preferred_element_type=jnp.float32), axis=-1
    )
    choose = (routes[:, :, None] == jnp.arange(expert_count)[None, None, :]).astype(jnp.float32)
    gates = jnp.sum(choose * expert_probs[:, None, :], -1)
    flat_routes = routes.reshape(-1)
    hits = (flat_routes[:, None] == jnp.arange(expert_count)[None, :]).astype(jnp.int32)
    slot_index = jnp.sum((jnp.cumsum(hits, 0) - hits) * hits, 1)
    target = flat_routes * capacity + slot_index
    placing = (jnp.arange(expert_count * capacity)[:, None] == target[None, :]).astype(jnp.bfloat16)
    per_token = jnp.sum(placing.reshape(expert_count * capacity, tok_count, top_count), -1)

    def build_rows():
        return to_owners(
            jnp.dot(per_token, normal_b, preferred_element_type=jnp.float32).astype(jnp.bfloat16),
            expert_count,
            devices,
            capacity,
        )

    received = lax.all_to_all(build_rows(), ("row", "col"), split_axis=0, concat_axis=0, tiled=True)
    gate_three = w_gate.reshape(width, owned, piece_width)
    up_three = w_up.reshape(width, owned, piece_width)
    down_three = w_down.reshape(owned, piece_width, width)
    gate_pre = jnp.einsum(
        "slcd,dlf->slcf", received, gate_three, preferred_element_type=jnp.float32
    )
    up_pre = jnp.einsum("slcd,dlf->slcf", received, up_three, preferred_element_type=jnp.float32)
    hidden = (jax.nn.silu(gate_pre) * up_pre).astype(jnp.bfloat16)
    piece_out = jnp.einsum(
        "slcf,lfd->slcd", hidden, down_three, preferred_element_type=jnp.float32
    ).astype(jnp.bfloat16)
    returned = lax.all_to_all(piece_out, ("row", "col"), split_axis=0, concat_axis=0, tiled=True)
    table_out = from_owners(returned, expert_count, capacity)
    picked = table_out[target].reshape(tok_count, top_count, width)
    moe = jnp.sum(gates[:, :, None] * picked, 1)
    output = (residual + moe).astype(jnp.bfloat16)
    grad_f = out_grad.astype(jnp.float32)
    grad_gates = jnp.sum(grad_f[:, None, :] * picked, -1)
    contrib = (
        (gates[:, :, None] * grad_f[:, None, :])
        .astype(jnp.bfloat16)
        .reshape(tok_count * top_count, width)
    )
    grad_table = jnp.dot(placing, contrib, preferred_element_type=jnp.float32).astype(jnp.bfloat16)
    grad_sent = to_owners(grad_table, expert_count, devices, capacity)
    rows_back, grad_recv = (
        lax.all_to_all(build_rows(), ("row", "col"), split_axis=0, concat_axis=0, tiled=True),
        lax.all_to_all(grad_sent, ("row", "col"), split_axis=0, concat_axis=0, tiled=True),
    )
    gate_pre = jnp.einsum(
        "slcd,dlf->slcf", rows_back, gate_three, preferred_element_type=jnp.float32
    )
    up_pre = jnp.einsum("slcd,dlf->slcf", rows_back, up_three, preferred_element_type=jnp.float32)
    sigmoid_gate = jax.nn.sigmoid(gate_pre)
    activated = gate_pre * sigmoid_gate
    hidden_back = (activated * up_pre).astype(jnp.bfloat16)
    grad_hidden = jnp.einsum(
        "slcd,lfd->slcf", grad_recv, down_three, preferred_element_type=jnp.float32
    )
    down_grad = jnp.einsum(
        "slcf,slcd->lfd", hidden_back, grad_recv, preferred_element_type=jnp.float32
    ).reshape(local_units, width)
    grad_gate_pre = (
        grad_hidden * up_pre * sigmoid_gate * (1.0 + gate_pre * (1.0 - sigmoid_gate))
    ).astype(jnp.bfloat16)
    grad_up_pre = (grad_hidden * activated).astype(jnp.bfloat16)
    gate_grad = jnp.einsum(
        "slcd,slcf->dlf", rows_back, grad_gate_pre, preferred_element_type=jnp.float32
    ).reshape(width, local_units)
    up_grad = jnp.einsum(
        "slcd,slcf->dlf", rows_back, grad_up_pre, preferred_element_type=jnp.float32
    ).reshape(width, local_units)
    grad_rows = (
        jnp.einsum("slcf,dlf->slcd", grad_gate_pre, gate_three, preferred_element_type=jnp.float32)
        + jnp.einsum("slcf,dlf->slcd", grad_up_pre, up_three, preferred_element_type=jnp.float32)
    ).astype(jnp.bfloat16)
    grad_home = lax.all_to_all(grad_rows, ("row", "col"), split_axis=0, concat_axis=0, tiled=True)
    grad_table_in = from_owners(grad_home, expert_count, capacity)
    grad_probs = jnp.sum(grad_gates[:, :, None] * choose, 1)
    grad_logits = (
        expert_probs * (grad_probs - jnp.sum(expert_probs * grad_probs, -1, keepdims=True))
    ).astype(jnp.bfloat16)
    router_local = jnp.einsum(
        "td,te->de", normal_b, grad_logits, preferred_element_type=jnp.float32
    )
    grad_normal_b = jnp.sum(
        grad_table_in[target].reshape(tok_count, top_count, width), 1
    ) + times_t(grad_logits, router)
    grad_norm_second, ffn_gain_local = norm_back(residual, inv_second, ffn_gain, grad_normal_b)
    grad_residual = grad_f + grad_norm_second
    grad_attn = grad_residual.astype(jnp.bfloat16)
    incoming = lax.all_gather(grad_attn, "col", axis=0, tiled=True)
    grad_attended = times_t(incoming, wo_full)
    grad_attended, wout_local = (
        grad_attended,
        jnp.einsum("th,td->hd", attended, incoming, preferred_element_type=jnp.float32),
    )
    grad_out_heads = grad_attended.astype(jnp.bfloat16).reshape(length, heads_here, HEAD_DIM)
    grad_query_parts = []
    grad_key = jnp.zeros((length, heads_here, HEAD_DIM), jnp.float32)
    grad_value = jnp.zeros((length, heads_here, HEAD_DIM), jnp.float32)
    for block_index, row_start in enumerate(range(0, length, block)):
        row_stop = row_start + block
        scores = score_block(query_heads, key_heads, doc_ids, row_start, row_stop, factor)
        probs_block = jnp.exp(scores - log_totals[block_index])
        weights = probs_block.astype(jnp.bfloat16)
        grad_out_block = grad_out_heads[row_start:row_stop]
        grad_value = grad_value.at[:row_stop].add(
            jnp.einsum("hqk,qhd->khd", weights, grad_out_block, preferred_element_type=jnp.float32)
        )
        grad_weights = jnp.einsum(
            "qhd,khd->hqk",
            grad_out_block,
            value_heads[:row_stop],
            preferred_element_type=jnp.float32,
        )
        grad_scores = (
            probs_block * (grad_weights - jnp.sum(probs_block * grad_weights, -1, keepdims=True))
        ).astype(jnp.bfloat16)
        grad_query_parts.append(
            jnp.einsum(
                "hqk,khd->qhd",
                grad_scores,
                key_heads[:row_stop],
                preferred_element_type=jnp.float32,
            )
            * factor
        )
        grad_key = grad_key.at[:row_stop].add(
            jnp.einsum(
                "hqk,qhd->khd",
                grad_scores,
                query_heads[row_start:row_stop],
                preferred_element_type=jnp.float32,
            )
            * factor
        )
    grad_query_norm = rotate_back(
        jnp.concatenate(grad_query_parts, 0), cosines, sine_table
    ).reshape(length, head_cols)
    grad_key_norm = rotate_back(grad_key, cosines, sine_table).reshape(length, head_cols)
    grad_value_b = grad_value.reshape(length, head_cols).astype(jnp.bfloat16)
    query_scaled = grad_query_norm * query_gain
    key_scaled = grad_key_norm * key_gain
    query_sum, key_sum = lax.psum(
        (jnp.sum(query_scaled * query_raw, -1), jnp.sum(key_scaled * key_raw, -1)), "col"
    )
    grad_query_b = (
        inv_query * query_scaled
        - query_raw * inv_query * inv_query * inv_query * (query_sum / D)[:, None]
    ).astype(jnp.bfloat16)
    grad_key_b = (
        inv_key * key_scaled - key_raw * inv_key * inv_key * inv_key * (key_sum / D)[:, None]
    ).astype(jnp.bfloat16)
    query_gain_local = jnp.sum(grad_query_norm * query_raw * inv_query, 0)
    key_gain_local = jnp.sum(grad_key_norm * key_raw * inv_key, 0)
    wq_local = jnp.einsum("td,th->dh", seq_rows, grad_query_b, preferred_element_type=jnp.float32)
    wk_local = jnp.einsum("td,th->dh", seq_rows, grad_key_b, preferred_element_type=jnp.float32)
    wv_local = jnp.einsum("td,th->dh", seq_rows, grad_value_b, preferred_element_type=jnp.float32)
    grad_normal_a = lax.psum_scatter(
        (
            times_t(grad_query_b, wq_full)
            + times_t(grad_key_b, wk_full)
            + times_t(grad_value_b, wv_full)
        ).astype(jnp.bfloat16),
        "col",
        scatter_dimension=0,
        tiled=True,
    ).astype(jnp.float32)
    grad_norm_first, attn_gain_local = norm_back(inputs_f, inv_first, attn_gain, grad_normal_a)
    input_grad = grad_residual + grad_norm_first
    tiled_query = jnp.broadcast_to(query_gain_local[None, :], (rows_total, head_cols))
    tiled_key = jnp.broadcast_to(key_gain_local[None, :], (rows_total, head_cols))
    query_grad, key_grad, value_grad, out_proj_grad, query_gain_sum, key_gain_sum = (
        lax.psum_scatter(
            wq_local.astype(jnp.bfloat16), "row", scatter_dimension=0, tiled=True
        ).astype(jnp.float32),
        lax.psum_scatter(
            wk_local.astype(jnp.bfloat16), "row", scatter_dimension=0, tiled=True
        ).astype(jnp.float32),
        lax.psum_scatter(
            wv_local.astype(jnp.bfloat16), "row", scatter_dimension=0, tiled=True
        ).astype(jnp.float32),
        lax.psum_scatter(
            wout_local.astype(jnp.bfloat16), "row", scatter_dimension=1, tiled=True
        ).astype(jnp.float32),
        lax.psum_scatter(
            tiled_query.astype(jnp.bfloat16), "row", scatter_dimension=0, tiled=True
        ).astype(jnp.float32),
        lax.psum_scatter(
            tiled_key.astype(jnp.bfloat16), "row", scatter_dimension=0, tiled=True
        ).astype(jnp.float32),
    )
    router_grad, attn_gain_grad, ffn_gain_grad = lax.psum(
        (router_local, attn_gain_local, ffn_gain_local), ("row", "col")
    )
    return (
        output,
        input_grad,
        attn_gain_grad,
        ffn_gain_grad,
        query_gain_sum[0],
        key_gain_sum[0],
        query_grad,
        key_grad,
        value_grad,
        out_proj_grad,
        router_grad,
        gate_grad,
        up_grad,
        down_grad,
    )


def solution(mesh):
    return jax.shard_map(
        local,
        mesh=mesh,
        in_specs=(
            P(("row", "col"), None),
            P(("row", "col"), None),
            P("row", None),
            P(("row", "col"), None),
            P(),
            P(),
            P("col"),
            P("col"),
            P("row", "col"),
            P("row", "col"),
            P("row", "col"),
            P("col", "row"),
            P(),
            P(None, ("row", "col")),
            P(None, ("row", "col")),
            P(("row", "col"), None),
        ),
        out_specs=(
            P(("row", "col"), None),
            P(("row", "col"), None),
            P(),
            P(),
            P("col"),
            P("col"),
            P("row", "col"),
            P("row", "col"),
            P("row", "col"),
            P("col", "row"),
            P(),
            P(None, ("row", "col")),
            P(None, ("row", "col")),
            P(("row", "col"), None),
        ),
        check_vma=False,
    )
```

profile of v0, /device:TPU:0, one launch (start us, length us, event | category | flops | bytes accessed | tf_op | source)
XLA Modules:
  0.0 2178.6 jit_solution(13830173514090648985)
XLA Ops:
  19.6 20.9 all-gather.13.cloned.1.call-done
  40.6 82.9 %all-gather.7.cloned.1.call-done = bf16[1024,2048]{1,0:T(8,128)(2,1)} async-done(((bf16[256,2048]{1,0:T(8,128)(2,1)}), bf16[1024,2048]{1,0:T(8,128)(2,1)}) %all-gather.7.cloned.1.call-update) | async-done | bytes 4194320 | tf_op jit(solution)/shard_map/all_gather | solution.py:133
  128.8 23.1 %all-gather.11.cloned.1.call-done = bf16[2048,512]{1,0:T(8,128)(2,1)} async-done(((bf16[256,512]{1,0:T(8,128)(2,1)}), bf16[2048,512]{1,0:T(8,128)(2,1)}) %all-gather.11.cloned.1.call-update) | async-done | bytes 2097168 | tf_op jit(solution)/shard_map/all_gather | solution.py:135
  240.3 32.3 %fusion.5 = bf16[3072,256]{1,0:T(8,128)(2,1)S(1)} fusion(s32[256,8]{0,1:T(8,128)S(1)} %copy.200), kind=kLoop, calls=%fused_computation.14 | loop fusion | flops 18087936 | bytes 1581056 | tf_op jit(solution)/shard_map/reduce_sum | solution.py:196
  272.6 91.0 %reduce-scatter.7.cloned.1.call-done = f32[256,2048]{1,0:T(8,128)} async-done(((f32[1024,2048]{1,0:T(8,128)}), f32[256,2048]{1,0:T(8,128)}) %reduce-scatter.7.cloned.1.call-update) | async-done | bytes 2097168 | tf_op jit(solution)/shard_map/reduce_scatter | solution.py:177
  391.7 30.1 %fusion.17 = bf16[3072,2048]{1,0:T(8,128)(2,1)} fusion(f32[256,2048]{1,0:T(8,128)S(1)} %copy-done.30, f32[2048]{0:T(1024)S(1)} %mul.752, pred[3072,2048]{1,0:T(32,128)(4,1)} %iota_compare_fusion.13), kind=kOutput, calls=%fused_computation.35 | convolution fusion | flops 25784483840 | bytes 20979712 | tf_op jit(solution)/shard_map/dot_general | solution.py:230
  421.8 228.7 %all-to-all-done = bf16[32,2,48,2048]{3,2,1,0:T(8,128)(2,1)} async-done(((bf16[32,2,48,2048]{3,2,1,0:T(8,128)(2,1)}), bf16[32,2,48,2048]{3,2,1,0:T(8,128)(2,1)}, u32[]{:S(2)}, u32[]{:S(2)}) %all-to-all-start) | async-done | bytes 12582944 | tf_op jit(solution)/shard_map/all_to_all | solution.py:206
  690.7 20.8 fusion.31
  729.8 203.0 %all-to-all-done.2 = bf16[32,2,48,2048]{3,2,1,0:T(8,128)(2,1)} async-done(((bf16[32,2,48,2048]{3,2,1,0:T(8,128)(2,1)}), bf16[32,2,48,2048]{3,2,1,0:T(8,128)(2,1)}, u32[]{:S(2)}, u32[]{:S(2)}) %all-to-all-start.2) | async-done | bytes 12582944 | tf_op jit(solution)/shard_map/all_to_all | solution.py:234
  932.7 27.6 %fusion.10 = (bf16[32,2,48,1024]{3,2,0,1:T(8,128)(2,1)}, bf16[32,2,48,1024]{3,2,0,1:T(8,128)(2,1)}, bf16[32,2,48,1024]{3,2,0,1:T(8,128)(2,1)}) fusion(f32[2,32,48,1024]{3,2,1,0:T(8,128)} %fusion.31, f32[2,32,48,1024]{3,2,1,0:T(8,128)} %fusion.29, bf16[2,1024,2048,1]{2,1,3,0:T(8,128)(2,1)} %bitcast.259, bf16[32,2,48,2048]{3,2,1,0:T(8,128)(2,1)} %all-to-all-done.2), kind=kOutput, calls=%fused_computation.23 | convolution fusion | flops 12932087808 | bytes 65011712 | tf_op jit(solution)/shard_map/slcd,lfd->slcf/dot_general | solution.py:243
  960.3 22.4 %fusion.36 = f32[2,32,48,2048]{3,2,1,0:T(8,128)} fusion(bf16[32,2,48,1024]{3,2,0,1:T(8,128)(2,1)} %get-tuple-element.169, bf16[2048,2,1024,1]{2,1,0,3:T(2,128)(2,1)} %bitcast.234), kind=kOutput, calls=%fused_computation.61 | convolution fusion | flops 12884901888 | bytes 39845888 | tf_op jit(solution)/shard_map/slcf,dlf->slcd/dot_general | solution.py:260
  982.7 23.6 %fusion.6 = bf16[32,2,48,2048]{3,2,0,1:T(8,128)(2,1)} fusion(f32[2,32,48,2048]{3,2,1,0:T(8,128)} %fusion.36, bf16[32,2,48,1024]{3,2,0,1:T(8,128)(2,1)} %get-tuple-element.168, bf16[2048,2,1024,1]{2,1,0,3:T(2,128)(2,1)} %bitcast.231), kind=kOutput, calls=%fused_computation.15 | convolution fusion | flops 12897484800 | bytes 52428800 | tf_op jit(solution)/shard_map/slcf,dlf->slcd/dot_general | solution.py:261
  1051.0 248.4 %all-to-all-done.3 = bf16[32,2,48,2048]{3,2,1,0:T(8,128)(2,1)} async-done(((bf16[32,2,48,2048]{3,2,1,0:T(8,128)(2,1)}), bf16[32,2,48,2048]{3,2,1,0:T(8,128)(2,1)}, u32[]{:S(2)}, u32[]{:S(2)}) %all-to-all-start.3) | async-done | bytes 12582944 | tf_op jit(solution)/shard_map/all_to_all | solution.py:263
  1325.4 24.4 %gather_fusion.1 = f32[2048,2048]{1,0:T(8,128)} fusion(f32[3072,2048]{1,0:T(8,128)} %bitcast_convert_fusion, s32[2048]{0:T(1024)S(1)} %broadcast_clamp_fusion), kind=kCustom, calls=%fused_computation.1 | custom fusion | bytes 33562624 | tf_op jit(solution)/shard_map/gather | solution.py:273
  1359.3 222.3 %all-to-all-done.1 = bf16[32,2,48,2048]{3,2,1,0:T(8,128)(2,1)} async-done(((bf16[32,2,48,2048]{3,2,1,0:T(8,128)(2,1)}), bf16[32,2,48,2048]{3,2,1,0:T(8,128)(2,1)}, u32[]{:S(2)}, u32[]{:S(2)}) %all-to-all-start.1) | async-done | bytes 12582944 | tf_op jit(solution)/shard_map/all_to_all | solution.py:218
  1595.9 24.5 %gather_fusion = f32[2048,2048]{1,0:T(8,128)} fusion(f32[3072,2048]{1,0:T(8,128)} %bitcast_convert_fusion.1, s32[2048]{0:T(1024)S(1)} %broadcast_clamp_fusion), kind=kCustom, calls=%fused_computation | custom fusion | bytes 33562624 | tf_op jit(solution)/shard_map/gather | solution.py:220
  1639.5 87.4 %all-gather.17.cloned.1.call-done = bf16[1024,2048]{1,0:T(8,128)(2,1)} async-done(((bf16[256,2048]{1,0:T(8,128)(2,1)}), bf16[1024,2048]{1,0:T(8,128)(2,1)}) %all-gather.17.cloned.1.call-update) | async-done | bytes 4194320 | tf_op jit(solution)/shard_map/all_gather | solution.py:278
  1802.5 21.6 fusion.27
  1830.3 21.9 %fusion.25 = f32[2,1024,2048,1]{2,1,3,0:T(8,128)} fusion(bf16[32,2,48,1024]{3,2,0,1:T(8,128)(2,1)} %get-tuple-element.168, bf16[32,2,48,2048]{3,2,1,0:T(8,128)(2,1)} %all-to-all-done), kind=kOutput, calls=%fused_computation.50 | convolution fusion | flops 12884901888 | bytes 35651584 | tf_op jit(solution)/shard_map/slcd,slcf->dlf/dot_general | solution.py:256
  1899.0 21.8 %fusion.18 = f32[2,1024,2048,1]{2,1,3,0:T(8,128)} fusion(bf16[32,2,48,1024]{3,2,0,1:T(8,128)(2,1)} %get-tuple-element.170, bf16[32,2,48,2048]{3,2,1,0:T(8,128)(2,1)} %all-to-all-done.2), kind=kOutput, calls=%fused_computation.37 | convolution fusion | flops 12884901888 | bytes 35651584 | tf_op jit(solution)/shard_map/slcf,slcd->lfd/dot_general | solution.py:246
  1923.5 23.1 %all-reduce.7 = (bf16[8,512]{1,0:T(8,128)(2,1)S(1)}, bf16[8,512]{1,0:T(8,128)(2,1)S(1)}) all-reduce(bf16[8,512]{1,0:T(8,128)(2,1)S(1)} %broadcast_in_dim.40, bf16[8,512]{1,0:T(8,128)(2,1)S(1)} %broadcast_in_dim.41), channel_id=4, replica_groups=mesh['row'=8,'col'=4] {'row'}, use_global_device_ids=true, to_apply=%region_37.38.clone | all-reduce | flops 8192 | bytes 32768
  1957.4 77.2 %reduce-scatter.9.cloned.1.call-done = bf16[256,2048]{1,0:T(8,128)(2,1)} async-done(((bf16[1024,2048]{1,0:T(8,128)(2,1)}), bf16[256,2048]{1,0:T(8,128)(2,1)}) %reduce-scatter.9.cloned.1.call-update) | async-done | bytes 1048592 | tf_op jit(solution)/shard_map/reduce_scatter | solution.py:346
  2042.5 41.0 %all-reduce.4 = (f32[2048]{0:T(1024)}, f32[2048]{0:T(1024)}) all-reduce(f32[2048]{0:T(1024)S(1)} %get-tuple-element.156, f32[2048]{0:T(1024)S(1)} %copy-done.76), channel_id=1, replica_groups=mesh['row'=8,'col'=4] {'row','col'}, use_global_device_ids=true, to_apply=%region_33.34 | all-reduce | flops 4096 | bytes 32768 | tf_op jit(solution)/shard_map/psum | solution.py:380
  2083.5 86.2 %all-reduce.10.cloned.1.call-done = f32[2048,64]{0,1:T(8,128)} async-done(((f32[2048,64]{0,1:T(8,128)}), f32[2048,64]{0,1:T(8,128)}) %all-reduce.10.cloned.1.call-update) | async-done | bytes 524304 | tf_op jit(solution)/shard_map/psum | solution.py:380
  (376 shorter events, 456.6 us)
Async XLA Ops:
  7.2 382.5 %copy-start = (bf16[2048,64]{0,1:T(8,128)(2,1)S(1)}, bf16[2048,64]{0,1:T(8,128)(2,1)}, u32[]{:S(2)}) copy-start(bf16[2048,64]{0,1:T(8,128)(2,1)} %param.40) | copy-start | bytes 786436
  7.2 33.4 %all-gather.13.cloned.1.call-start = ((), (), s32[]{:S(2)}) async-start(), calls=%async_computation.13 | async-start | bytes 2359296 | tf_op jit(solution)/shard_map/all_gather | solution.py:136
  7.9 115.6 %all-gather.7.cloned.1.call-start = ((), (), s32[]{:S(2)}) async-start(), calls=%async_computation.10 | async-start | bytes 5242880 | tf_op jit(solution)/shard_map/all_gather | solution.py:133
  12.6 139.2 %all-gather.11.cloned.1.call-start = ((), (), s32[]{:S(2)}) async-start(), calls=%async_computation.12 | async-start | bytes 2359296 | tf_op jit(solution)/shard_map/all_gather | solution.py:135
  13.4 175.6 %all-gather.9.cloned.1.call-start = ((), (), s32[]{:S(2)}) async-start(), calls=%async_computation.11 | async-start | bytes 2359296 | tf_op jit(solution)/shard_map/all_gather | solution.py:137
  13.9 197.6 %all-gather.15.cloned.1.call-start = ((), (), s32[]{:S(2)}) async-start(), calls=%async_computation.14 | async-start | bytes 2359296 | tf_op jit(solution)/shard_map/all_gather | solution.py:138
  14.5 349.1 %reduce-scatter.7.cloned.1.call-start = ((), (), s32[]{:S(2)}) async-start(), calls=%async_computation.15 | async-start | bytes 10485760 | tf_op jit(solution)/shard_map/reduce_scatter | solution.py:177
  219.6 144.0 %copy-start.8 = (bf16[256,2048]{1,0:T(8,128)(2,1)S(1)}, bf16[256,2048]{1,0:T(8,128)(2,1)}, u32[]{:S(2)}) copy-start(bf16[256,2048]{1,0:T(8,128)(2,1)} %param.28) | copy-start | bytes 3145732
  239.2 127.7 %copy-start.60 = (f32[2048]{0:T(1024)S(1)}, f32[2048]{0:T(1024)}, u32[]{:S(2)}) copy-start(f32[2048]{0:T(1024)} %param.33) | copy-start | bytes 24580
  239.5 141.7 %copy-start.58 = (s32[2048]{0:T(1024)}, s32[2048]{0:T(1024)S(1)}, u32[]{:S(2)}) copy-start(s32[2048]{0:T(1024)S(1)} %fusion.84) | copy-start | bytes 24580
  373.8 276.7 %all-to-all-start = ((bf16[32,2,48,2048]{3,2,1,0:T(8,128)(2,1)}), bf16[32,2,48,2048]{3,2,1,0:T(8,128)(2,1)}, u32[]{:S(2)}, u32[]{:S(2)}) async-start(bf16[32,2,48,2048]{3,2,1,0:T(8,128)(2,1)} %bitcast.227), calls=%async_computation.1 | async-start | bytes 25165824 | tf_op jit(solution)/shard_map/all_to_all | solution.py:206
  650.5 282.3 %all-to-all-start.2 = ((bf16[32,2,48,2048]{3,2,1,0:T(8,128)(2,1)}), bf16[32,2,48,2048]{3,2,1,0:T(8,128)(2,1)}, u32[]{:S(2)}, u32[]{:S(2)}) async-start(bf16[32,2,48,2048]{3,2,1,0:T(8,128)(2,1)} %bitcast.230), calls=%async_computation.3 | async-start | bytes 25165824 | tf_op jit(solution)/shard_map/all_to_all | solution.py:234
  1017.0 282.3 %all-to-all-start.3 = ((bf16[32,2,48,2048]{3,2,1,0:T(8,128)(2,1)}), bf16[32,2,48,2048]{3,2,1,0:T(8,128)(2,1)}, u32[]{:S(2)}, u32[]{:S(2)}) async-start(bf16[32,2,48,2048]{3,2,1,0:T(8,128)(2,1)} %copy.210), calls=%async_computation.4 | async-start | bytes 25165824 | tf_op jit(solution)/shard_map/all_to_all | solution.py:263
  1050.9 259.8 %copy-start.55 = (s32[256,8]{1,0:T(8,128)S(1)}, s32[256,8]{1,0:T(8,128)}, u32[]{:S(2)}) copy-start(s32[256,8]{1,0:T(8,128)} %get-tuple-element.191) | copy-start | bytes 24580
  1051.0 259.9 %copy-start.59 = (s32[2048]{0:T(1024)S(1)}, s32[2048]{0:T(1024)}, u32[]{:S(2)}) copy-start(s32[2048]{0:T(1024)} %copy-done.58) | copy-start | bytes 24580
  1299.3 282.3 %all-to-all-start.1 = ((bf16[32,2,48,2048]{3,2,1,0:T(8,128)(2,1)}), bf16[32,2,48,2048]{3,2,1,0:T(8,128)(2,1)}, u32[]{:S(2)}, u32[]{:S(2)}) async-start(bf16[32,2,48,2048]{3,2,1,0:T(8,128)(2,1)} %copy.205), calls=%async_computation.2 | async-start | bytes 25165824 | tf_op jit(solution)/shard_map/all_to_all | solution.py:218
  1310.7 416.3 %all-gather.17.cloned.1.call-start = ((), (), s32[]{:S(2)}) async-start(), calls=%async_computation.16 | async-start | bytes 5242880 | tf_op jit(solution)/shard_map/all_gather | solution.py:278
  1639.4 309.6 %reduce-scatter.11.cloned.1.call-start = ((), (), s32[]{:S(2)}) async-start(), calls=%async_computation.18 | async-start | bytes 2359296 | tf_op jit(solution)/shard_map/reduce_scatter | solution.py:361
  1780.8 170.1 %reduce-scatter.13.cloned.1.call-start = ((), (), s32[]{:S(2)}) async-start(), calls=%async_computation.19 | async-start | bytes 2359296 | tf_op jit(solution)/shard_map/reduce_scatter | solution.py:364
  1788.4 164.3 %reduce-scatter.15.cloned.1.call-start = ((), (), s32[]{:S(2)}) async-start(), calls=%async_computation.20 | async-start | bytes 2359296 | tf_op jit(solution)/shard_map/reduce_scatter | solution.py:367
  1802.3 153.3 %reduce-scatter.17.cloned.1.call-start = ((), (), s32[]{:S(2)}) async-start(), calls=%async_computation.21 | async-start | bytes 2359296 | tf_op jit(solution)/shard_map/reduce_scatter | solution.py:370
  1830.0 204.6 %reduce-scatter.9.cloned.1.call-start = ((), (), s32[]{:S(2)}) async-start(), calls=%async_computation.17 | async-start | bytes 5242880 | tf_op jit(solution)/shard_map/reduce_scatter | solution.py:346
  1898.9 270.8 %all-reduce.10.cloned.1.call-start = ((), (), s32[]{:S(2)}) async-start(), calls=%async_computation.22 | async-start | bytes 1048576 | tf_op jit(solution)/shard_map/psum | solution.py:380
  2036.5 135.1 %copy-start.1 = (bf16[2048,64]{0,1:T(8,128)(2,1)S(1)}, bf16[2048,64]{0,1:T(8,128)(2,1)}, u32[]{:S(2)}) copy-start(bf16[2048,64]{0,1:T(8,128)(2,1)} %param.40) | copy-start | bytes 786436
  (98 other events, 1663.6 us)
Sparse Core Ops, SparseCore 0:
  9.9 30.5 all-gather.12
  42.7 80.7 all-gather.6
  125.4 26.4 all-gather.10
  153.6 27.8 all-gather.8
  183.3 28.2 all-gather.14
  219.0 144.5 reduce-scatter.6
  1639.5 87.3 all-gather.16
  1780.9 40.2 reduce-scatter.10
  1824.8 41.2 reduce-scatter.12
  1869.3 41.2 reduce-scatter.14
  1914.2 41.4 reduce-scatter.16
  1957.8 76.7 reduce-scatter.8
  2041.3 128.3 all-reduce.9
where the time goes:
time: 2190 us; the launch traced here: 2180 us
  waiting for transfers between devices  1380 us (63%)
  matrix products  320 us (15%)
  other arithmetic  172 us (8%)
  local copies, waits for them, and re-layouts  163 us (7%)
  blocking collectives  85.5 us (4%)
  starting transfers between devices  41.2 us (2%)
    all_to_all x1, waiting for transfers between devices, local(): lax.all_to_all(grad_rows, ('row', 'col'), split_axis=0, concat_axis=0, ti...  248 us
    all_to_all x1, waiting for transfers between devices, local(): lax.all_to_all(build_rows(), ('row', 'col'), split_axis=0, concat_axis=0,...  229 us
    all_to_all x1, waiting for transfers between devices, local(): lax.all_to_all(piece_out, ('row', 'col'), split_axis=0, concat_axis=0, ti...  222 us
    all_to_all x1, waiting for transfers between devices, local(): lax.all_to_all(grad_sent, ('row', 'col'), split_axis=0, concat_axis=0, ti...  203 us
    reduce_scatter x1, waiting for transfers between devices, local(): lax.psum_scatter(jnp.dot(attended, wo_full, preferred_element_type=jnp.fl...  91 us
    all_gather x1, waiting for transfers between devices, local(): incoming = lax.all_gather(grad_attn, 'col', axis=0, tiled=True)  87.4 us
    psum x1, waiting for transfers between devices, local(): lax.psum((router_local, attn_gain_local, ffn_gain_local), ('row', 'col'))  86.2 us
    all_gather x1, waiting for transfers between devices, local(): seq_rows = lax.all_gather(normal_a, 'col', axis=0, tiled=True)  82.9 us
  transfers between devices with their start and end apart: 17, of which 13 were waited for; matrix products, arithmetic and copies ran while one was open for 20% of the time, Pallas kernels for 0%

commit v1 on v0

v1 whole, which is shorter than its diff:
```python
import functools

import jax
import jax.numpy as jnp
from jax import lax
from jax.experimental import pallas as pl
from jax.experimental.pallas import tpu as pltpu
from jax.sharding import PartitionSpec as P

HEAD_DIM = 128
VMEM_BYTES = 52 * 2**20


EPSILON = 1e-05
ROPE_BASE = 10000.0
MASKED = -1e30


def rms_scale(values):
    return lax.rsqrt(jnp.mean(values * values, -1, keepdims=True) + EPSILON)


def norm_back(values, scale, gain, grad_in):
    scaled_grad = grad_in * gain
    gain_grad = jnp.sum(grad_in * values * scale, 0)
    value_grad = scale * scaled_grad - values * scale * scale * scale * jnp.mean(
        scaled_grad * values, -1, keepdims=True
    )
    return (value_grad, gain_grad)


def times_t(left, right):
    return lax.dot_general(
        left, right, (((1,), (1,)), ((), ())), preferred_element_type=jnp.float32
    )


def rope_tables(length, head_size):
    half = head_size // 2
    freq = jnp.exp(jnp.arange(half, dtype=jnp.float32) * (-2.0 * jnp.log(ROPE_BASE) / head_size))
    angles = jnp.arange(length, dtype=jnp.float32)[:, None] * freq[None, :]
    return (jnp.cos(angles), jnp.sin(angles))


def first_t(left, right):
    return lax.dot_general(
        left, right, (((0,), (0,)), ((), ())), preferred_element_type=jnp.float32
    )


def shift(value, axis, step=1):
    count = lax.axis_size(axis)
    return lax.ppermute(value, axis, [(i, (i + step) % count) for i in range(count)])


def after(value, *earlier):
    return lax.optimization_barrier((value,) + earlier)[0]


def ring_blocks(value, axis, waits=()):
    blocks = [value]
    for hop in range(lax.axis_size(axis) - 1):
        sent = blocks[-1]
        if hop < len(waits):
            sent = after(sent, waits[hop])
        blocks.append(shift(sent, axis))
    return blocks


def hop_blocks(value, axis):
    return [value] + [shift(value, axis, step) for step in range(1, lax.axis_size(axis))]


def ring_sum(parts, axis):
    total = parts[1].astype(jnp.bfloat16)
    for part in parts[2:]:
        total = (shift(total, axis).astype(jnp.float32) + part).astype(jnp.bfloat16)
    return shift(total, axis).astype(jnp.float32) + parts[0]


def exchange_sum(value, axis, place=None):
    parts = [value] + [shift(value, axis, step) for step in range(1, lax.axis_size(axis))]
    if place is None:
        return sum(parts[1:], parts[0])
    return jnp.sum(natural([part[None] for part in parts], place), 0)


def butterfly_sum(value, axis):
    count = lax.axis_size(axis)
    step = 1
    while step < count:
        value = value + lax.ppermute(value, axis, [(i, i ^ step) for i in range(count)])
        step *= 2
    return value


def natural(blocks, place):
    size = blocks[0].shape[0]
    count = len(blocks)
    whole = jnp.zeros((count * size,) + blocks[0].shape[1:], blocks[0].dtype)
    for back, block in enumerate(blocks):
        whole = lax.dynamic_update_slice_in_dim(
            whole, block, ((place - back) % count) * size, 0
        )
    return whole


def block_of(whole, index, count):
    size = whole.shape[0] // count
    return lax.dynamic_slice_in_dim(whole, (index % count) * size, size, 0)


def split_two(values):
    high = lax.reduce_precision(values, 8, 7)
    return high.astype(jnp.bfloat16), (values - high).astype(jnp.bfloat16)


def kernel_params():
    return pltpu.CompilerParams(vmem_limit_bytes=VMEM_BYTES)


def cost(flops, moved):
    return pl.CostEstimate(flops=int(flops), bytes_accessed=int(moved), transcendentals=0)


def down_t_kernel(grad_ref, down_ref, out_ref):
    rows = out_ref.shape[1]
    grads = grad_ref[...].reshape(rows, grad_ref.shape[-1])
    out_ref[0] = times_t(grads, down_ref[...])


def down_t(grads, w_down, units):
    sources, owned, cap, width = grads.shape
    rows = sources * cap
    tile = min(units, 512)
    tiles = units // tile
    return pl.pallas_call(
        down_t_kernel,
        grid=(owned, tiles),
        in_specs=[
            pl.BlockSpec((sources, 1, cap, width), lambda l, f: (0, l, 0, 0)),
            pl.BlockSpec((tile, width), lambda l, f: (l * tiles + f, 0)),
        ],
        out_specs=pl.BlockSpec((1, rows, tile), lambda l, f: (l, 0, f)),
        out_shape=jax.ShapeDtypeStruct((owned, rows, units), jnp.float32),
        compiler_params=kernel_params(),
        cost_estimate=cost(
            2 * owned * rows * units * width, 2 * owned * (rows + units) * width
        ),
        name="down_t",
    )(grads, w_down)


def expert_kernel(
    rows_ref, gate_ref, up_ref, down_grad_ref, mark_ref, back_ref, hid_ref, dgate_ref, dup_ref,
    total, scalar
):
    step = pl.program_id(1)
    rows, width = total.shape
    packed = rows_ref[...].reshape(rows, rows_ref.shape[-1])
    inputs = packed[:, :width]
    mark = mark_ref[0]
    gate = jnp.sum(
        packed[:, width:].astype(jnp.float32) * (mark[0:1] + mark[1:2]), -1, keepdims=True
    )
    gate_pre = jnp.dot(inputs, gate_ref[...], preferred_element_type=jnp.float32)
    up_pre = jnp.dot(inputs, up_ref[...], preferred_element_type=jnp.float32)
    sigmoid = jax.nn.sigmoid(gate_pre)
    active = gate_pre * sigmoid
    hidden = active * up_pre
    raw_grad = down_grad_ref[0]
    gate_part = jnp.sum(hidden * raw_grad, -1, keepdims=True)
    grad_hidden = raw_grad * gate
    grad_gate = (grad_hidden * up_pre * sigmoid * (1.0 + gate_pre * (1.0 - sigmoid))).astype(
        jnp.bfloat16
    )
    grad_up = (grad_hidden * active).astype(jnp.bfloat16)
    hid_ref[0] = (hidden * gate).astype(jnp.bfloat16)
    dgate_ref[0] = grad_gate
    dup_ref[0] = grad_up
    back = times_t(grad_gate, gate_ref[...]) + times_t(grad_up, up_ref[...])

    @pl.when(step == 0)
    def _():
        total[...] = back
        scalar[...] = jnp.broadcast_to(gate_part, scalar.shape)

    @pl.when(step > 0)
    def _():
        total[...] += back
        scalar[...] += jnp.broadcast_to(gate_part, scalar.shape)

    @pl.when(step == pl.num_programs(1) - 1)
    def _():
        sources, _, cap, packed_width = back_ref.shape
        back_ref[:, :, :, :width] = (
            total[...].astype(jnp.bfloat16).reshape(sources, 1, cap, width)
        )
        value = scalar[:, 0:1]
        high = value.astype(jnp.bfloat16).astype(jnp.float32)
        low = value - high
        extra = high * mark[0:1] + low * mark[1:2]
        back_ref[:, :, :, width:] = extra.astype(jnp.bfloat16).reshape(
            sources, 1, cap, packed_width - width
        )


def expert_core(packed, w_gate, w_up, raw_grad, marks, units):
    sources, owned, cap, packed_width = packed.shape
    rows = sources * cap
    width = w_gate.shape[0]
    tile = min(units, 512)
    tiles = units // tile
    hidden_shape = jax.ShapeDtypeStruct((owned, rows, units), jnp.bfloat16)
    hidden_spec = pl.BlockSpec((1, rows, tile), lambda l, f: (l, 0, f))
    weight_spec = pl.BlockSpec((width, tile), lambda l, f: (0, l * tiles + f))
    packed_spec = pl.BlockSpec((sources, 1, cap, packed_width), lambda l, f: (0, l, 0, 0))
    return pl.pallas_call(
        expert_kernel,
        grid=(owned, tiles),
        in_specs=[
            packed_spec,
            weight_spec,
            weight_spec,
            hidden_spec,
            pl.BlockSpec((1, 8, packed_width - width), lambda l, f: (l, 0, 0)),
        ],
        out_specs=[packed_spec, hidden_spec, hidden_spec, hidden_spec],
        out_shape=[
            jax.ShapeDtypeStruct(packed.shape, jnp.bfloat16),
            hidden_shape,
            hidden_shape,
            hidden_shape,
        ],
        scratch_shapes=[
            pltpu.VMEM((rows, width), jnp.float32),
            pltpu.VMEM((rows, 128), jnp.float32),
        ],
        compiler_params=kernel_params(),
        cost_estimate=cost(
            8 * owned * rows * units * width, 4 * owned * (rows + 2 * units) * width
        ),
        name="expert_core",
    )(packed, w_gate, w_up, raw_grad, marks)


def expert_out_kernel(*refs):
    *hid_refs, down_ref, out_ref = refs

    for block, hid_ref in enumerate(hid_refs):

        @pl.when(pl.program_id(0) == block)
        def _():
            out = jnp.dot(hid_ref[0], down_ref[...], preferred_element_type=jnp.float32)
            out_ref[...] = out.astype(jnp.bfloat16).reshape(out_ref.shape)


def expert_out(hiddens, w_down, sources):
    count = len(hiddens)
    owned, rows, units = hiddens[0].shape
    width = w_down.shape[1]
    cap = rows // sources
    tile = min(width, 1024)
    return pl.pallas_call(
        expert_out_kernel,
        grid=(count, owned, width // tile),
        in_specs=[pl.BlockSpec((1, rows, units), lambda b, l, d: (l, 0, 0))] * count
        + [pl.BlockSpec((units, tile), lambda b, l, d: (l, d))],
        out_specs=pl.BlockSpec(
            (sources, 1, cap, tile), lambda b, l, d: (0, b * owned + l, 0, d)
        ),
        out_shape=jax.ShapeDtypeStruct((sources, count * owned, cap, width), jnp.bfloat16),
        compiler_params=kernel_params(),
        cost_estimate=cost(
            2 * count * owned * rows * units * width, 2 * count * owned * (rows + units) * width
        ),
        name="expert_out",
    )(*hiddens, w_down)


def in_grads_kernel(count, *refs):
    row_refs, grad_refs, out_ref = refs[:count], refs[count : 2 * count], refs[2 * count]
    rows = grad_refs[0].shape[1]
    total = None
    for row_ref, grad_ref in zip(row_refs, grad_refs):
        part = first_t(row_ref[...].reshape(rows, row_ref.shape[-1]), grad_ref[0])
        total = part if total is None else total + part
    out_ref[...] = total


def in_grads(packed, grads, width):
    count = len(packed)
    sources, owned, cap, _ = packed[0].shape
    _, rows, units = grads[0].shape
    tile = min(width, 512)
    return pl.pallas_call(
        functools.partial(in_grads_kernel, count),
        grid=(owned, width // tile),
        in_specs=[pl.BlockSpec((sources, 1, cap, tile), lambda l, d: (0, l, 0, d))] * count
        + [pl.BlockSpec((1, rows, units), lambda l, d: (l, 0, 0))] * count,
        out_specs=pl.BlockSpec((tile, units), lambda l, d: (d, l)),
        out_shape=jax.ShapeDtypeStruct((width, owned * units), jnp.float32),
        compiler_params=kernel_params(),
        cost_estimate=cost(
            2 * owned * count * rows * units * width, 4 * owned * units * width
        ),
        name="in_grads",
    )(*packed, *grads)


def down_grads_kernel(count, *refs):
    hid_refs, grad_refs = refs[:count], refs[count : 2 * count]
    out_ref = refs[2 * count]
    rows = hid_refs[0].shape[1]
    total = None
    for hid_ref, grad_ref in zip(hid_refs, grad_refs):
        part = first_t(hid_ref[0], grad_ref[...].reshape(rows, grad_ref.shape[-1]))
        total = part if total is None else total + part
    out_ref[...] = total


def down_grads(hiddens, grads):
    count = len(hiddens)
    sources, owned, cap, width = grads[0].shape
    _, rows, units = hiddens[0].shape
    tile = min(units, 256)
    tiles = units // tile
    return pl.pallas_call(
        functools.partial(down_grads_kernel, count),
        grid=(owned, tiles),
        in_specs=[pl.BlockSpec((1, rows, tile), lambda l, f: (l, 0, f))] * count
        + [pl.BlockSpec((sources, 1, cap, width), lambda l, f: (0, l, 0, 0))] * count,
        out_specs=pl.BlockSpec((tile, width), lambda l, f: (l * tiles + f, 0)),
        out_shape=jax.ShapeDtypeStruct((owned * units, width), jnp.float32),
        compiler_params=kernel_params(),
        cost_estimate=cost(
            2 * owned * count * rows * units * width, 4 * owned * units * width
        ),
        name="down_grads",
    )(*hiddens, *grads)


def turn(values, cosines, sines):
    return values * cosines + pltpu.roll(values, values.shape[-1] // 2, 1) * sines


def score_t(keys, queries, key_docs, query_docs, first, factor):
    scores = times_t(keys, queries) * factor
    key_pos = lax.broadcasted_iota(jnp.int32, scores.shape, 0)
    query_pos = first + lax.broadcasted_iota(jnp.int32, scores.shape, 1)
    return jnp.where((key_pos <= query_pos) & (key_docs == query_docs), scores, MASKED)


def attend_kernel(
    block, factor, query_ref, key_ref, value_ref, inv_query_ref, inv_key_ref, query_gain_ref,
    key_gain_ref, cos_ref, sin_ref, doc_col_ref, doc_row_ref, query_out, key_out, value_out,
    attended_ref, log_ref
):
    cosines, sines = cos_ref[...], sin_ref[...]
    queries = turn(query_ref[...] * inv_query_ref[...] * query_gain_ref[...], cosines, sines)
    keys = turn(key_ref[...] * inv_key_ref[...] * key_gain_ref[...], cosines, sines)
    query_out[...] = queries.astype(jnp.bfloat16)
    key_out[...] = keys.astype(jnp.bfloat16)
    value_out[...] = value_ref[...].astype(jnp.bfloat16)
    for first in range(0, query_ref.shape[0], block):
        stop = first + block
        scores = score_t(
            key_out[:stop, :],
            query_out[first:stop, :],
            doc_col_ref[:stop, :],
            doc_row_ref[:, first:stop],
            first,
            factor,
        )
        peak = jnp.max(scores, 0, keepdims=True)
        exps = jnp.exp(scores - peak)
        total = jnp.sum(exps, 0, keepdims=True)
        log_ref[0, :, first:stop] = peak + jnp.log(total)
        weights = (exps * (1.0 / total)).astype(jnp.bfloat16)
        attended_ref[first:stop, :] = first_t(value_out[:stop, :], weights).T.astype(jnp.bfloat16)


def attend(qkv, inv_query, inv_key, query_gain, key_gain, tables, doc_ids, block, factor):
    length = qkv.shape[0]
    head_cols = qkv.shape[1] // 3
    heads = head_cols // HEAD_DIM
    head_spec = pl.BlockSpec((length, HEAD_DIM), lambda h: (0, h))
    gain_spec = pl.BlockSpec((1, HEAD_DIM), lambda h: (0, h))

    def whole(shape):
        return pl.BlockSpec(shape, lambda h: (0, 0))

    out = jax.ShapeDtypeStruct((length, head_cols), jnp.bfloat16)
    return pl.pallas_call(
        functools.partial(attend_kernel, block, factor),
        grid=(heads,),
        in_specs=[
            head_spec,
            pl.BlockSpec((length, HEAD_DIM), lambda h: (0, heads + h)),
            pl.BlockSpec((length, HEAD_DIM), lambda h: (0, 2 * heads + h)),
            whole((length, 1)),
            whole((length, 1)),
            gain_spec,
            gain_spec,
            whole((length, HEAD_DIM)),
            whole((length, HEAD_DIM)),
            whole((length, 1)),
            whole((1, length)),
        ],
        out_specs=[head_spec] * 4 + [pl.BlockSpec((1, 1, length), lambda h: (h, 0, 0))],
        out_shape=[out] * 4 + [jax.ShapeDtypeStruct((heads, 1, length), jnp.float32)],
        compiler_params=kernel_params(),
        cost_estimate=cost(24 * head_cols * length * length, 20 * length * head_cols),
        name="attend",
    )(
        qkv,
        qkv,
        qkv,
        inv_query,
        inv_key,
        query_gain[None, :],
        key_gain[None, :],
        tables[0],
        tables[1],
        doc_ids[:, None],
        doc_ids[None, :],
    )


def attend_back_kernel(
    block, factor, query_ref, key_ref, value_ref, out_grad_ref, log_ref, raw_query_ref,
    raw_key_ref, inv_query_ref, inv_key_ref, query_gain_ref, key_gain_ref, cos_ref, sin_ref,
    doc_col_ref, doc_row_ref, query_out, key_out, value_out, query_sum_ref, key_sum_ref,
    query_gain_out, key_gain_out, query_grad, key_grad, value_grad
):
    key_grad[...] = jnp.zeros(key_grad.shape, jnp.float32)
    value_grad[...] = jnp.zeros(value_grad.shape, jnp.float32)
    for first in range(0, query_ref.shape[0], block):
        stop = first + block
        keys = key_ref[:stop, :]
        queries = query_ref[first:stop, :]
        out_grads = out_grad_ref[first:stop, :]
        scores = score_t(
            keys, queries, doc_col_ref[:stop, :], doc_row_ref[:, first:stop], first, factor
        )
        probs = jnp.exp(scores - log_ref[0, :, first:stop])
        prob_grads = times_t(value_ref[:stop, :], out_grads)
        mean = jnp.sum(probs * prob_grads, 0, keepdims=True)
        score_grads = (probs * (prob_grads - mean)).astype(jnp.bfloat16)
        value_grad[:stop, :] += jnp.dot(
            probs.astype(jnp.bfloat16), out_grads, preferred_element_type=jnp.float32
        )
        key_grad[:stop, :] += jnp.dot(score_grads, queries, preferred_element_type=jnp.float32)
        query_grad[first:stop, :] = first_t(keys, score_grads).T
    cosines, sines = cos_ref[...], -sin_ref[...]
    value_out[...] = value_grad[...].astype(jnp.bfloat16)
    head = pl.program_id(0)
    for grad, raw_ref, inv_ref, gain_ref, out_ref, sum_ref, gain_out in (
        (
            query_grad, raw_query_ref, inv_query_ref, query_gain_ref, query_out, query_sum_ref,
            query_gain_out
        ),
        (key_grad, raw_key_ref, inv_key_ref, key_gain_ref, key_out, key_sum_ref, key_gain_out),
    ):
        norm_grad = turn(grad[...] * factor, cosines, sines)
        raw = raw_ref[...]
        scaled = norm_grad * gain_ref[...]
        out_ref[...] = scaled
        part = jnp.sum(scaled * raw, -1, keepdims=True)
        gain_out[...] = jnp.sum(norm_grad * raw * inv_ref[...], 0, keepdims=True)

        @pl.when(head == 0)
        def _():
            sum_ref[...] = part

        @pl.when(head > 0)
        def _():
            sum_ref[...] += part


def attend_back(
    parts, out_grads, logs, qkv, inv_query, inv_key, query_gain, key_gain, tables, doc_ids, block,
    factor
):
    length = qkv.shape[0]
    head_cols = qkv.shape[1] // 3
    heads = head_cols // HEAD_DIM
    head_spec = pl.BlockSpec((length, HEAD_DIM), lambda h: (0, h))
    gain_spec = pl.BlockSpec((1, HEAD_DIM), lambda h: (0, h))

    def whole(shape):
        return pl.BlockSpec(shape, lambda h: (0, 0))

    wide = jax.ShapeDtypeStruct((length, head_cols), jnp.float32)
    narrow = jax.ShapeDtypeStruct((length, head_cols), jnp.bfloat16)
    column = jax.ShapeDtypeStruct((length, 1), jnp.float32)
    gains = jax.ShapeDtypeStruct((1, head_cols), jnp.float32)
    return pl.pallas_call(
        functools.partial(attend_back_kernel, block, factor),
        grid=(heads,),
        in_specs=[head_spec] * 4
        + [
            pl.BlockSpec((1, 1, length), lambda h: (h, 0, 0)),
            head_spec,
            pl.BlockSpec((length, HEAD_DIM), lambda h: (0, heads + h)),
            whole((length, 1)),
            whole((length, 1)),
            gain_spec,
            gain_spec,
            whole((length, HEAD_DIM)),
            whole((length, HEAD_DIM)),
            whole((length, 1)),
            whole((1, length)),
        ],
        out_specs=[
            head_spec,
            head_spec,
            head_spec,
            whole((length, 1)),
            whole((length, 1)),
            gain_spec,
            gain_spec,
        ],
        out_shape=[wide, wide, narrow, column, column, gains, gains],
        scratch_shapes=[pltpu.VMEM((length, HEAD_DIM), jnp.float32)] * 3,
        compiler_params=kernel_params(),
        cost_estimate=cost(40 * head_cols * length * length, 40 * length * head_cols),
        name="attend_back",
    )(
        *parts,
        out_grads,
        logs,
        qkv,
        qkv,
        inv_query,
        inv_key,
        query_gain[None, :],
        key_gain[None, :],
        tables[0],
        tables[1],
        doc_ids[:, None],
        doc_ids[None, :],
    )


def placings(routes, owners, capacity):
    tok_count = routes.shape[0]
    named = jnp.any(owners[:, None, None] == routes[None, :, :], -1)
    before = (
        jnp.arange(tok_count)[:, None] < jnp.arange(tok_count)[None, :]
    ).astype(jnp.bfloat16)
    slot = jnp.dot(named.astype(jnp.bfloat16), before, preferred_element_type=jnp.float32)
    hit = (slot[:, None, :] == jnp.arange(capacity, dtype=jnp.float32)[None, :, None]) & named[
        :, None, :
    ]
    return hit.astype(jnp.bfloat16).reshape(owners.shape[0] * capacity, tok_count)


def local(
    tokens,
    out_grad,
    segments,
    routes,
    attn_gain,
    ffn_gain,
    query_gain,
    key_gain,
    w_query,
    w_key,
    w_value,
    w_out,
    router,
    w_gate,
    w_up,
    w_down,
):
    rows_total = lax.axis_size("row")
    cols_total = lax.axis_size("col")
    devices = rows_total * cols_total
    place = lax.axis_index("col")
    tok_count, width = tokens.shape
    top_count = routes.shape[1]
    expert_count = router.shape[1]
    capacity = tok_count * top_count * 3 // (expert_count * 2)
    capacity = -(-capacity // 16) * 16
    local_units = w_gate.shape[1]
    ff_units = local_units * devices // expert_count
    units = min(local_units, ff_units)
    owned = local_units // units
    head_cols = w_query.shape[1]
    doc_ids = segments[0]
    length = doc_ids.shape[0]
    block = min(length, 256)
    factor = 1.0 / HEAD_DIM**0.5
    extra = -(-2 * expert_count // 128) * 128

    inputs_f = tokens.astype(jnp.float32)
    inv_first = rms_scale(inputs_f)
    normal_a = (inputs_f * inv_first * attn_gain).astype(jnp.bfloat16)
    wqkv = lax.all_gather(
        jnp.concatenate([w_query, w_key, w_value], 1), "row", axis=0, tiled=True
    )
    wo_full = lax.all_gather(w_out, "row", axis=1, tiled=True)
    a_blocks = ring_blocks(normal_a, "col")
    g_blocks = [out_grad, shift(after(out_grad, a_blocks[-1]), "col")]

    route_blocks = hop_blocks(routes, "col")
    plane_ids = (jnp.arange(rows_total) * cols_total + place)[:, None] * local_units
    owners = ((plane_ids + jnp.arange(owned)[None, :] * units) // ff_units).reshape(-1)
    row_place = lax.axis_index("row")
    my_ids = (
        (row_place * cols_total + place) * local_units + jnp.arange(owned) * units
    ) // ff_units
    extra_ids = jnp.arange(extra)
    marks = jnp.concatenate(
        [
            (extra_ids[None, None, :] == my_ids[:, None, None]).astype(jnp.float32),
            (extra_ids[None, None, :] == my_ids[:, None, None] + expert_count).astype(
                jnp.float32
            ),
            jnp.zeros((owned, 6, extra), jnp.float32),
        ],
        1,
    )
    placed = [placings(block_routes, owners, capacity) for block_routes in route_blocks]

    queue = []

    def in_plane(table, *earlier):
        if queue or earlier:
            table = after(table, *queue[-1:], *earlier)
        queue.append(lax.all_to_all(table, "row", split_axis=0, concat_axis=0, tiled=True))
        return queue[-1]

    def to_experts(values, back, *earlier):
        table = jnp.dot(placed[back], values, preferred_element_type=jnp.float32)
        table = table.astype(jnp.bfloat16).reshape(rows_total, owned, capacity, -1)
        return in_plane(table, *earlier)

    def to_tokens(table, back, *earlier):
        home = in_plane(table, *earlier)
        return first_t(
            placed[back], home.reshape(rows_total * owned * capacity, table.shape[-1])
        )

    g_rows = [to_experts(out_grad, 0)]
    seq_rows = after(natural(a_blocks, place), g_rows[0])
    qkv = jnp.dot(seq_rows, wqkv, preferred_element_type=jnp.float32)
    query_raw = qkv[:, :head_cols]
    key_raw = qkv[:, head_cols : 2 * head_cols]
    squares = exchange_sum(
        jnp.stack([jnp.sum(query_raw * query_raw, -1), jnp.sum(key_raw * key_raw, -1)]), "col"
    )
    g_blocks.append(shift(after(g_blocks[1], squares), "col"))
    g_rows.append(to_experts(after(g_blocks[1], qkv), 1))
    inv_query = lax.rsqrt(squares[0] / width + EPSILON)[:, None]
    inv_key = lax.rsqrt(squares[1] / width + EPSILON)[:, None]
    cosines, sine_table = rope_tables(length, HEAD_DIM)
    tables = (
        jnp.concatenate([cosines, cosines], -1),
        jnp.concatenate([-sine_table, sine_table], -1),
    )
    *heads_out, attended, logs = attend(
        qkv, inv_query, inv_key, query_gain, key_gain, tables, doc_ids, block, factor
    )
    attended = after(attended, g_blocks[2])
    raw_grads = [down_t(rows, w_down, units) for rows in g_rows]
    g_rows.append(to_experts(g_blocks[2], 2))
    parts = [
        jnp.dot(
            block_of(attended, place - back, cols_total),
            wo_full,
            preferred_element_type=jnp.float32,
        )
        for back in range(cols_total)
    ]
    parts[2] = after(parts[2], raw_grads[0])
    parts[3] = after(parts[3], raw_grads[1])
    parts[0] = after(parts[0], g_rows[2])
    attn = ring_sum(parts, "col")
    residual = inputs_f + attn
    inv_second = rms_scale(residual)
    normal_b = (residual * inv_second * ffn_gain).astype(jnp.bfloat16)
    expert_probs = jax.nn.softmax(
        jnp.dot(normal_b, router, preferred_element_type=jnp.float32), axis=-1
    )

    high, low = split_two(expert_probs)
    packed_b = jnp.concatenate(
        [normal_b, high, low, jnp.zeros((tok_count, extra - 2 * expert_count), jnp.bfloat16)], 1
    )
    b_blocks = [packed_b, shift(packed_b, "col")]
    b_rows = [to_experts(packed_b, 0)]
    raw_grads.append(down_t(g_rows[2], w_down, units))
    core = []

    def run_core():
        back = len(core)
        core.append(expert_core(b_rows[back], w_gate, w_up, raw_grads[back], marks, units))

    b_rows.append(to_experts(after(b_blocks[1], raw_grads[2]), 1))
    run_core()
    for back in range(2, cols_total):
        if back > 2:
            g_blocks.append(shift(after(g_blocks[-1], b_blocks[-1]), "col"))
            b_blocks[-1] = after(b_blocks[-1], g_blocks[-1])
        b_blocks.append(shift(b_blocks[-1], "col"))
        if back > 2:
            g_rows.append(to_experts(after(g_blocks[back], core[-1][1]), back))
            run_core()
            raw_grads.append(down_t(g_rows[back], w_down, units))
        b_rows.append(to_experts(after(b_blocks[back], core[-1][1]), back))
        if back == 2:
            run_core()
    last = cols_total - 1
    share = to_tokens(core[1][0], 1, raw_grads[last], core[-1][1])
    grad_packed = share.astype(jnp.bfloat16)
    run_core()
    hiddens = [part[1] for part in core]
    gate_grad = in_grads(b_rows, [part[2] for part in core], width)
    up_grad = in_grads(b_rows, [part[3] for part in core], width)
    down_grad = down_grads(hiddens, g_rows)
    order = list(range(1, cols_total)) + [0]
    out_groups = [order[i : i + 2] for i in range(0, cols_total, 2)]
    outs = [
        expert_out([hiddens[back] for back in group], w_down, rows_total)
        for group in out_groups
    ]
    totals = [None, None, grad_packed]
    for back in range(2, cols_total):
        beside = {2: [hiddens[last]], last: [gate_grad, outs[0]]}.get(back, [])
        if totals[back - 1] is not None:
            beside = beside + [totals[back - 1]]
        share = to_tokens(core[back][0], back, *beside)
        grad_packed = (shift(grad_packed, "col").astype(jnp.float32) + share).astype(
            jnp.bfloat16
        )
        totals.append(grad_packed)
    share = to_tokens(core[0][0], 0, up_grad, totals[-2], *outs[1:])
    share = after(share, down_grad)
    grad_packed = shift(grad_packed, "col").astype(jnp.float32) + share

    def outs_home(number):
        home = in_plane(outs[number])
        for slot, back in enumerate(out_groups[number]):
            rows = home[:, slot * owned : (slot + 1) * owned]
            rows = rows.reshape(rows_total * owned * capacity, width)
            out_shares[back] = first_t(placed[back], rows)

    out_shares = {}
    outs_home(0)

    grad_f = out_grad.astype(jnp.float32)
    grad_probs = (
        grad_packed[:, width : width + expert_count]
        + grad_packed[:, width + expert_count : width + 2 * expert_count]
    )
    grad_logits = (
        expert_probs * (grad_probs - jnp.sum(expert_probs * grad_probs, -1, keepdims=True))
    ).astype(jnp.bfloat16)
    grad_normal_b = grad_packed[:, :width] + times_t(grad_logits, router)
    grad_norm_second, ffn_gain_local = norm_back(residual, inv_second, ffn_gain, grad_normal_b)
    grad_residual = grad_f + grad_norm_second
    grad_attn = grad_residual.astype(jnp.bfloat16)
    small = jnp.concatenate(
        [grad_logits]
        + [part.reshape(tok_count, -1) for part in split_two(ffn_gain_local)]
        + [jnp.zeros((tok_count, 128 - expert_count - 2 * width // tok_count), jnp.bfloat16)],
        1,
    )

    grad_blocks = ring_blocks(grad_attn, "col")
    incoming = after(natural(grad_blocks, place), out_shares[1])
    for number in range(1, len(outs)):
        outs_home(number)
    moe = after(out_shares[1].astype(jnp.bfloat16), grad_blocks[-1])
    moe = (shift(moe, "col").astype(jnp.float32) + out_shares[2]).astype(jnp.bfloat16)
    wout_local = first_t(incoming, attended).astype(jnp.bfloat16)
    grad_out_heads = times_t(incoming, wo_full).astype(jnp.bfloat16)
    (
        query_scaled,
        key_scaled,
        grad_value_b,
        query_sum,
        key_sum,
        query_gain_local,
        key_gain_local,
    ) = attend_back(
        heads_out,
        grad_out_heads,
        logs,
        qkv,
        inv_query,
        inv_key,
        query_gain,
        key_gain,
        tables,
        doc_ids,
        block,
        factor,
    )
    sums = exchange_sum(jnp.stack([query_sum[:, 0], key_sum[:, 0]]), "col")
    small_blocks = hop_blocks(after(small, query_sum), "col")
    small_rows = natural(small_blocks, place)
    router_local = first_t(natural(b_blocks, place)[:, :width], small_rows[:, :expert_count])
    gain_width = width // tok_count
    gain_parts = small_rows[:, expert_count : expert_count + 2 * gain_width].astype(jnp.float32)
    gain_parts = gain_parts[:, :gain_width] + gain_parts[:, gain_width:]
    ffn_gain_part = jnp.sum(gain_parts.reshape(cols_total, width), 0)
    early = jnp.concatenate(
        [
            router_local.reshape(rows_total, -1, expert_count),
            ffn_gain_part.reshape(rows_total, -1, expert_count),
        ],
        1,
    )
    early = jnp.sum(in_plane(early), 0)
    moe = after(moe, sums)
    for back in order[2:]:
        moe = shift(moe, "col").astype(jnp.float32) + out_shares[back]
        if back:
            moe = moe.astype(jnp.bfloat16)
    output = (residual + moe).astype(jnp.bfloat16)
    grad_query_b = (
        inv_query * query_scaled
        - query_raw * inv_query * inv_query * inv_query * (sums[0] / width)[:, None]
    ).astype(jnp.bfloat16)
    grad_key_b = (
        inv_key * key_scaled - key_raw * inv_key * inv_key * inv_key * (sums[1] / width)[:, None]
    ).astype(jnp.bfloat16)
    grad_qkv = jnp.concatenate([grad_query_b, grad_key_b, grad_value_b], 1)
    da_parts = [
        times_t(block_of(grad_qkv, place - back, cols_total), wqkv) for back in range(cols_total)
    ]
    da_total = da_parts[1].astype(jnp.bfloat16)
    for back in range(2, cols_total):
        da_came = shift(da_total, "col")
        if back == 2:
            first_came = da_came
        da_total = (da_came.astype(jnp.float32) + da_parts[back]).astype(jnp.bfloat16)
    grad_normal_a = shift(da_total, "col").astype(jnp.float32) + da_parts[0]
    wqkv_local = first_t(seq_rows, after(grad_qkv, first_came)).astype(jnp.bfloat16)
    attn_gain_local = (
        jnp.sum(wqkv.astype(jnp.float32) * wqkv_local.astype(jnp.float32), -1) / attn_gain
    )
    core_place = row_place % 2

    def over_cores(value):
        halves = value.reshape(rows_total // 2, 2, -1, value.shape[-1])
        other = lax.ppermute(
            lax.dynamic_index_in_dim(halves, 1 - core_place, 1, False),
            "row",
            [(i, i ^ 1) for i in range(rows_total)],
        )
        return (
            lax.dynamic_index_in_dim(halves, core_place, 1, False).astype(jnp.float32) + other
        ).astype(jnp.bfloat16)

    pair = jnp.concatenate([over_cores(wqkv_local), over_cores(wout_local)], -1)
    pair = lax.all_to_all(
        after(pair, queue[-1]),
        "row",
        split_axis=0,
        concat_axis=0,
        tiled=True,
        axis_index_groups=[list(range(core, rows_total, 2)) for core in range(2)],
    )
    queue.append(pair)
    late = jnp.concatenate([attn_gain_local, query_gain_local[0], key_gain_local[0]])
    late = jnp.concatenate([early.reshape(-1), late]).reshape(1, -1, 128)
    spread = in_plane(jnp.broadcast_to(late, (rows_total,) + late.shape[1:]))
    spread = spread.reshape(rows_total, -1)
    late = jnp.sum(spread[:, early.size :], 0)
    early = spread[:, : early.size].reshape((rows_total,) + early.shape)
    attn_gain_grad = exchange_sum(late[:width], "col", place)

    weight_grads = jnp.sum(pair.astype(jnp.float32), 0)
    wqkv_grad = weight_grads[:, : 3 * head_cols]
    out_proj_grad = weight_grads[:, 3 * head_cols :].T
    router_grad = early[:, : width // rows_total].reshape(width, expert_count)
    ffn_gain_grad = early[:, width // rows_total :].reshape(width)
    grad_norm_first, _ = norm_back(inputs_f, inv_first, attn_gain, grad_normal_a)
    input_grad = grad_residual + grad_norm_first
    return (
        output,
        input_grad,
        attn_gain_grad,
        ffn_gain_grad,
        late[width : width + head_cols],
        late[width + head_cols :],
        wqkv_grad[:, :head_cols],
        wqkv_grad[:, head_cols : 2 * head_cols],
        wqkv_grad[:, 2 * head_cols :],
        out_proj_grad,
        router_grad,
        gate_grad,
        up_grad,
        down_grad,
    )


def solution(mesh):
    return jax.shard_map(
        local,
        mesh=mesh,
        in_specs=(
            P(("row", "col"), None),
            P(("row", "col"), None),
            P("row", None),
            P(("row", "col"), None),
            P(),
            P(),
            P("col"),
            P("col"),
            P("row", "col"),
            P("row", "col"),
            P("row", "col"),
            P("col", "row"),
            P(),
            P(None, ("row", "col")),
            P(None, ("row", "col")),
            P(("row", "col"), None),
        ),
        out_specs=(
            P(("row", "col"), None),
            P(("row", "col"), None),
            P(),
            P(),
            P("col"),
            P("col"),
            P("row", "col"),
            P("row", "col"),
            P("row", "col"),
            P("col", "row"),
            P(),
            P(None, ("row", "col")),
            P(None, ("row", "col")),
            P(("row", "col"), None),
        ),
        check_vma=False,
    )
```

time: 2190 us -> 1020 us (0.47)
  waiting for transfers between devices: 1380 us -> 414 us
  Pallas kernels: 0 us -> 252 us
  matrix products: 320 us -> 115 us
  other arithmetic: 172 us -> 46.6 us
  local copies, waits for them, and re-layouts: 163 us -> 63 us
  blocking collectives: 85.5 us -> 0 us
  starting transfers between devices: 41.2 us -> 105 us
    all_to_all x4 -> x17, waiting for transfers between devices: 902 us -> 91.7 us  [the longest x16 91.7 us: in_plane(): lax.all_to_all(table, 'row', split_axis=0, concat_axis=0, tiled=True)]
    ppermute x0 -> x41, waiting for transfers between devices: none -> 322 us  [the longest x39 322 us: shift(): lax.ppermute(value, axis, [(i, (i + step) % count) for i in range(count)])]
    pallas_call x0 -> x15, Pallas kernels: none -> 252 us  [the longest x4 83.9 us: expert_core(): pl.pallas_call(expert_kernel, grid=(owned, tiles), in_specs=[packed_spec,...]
    all_gather x6 -> x2, waiting for transfers between devices: 221 us -> 0.01 us  [the longest x1 0.01 us: local(): lax.all_gather(jnp.concatenate([w_query, w_key, w_value], 1), 'row', axis...]
    dot_general x32 -> x28, matrix products: 300 us -> 88.1 us  [the longest x11 43.9 us: first_t(): lax.dot_general(left, right, (((0,), (0,)), ((), ())), preferred_element_...]
    reduce_scatter x6 -> x0, waiting for transfers between devices: 169 us -> none  [the longest x1 91 us: local(): lax.psum_scatter(jnp.dot(attended, wo_full, preferred_element_type=jnp.fl...]
    psum x1 -> x0, waiting for transfers between devices: 86.2 us -> none  [local(): lax.psum((router_local, attn_gain_local, ffn_gain_local), ('row', 'col'))]
    psum x3 -> x0, blocking collectives: 62.4 us -> none  [the longest x1 41 us: local(): lax.psum((router_local, attn_gain_local, ffn_gain_local), ('row', 'col'))]
  transfers between devices with their start and end apart: 17 -> 60, of which waited for: 13 -> 30; matrix products, arithmetic and copies ran while one was open for 20% -> 18% of each run, Pallas kernels for 0% -> 23%
where the time goes in v1:
time: 1020 us; the launch traced here: 1010 us
  waiting for transfers between devices  414 us (41%)
  Pallas kernels  252 us (25%)
  matrix products  115 us (11%)
  starting transfers between devices  105 us (10%)
  local copies, waits for them, and re-layouts  63 us (6%)
  other arithmetic  46.6 us (5%)
  between operations  16.4 us (2%)
    ppermute x39, waiting for transfers between devices, shift(): lax.ppermute(value, axis, [(i, (i + step) % count) for i in range(count)])  322 us
    all_to_all x16, waiting for transfers between devices, in_plane(): lax.all_to_all(table, 'row', split_axis=0, concat_axis=0, tiled=True)  91.7 us
    pallas_call x4, Pallas kernels, expert_core(): pl.pallas_call(expert_kernel, grid=(owned, tiles), in_specs=[packed_spec,...  83.9 us
    all_to_all x16, starting transfers between devices, in_plane(): lax.all_to_all(table, 'row', split_axis=0, concat_axis=0, tiled=True)  71.1 us
    pallas_call x2, Pallas kernels, in_grads(): pl.pallas_call(functools.partial(in_grads_kernel, count), grid=(owned, wi...  46.4 us
    dot_general x11, matrix products, first_t(): lax.dot_general(left, right, (((0,), (0,)), ((), ())), preferred_element_...  43.9 us
    pallas_call x4, Pallas kernels, down_t(): pl.pallas_call(down_t_kernel, grid=(owned, tiles), in_specs=[pl.BlockSpec...  35.1 us
    pallas_call x2, Pallas kernels, expert_out(): pl.pallas_call(expert_out_kernel, grid=(count, owned, width // tile), in_...  30.2 us
  transfers between devices with their start and end apart: 60, of which 30 were waited for; matrix products, arithmetic and copies ran while one was open for 18% of the time, Pallas kernels for 23%

profile of v1, /device:TPU:0, one launch (start us, length us, event | category | flops | bytes accessed | tf_op | source)
XLA Modules:
  0.0 1011.5 jit_solution(8969162450382835336)
XLA Ops:
  31.5 15.7 %collective-permute-done = bf16[256,2048]{1,0:T(8,128)(2,1)} collective-permute-done((bf16[256,2048]{1,0:T(8,128)(2,1)}, bf16[256,2048]{1,0:T(8,128)(2,1)}, u32[]{:S(2)}, u32[]{:S(2)}) %collective-permute-start) | collective-permute-done | bytes 1048608 | tf_op jit(solution)/shard_map/ppermute | solution.py:53
  47.2 25.2 %collective-permute-done.1 = bf16[256,2048]{1,0:T(8,128)(2,1)} collective-permute-done((bf16[256,2048]{1,0:T(8,128)(2,1)}, bf16[256,2048]{1,0:T(8,128)(2,1)}, u32[]{:S(2)}, u32[]{:S(2)}) %collective-permute-start.1) | collective-permute-done | bytes 1048608 | tf_op jit(solution)/shard_map/ppermute | solution.py:53
  81.5 15.2 %collective-permute-done.2 = bf16[256,2048]{1,0:T(8,128)(2,1)} collective-permute-done((bf16[256,2048]{1,0:T(8,128)(2,1)}, bf16[256,2048]{1,0:T(8,128)(2,1)}, u32[]{:S(2)}, u32[]{:S(2)}) %collective-permute-start.2) | collective-permute-done | bytes 1048608 | tf_op jit(solution)/shard_map/ppermute | solution.py:53
  145.3 13.7 %collective-permute-done.7 = bf16[256,2048]{1,0:T(8,128)(2,1)} collective-permute-done((bf16[256,2048]{1,0:T(8,128)(2,1)}, bf16[256,2048]{1,0:T(8,128)(2,1)}, u32[]{:S(2)}, u32[]{:S(2)}) %collective-permute-start.7) | collective-permute-done | bytes 1048608 | tf_op jit(solution)/shard_map/ppermute | solution.py:53
  200.7 16.0 %collective-permute-done.9 = bf16[256,2048]{1,0:T(8,128)(2,1)S(1)} collective-permute-done((bf16[256,2048]{1,0:T(8,128)(2,1)S(1)}, bf16[256,2048]{1,0:T(8,128)(2,1)S(1)}, u32[]{:S(2)}, u32[]{:S(2)}) %collective-permute-start.9) | collective-permute-done | bytes 1048608 | tf_op jit(solution)/shard_map/ppermute | solution.py:53
  220.5 22.4 %collective-permute-done.11 = bf16[256,2048]{1,0:T(8,128)(2,1)} collective-permute-done((bf16[256,2048]{1,0:T(8,128)(2,1)}, bf16[256,2048]{1,0:T(8,128)(2,1)}, u32[]{:S(2)}, u32[]{:S(2)}) %collective-permute-start.11) | collective-permute-done | bytes 1048608 | tf_op jit(solution)/shard_map/ppermute | solution.py:53
  264.9 19.9 %collective-permute-done.13 = bf16[256,2176]{1,0:T(8,128)(2,1)S(1)} collective-permute-done((bf16[256,2176]{1,0:T(8,128)(2,1)S(1)}, bf16[256,2176]{1,0:T(8,128)(2,1)S(1)}, u32[]{:S(2)}, u32[]{:S(2)}) %collective-permute-start.13) | collective-permute-done | bytes 1114144 | tf_op jit(solution)/shard_map/ppermute | solution.py:53
  300.5 21.0 %expert_core.5 = (bf16[8,2,48,2176]{3,2,1,0:T(8,128)(2,1)}, bf16[2,384,1024]{2,1,0:T(8,128)(2,1)S(1)}, bf16[2,384,1024]{2,1,0:T(8,128)(2,1)}, bf16[2,384,1024]{2,1,0:T(8,128)(2,1)}) custom-call(bf16[8,2,48,2176]{3,2,1,0:T(8,128)(2,1)} %all-to-all-done.3.rows_ref.refs_0_, bf16[2048,2048]{1,0:T(8,128)(2,1)} %gate_ref.7, bf16[2048,2048]{1,0:T(8,128)(2,1)} %up_ref.7, ...), custom_call_target="tpu_custom_call" | custom-call | flops 12884901888 | bytes 39845888 | tf_op jit(solution)/shard_map/expert_core/pallas_call | solution.py:218
  344.7 21.0 %expert_core.4 = (bf16[8,2,48,2176]{3,2,1,0:T(8,128)(2,1)}, bf16[2,384,1024]{2,1,0:T(8,128)(2,1)S(1)}, bf16[2,384,1024]{2,1,0:T(8,128)(2,1)}, bf16[2,384,1024]{2,1,0:T(8,128)(2,1)}) custom-call(bf16[8,2,48,2176]{3,2,1,0:T(8,128)(2,1)} %all-to-all-done.4.rows_ref.refs_1_, bf16[2048,2048]{1,0:T(8,128)(2,1)} %gate_ref.7, bf16[2048,2048]{1,0:T(8,128)(2,1)} %up_ref.7, ...), custom_call_target="tpu_custom_call" | custom-call | flops 12884901888 | bytes 39845888 | tf_op jit(solution)/shard_map/expert_core/pallas_call | solution.py:218
  389.5 20.9 %expert_core.6 = (bf16[8,2,48,2176]{3,2,1,0:T(8,128)(2,1)}, bf16[2,384,1024]{2,1,0:T(8,128)(2,1)S(1)}, bf16[2,384,1024]{2,1,0:T(8,128)(2,1)}, bf16[2,384,1024]{2,1,0:T(8,128)(2,1)}) custom-call(bf16[8,2,48,2176]{3,2,1,0:T(8,128)(2,1)} %all-to-all-done.5.rows_ref.refs_2_, bf16[2048,2048]{1,0:T(8,128)(2,1)} %gate_ref.7, bf16[2048,2048]{1,0:T(8,128)(2,1)} %up_ref.7, ...), custom_call_target="tpu_custom_call" | custom-call | flops 12884901888 | bytes 39845888 | tf_op jit(solution)/shard_map/expert_core/pallas_call | solution.py:218
  440.4 31.2 %all-to-all-done.7.rows_ref.refs_3_ = bf16[8,2,48,2176]{3,2,1,0:T(8,128)(2,1)} async-done(((bf16[8,2,48,2176]{3,2,1,0:T(8,128)(2,1)}), bf16[8,2,48,2176]{3,2,1,0:T(8,128)(2,1)}, u32[]{:S(2)}, u32[]{:S(2)}) %all-to-all-start.7) | async-done | bytes 3342368 | tf_op jit(solution)/shard_map/all_to_all | solution.py:632
  476.1 21.0 %expert_core.7 = (bf16[8,2,48,2176]{3,2,1,0:T(8,128)(2,1)}, bf16[2,384,1024]{2,1,0:T(8,128)(2,1)S(1)}, bf16[2,384,1024]{2,1,0:T(8,128)(2,1)}, bf16[2,384,1024]{2,1,0:T(8,128)(2,1)}) custom-call(bf16[8,2,48,2176]{3,2,1,0:T(8,128)(2,1)} %all-to-all-done.7.rows_ref.refs_3_, bf16[2048,2048]{1,0:T(8,128)(2,1)} %gate_ref.7, bf16[2048,2048]{1,0:T(8,128)(2,1)} %up_ref.7, ...), custom_call_target="tpu_custom_call" | custom-call | flops 12884901888 | bytes 39845888 | tf_op jit(solution)/shard_map/expert_core/pallas_call | solution.py:218
  498.2 17.9 %all-to-all-done.8 = bf16[8,2,48,2176]{3,2,1,0:T(8,128)(2,1)} async-done(((bf16[8,2,48,2176]{3,2,1,0:T(8,128)(2,1)}), bf16[8,2,48,2176]{3,2,1,0:T(8,128)(2,1)}, u32[]{:S(2)}, u32[]{:S(2)}) %all-to-all-start.8) | async-done | bytes 3342368 | tf_op jit(solution)/shard_map/all_to_all | solution.py:632
  521.0 15.1 %expert_out.2 = bf16[8,4,48,2048]{3,2,1,0:T(8,128)(2,1)} custom-call(bf16[2,384,1024]{2,1,0:T(8,128)(2,1)S(1)} %get-tuple-element.92.refs_0_.refs_1_, bf16[2,384,1024]{2,1,0:T(8,128)(2,1)} %copy-done.11, bf16[2048,2048]{1,0:T(8,128)(2,1)} %refs_2_.3), custom_call_target="tpu_custom_call" | custom-call | flops 6442450944 | bytes 23068672 | tf_op jit(solution)/shard_map/expert_out/pallas_call | solution.py:264
  536.1 23.2 %in_grads.2 = f32[2048,2048]{1,0:T(8,128)} custom-call(bf16[8,2,48,2176]{3,2,1,0:T(8,128)(2,1)} %all-to-all-done.3.rows_ref.refs_0_, bf16[8,2,48,2176]{3,2,1,0:T(8,128)(2,1)} %all-to-all-done.4.rows_ref.refs_1_, bf16[8,2,48,2176]{3,2,1,0:T(8,128)(2,1)} %all-to-all-done.5.rows_ref.refs_2_, bf16[8,2,48,2176]{3,2,1,0:T(8,128)(2,1)} %all-to-all-done.7.rows_ref.refs_3_, ...), custom_call_target="tpu_custom_call" | custom-call | flops 12884901888 | bytes 16777216 | tf_op jit(solution)/shard_map/in_grads/pallas_call | solution.py:296
  567.3 15.1 %expert_out.3 = bf16[8,4,48,2048]{3,2,1,0:T(8,128)(2,1)} custom-call(bf16[2,384,1024]{2,1,0:T(8,128)(2,1)S(1)} %copy-done.13, bf16[2,384,1024]{2,1,0:T(8,128)(2,1)} %copy-done.8, bf16[2048,2048]{1,0:T(8,128)(2,1)} %refs_2_.3), custom_call_target="tpu_custom_call" | custom-call | flops 6442450944 | bytes 23068672 | tf_op jit(solution)/shard_map/expert_out/pallas_call | solution.py:264
  582.4 23.2 %in_grads.3 = f32[2048,2048]{1,0:T(8,128)} custom-call(bf16[8,2,48,2176]{3,2,1,0:T(8,128)(2,1)} %all-to-all-done.3.rows_ref.refs_0_, bf16[8,2,48,2176]{3,2,1,0:T(8,128)(2,1)} %all-to-all-done.4.rows_ref.refs_1_, bf16[8,2,48,2176]{3,2,1,0:T(8,128)(2,1)} %all-to-all-done.5.rows_ref.refs_2_, bf16[8,2,48,2176]{3,2,1,0:T(8,128)(2,1)} %all-to-all-done.7.rows_ref.refs_3_, ...), custom_call_target="tpu_custom_call" | custom-call | flops 12884901888 | bytes 16777216 | tf_op jit(solution)/shard_map/in_grads/pallas_call | solution.py:296
  619.1 28.2 %collective-permute-done.19 = bf16[256,2176]{1,0:T(8,128)(2,1)S(1)} collective-permute-done((bf16[256,2176]{1,0:T(8,128)(2,1)S(1)}, bf16[256,2176]{1,0:T(8,128)(2,1)S(1)}, u32[]{:S(2)}, u32[]{:S(2)}) %collective-permute-start.19) | collective-permute-done | bytes 1114144 | tf_op jit(solution)/shard_map/ppermute | solution.py:53
  652.0 26.1 %down_grads.1 = f32[2048,2048]{1,0:T(8,128)} custom-call(bf16[2,384,1024]{2,1,0:T(8,128)(2,1)S(1)} %copy-done.9, bf16[2,384,1024]{2,1,0:T(8,128)(2,1)} %copy-done.10, bf16[2,384,1024]{2,1,0:T(8,128)(2,1)} %copy-done.11, bf16[2,384,1024]{2,1,0:T(8,128)(2,1)} %copy-done.12, bf16[8,2,48,2048]{3,2,1,0:T(8,128)(2,1)} %all-to-all-done.grad_ref.refs_4_, ...), custom_call_target="tpu_custom_call" | custom-call | flops 12884901888 | bytes 16777216 | tf_op jit(solution)/shard_map/down_grads/pallas_call | solution.py:328
  694.6 27.4 %collective-permute-done.21 = bf16[256,2048]{1,0:T(8,128)(2,1)S(1)} collective-permute-done((bf16[256,2048]{1,0:T(8,128)(2,1)S(1)}, bf16[256,2048]{1,0:T(8,128)(2,1)S(1)}, u32[]{:S(2)}, u32[]{:S(2)}) %collective-permute-start.21) | collective-permute-done | bytes 1048608 | tf_op jit(solution)/shard_map/ppermute | solution.py:53
  724.0 24.6 %collective-permute-done.22 = bf16[256,2048]{1,0:T(8,128)(2,1)S(1)} collective-permute-done((bf16[256,2048]{1,0:T(8,128)(2,1)S(1)}, bf16[256,2048]{1,0:T(8,128)(2,1)S(1)}, u32[]{:S(2)}, u32[]{:S(2)}) %collective-permute-start.22) | collective-permute-done | bytes 1048608 | tf_op jit(solution)/shard_map/ppermute | solution.py:53
  758.0 16.7 %collective-permute-done.23 = bf16[256,2048]{1,0:T(8,128)(2,1)S(1)} collective-permute-done((bf16[256,2048]{1,0:T(8,128)(2,1)S(1)}, bf16[256,2048]{1,0:T(8,128)(2,1)S(1)}, u32[]{:S(2)}, u32[]{:S(2)}) %collective-permute-start.23) | collective-permute-done | bytes 1048608 | tf_op jit(solution)/shard_map/ppermute | solution.py:53
  786.7 17.0 %attend_back.1 = (f32[1024,512]{1,0:T(8,128)}, f32[1024,512]{1,0:T(8,128)}, bf16[1024,512]{1,0:T(8,128)(2,1)}, f32[1024,1]{1,0:T(8,128)S(1)}, f32[1024,1]{1,0:T(...) custom-call(bf16[1024,512]{1,0:T(8,128)(2,1)} %get-tuple-element.123.query_ref, ...), custom_call_target="tpu_custom_call" | custom-call | flops 21474836480 | bytes 20971520 | tf_op jit(solution)/shard_map/attend_back/pallas_call | solution.py:498
  887.3 21.9 %collective-permute-done.31 = bf16[256,2048]{1,0:T(8,128)(2,1)} collective-permute-done((bf16[256,2048]{1,0:T(8,128)(2,1)}, bf16[256,2048]{1,0:T(8,128)(2,1)}, u32[]{:S(2)}, u32[]{:S(2)}) %collective-permute-start.31) | collective-permute-done | bytes 1048608 | tf_op jit(solution)/shard_map/ppermute | solution.py:53
  (483 shorter events, 495.4 us)
Async XLA Ops:
  7.2 91.9 %all-gather.3.cloned.1.call-start = ((), (), s32[]{:S(2)}) async-start(), calls=%async_computation.17 | async-start | bytes 7077888 | tf_op jit(solution)/shard_map/all_gather | solution.py:600
  26.9 72.2 %all-to-all-start = ((bf16[8,2,48,2048]{3,2,1,0:T(8,128)(2,1)}), bf16[8,2,48,2048]{3,2,1,0:T(8,128)(2,1)}, u32[]{:S(2)}, u32[]{:S(2)}) async-start(bf16[8,2,48,2048]{3,2,1,0:T(8,128)(2,1)} %bitcast.2), calls=%async_computation | async-start | bytes 6291456 | tf_op jit(solution)/shard_map/all_to_all | solution.py:632
  31.4 127.6 %all-gather.5.cloned.1.call-start = ((), (), s32[]{:S(2)}) async-start(), calls=%async_computation.18 | async-start | bytes 2359296 | tf_op jit(solution)/shard_map/all_gather | solution.py:603
  126.5 51.6 %all-to-all-start.1 = ((bf16[8,2,48,2048]{3,2,1,0:T(8,128)(2,1)}), bf16[8,2,48,2048]{3,2,1,0:T(8,128)(2,1)}, u32[]{:S(2)}, u32[]{:S(2)}) async-start(bf16[8,2,48,2048]{3,2,1,0:T(8,128)(2,1)} %bitcast.159), calls=%async_computation.1 | async-start | bytes 6291456 | tf_op jit(solution)/shard_map/all_to_all | solution.py:632
  178.2 42.4 %all-to-all-start.2 = ((bf16[8,2,48,2048]{3,2,1,0:T(8,128)(2,1)}), bf16[8,2,48,2048]{3,2,1,0:T(8,128)(2,1)}, u32[]{:S(2)}, u32[]{:S(2)}) async-start(bf16[8,2,48,2048]{3,2,1,0:T(8,128)(2,1)} %bitcast.160), calls=%async_computation.2 | async-start | bytes 6291456 | tf_op jit(solution)/shard_map/all_to_all | solution.py:632
  251.2 44.5 %all-to-all-start.3 = ((bf16[8,2,48,2176]{3,2,1,0:T(8,128)(2,1)}), bf16[8,2,48,2176]{3,2,1,0:T(8,128)(2,1)}, u32[]{:S(2)}, u32[]{:S(2)}) async-start(bf16[8,2,48,2176]{3,2,1,0:T(8,128)(2,1)} %bitcast.157), calls=%async_computation.3 | async-start | bytes 6684672 | tf_op jit(solution)/shard_map/all_to_all | solution.py:632
  295.7 44.5 %all-to-all-start.4 = ((bf16[8,2,48,2176]{3,2,1,0:T(8,128)(2,1)}), bf16[8,2,48,2176]{3,2,1,0:T(8,128)(2,1)}, u32[]{:S(2)}, u32[]{:S(2)}) async-start(bf16[8,2,48,2176]{3,2,1,0:T(8,128)(2,1)} %bitcast.155), calls=%async_computation.4 | async-start | bytes 6684672 | tf_op jit(solution)/shard_map/all_to_all | solution.py:632
  340.2 44.5 %all-to-all-start.5 = ((bf16[8,2,48,2176]{3,2,1,0:T(8,128)(2,1)}), bf16[8,2,48,2176]{3,2,1,0:T(8,128)(2,1)}, u32[]{:S(2)}, u32[]{:S(2)}) async-start(bf16[8,2,48,2176]{3,2,1,0:T(8,128)(2,1)} %bitcast.156), calls=%async_computation.5 | async-start | bytes 6684672 | tf_op jit(solution)/shard_map/all_to_all | solution.py:632
  384.7 42.5 %all-to-all-start.6 = ((bf16[8,2,48,2048]{3,2,1,0:T(8,128)(2,1)}), bf16[8,2,48,2048]{3,2,1,0:T(8,128)(2,1)}, u32[]{:S(2)}, u32[]{:S(2)}) async-start(bf16[8,2,48,2048]{3,2,1,0:T(8,128)(2,1)} %bitcast.161), calls=%async_computation.6 | async-start | bytes 6291456 | tf_op jit(solution)/shard_map/all_to_all | solution.py:632
  427.2 44.5 %all-to-all-start.7 = ((bf16[8,2,48,2176]{3,2,1,0:T(8,128)(2,1)}), bf16[8,2,48,2176]{3,2,1,0:T(8,128)(2,1)}, u32[]{:S(2)}, u32[]{:S(2)}) async-start(bf16[8,2,48,2176]{3,2,1,0:T(8,128)(2,1)} %bitcast.158), calls=%async_computation.7 | async-start | bytes 6684672 | tf_op jit(solution)/shard_map/all_to_all | solution.py:632
  471.6 44.5 %all-to-all-start.8 = ((bf16[8,2,48,2176]{3,2,1,0:T(8,128)(2,1)}), bf16[8,2,48,2176]{3,2,1,0:T(8,128)(2,1)}, u32[]{:S(2)}, u32[]{:S(2)}) async-start(bf16[8,2,48,2176]{3,2,1,0:T(8,128)(2,1)} %get-tuple-element.107), calls=%async_computation.8 | async-start | bytes 6684672 | tf_op jit(solution)/shard_map/all_to_all | solution.py:632
  516.1 46.3 %all-to-all-start.9 = ((bf16[8,2,48,2176]{3,2,1,0:T(8,128)(2,1)}), bf16[8,2,48,2176]{3,2,1,0:T(8,128)(2,1)}, u32[]{:S(2)}, u32[]{:S(2)}) async-start(bf16[8,2,48,2176]{3,2,1,0:T(8,128)(2,1)} %get-tuple-element.109), calls=%async_computation.9 | async-start | bytes 6684672 | tf_op jit(solution)/shard_map/all_to_all | solution.py:632
  562.4 51.7 %all-to-all-start.10 = ((bf16[8,2,48,2176]{3,2,1,0:T(8,128)(2,1)}), bf16[8,2,48,2176]{3,2,1,0:T(8,128)(2,1)}, u32[]{:S(2)}, u32[]{:S(2)}) async-start(bf16[8,2,48,2176]{3,2,1,0:T(8,128)(2,1)} %get-tuple-element.114), calls=%async_computation.10 | async-start | bytes 6684672 | tf_op jit(solution)/shard_map/all_to_all | solution.py:632
  614.2 63.8 %all-to-all-start.11 = ((bf16[8,2,48,2176]{3,2,1,0:T(8,128)(2,1)}), bf16[8,2,48,2176]{3,2,1,0:T(8,128)(2,1)}, u32[]{:S(2)}, u32[]{:S(2)}) async-start(bf16[8,2,48,2176]{3,2,1,0:T(8,128)(2,1)} %get-tuple-element.119), calls=%async_computation.11 | async-start | bytes 6684672 | tf_op jit(solution)/shard_map/all_to_all | solution.py:632
  681.1 94.6 %all-to-all-start.12 = ((bf16[8,4,48,2048]{3,2,1,0:T(8,128)(2,1)}), bf16[8,4,48,2048]{3,2,1,0:T(8,128)(2,1)}, u32[]{:S(2)}, u32[]{:S(2)}) async-start(bf16[8,4,48,2048]{3,2,1,0:T(8,128)(2,1)} %expert_out.2), calls=%async_computation.12 | async-start | bytes 12582912 | tf_op jit(solution)/shard_map/all_to_all | solution.py:632
  813.5 57.2 %collective-permute-start.34 = (bf16[256,128]{1,0:T(8,128)(2,1)S(1)}, bf16[256,128]{1,0:T(8,128)(2,1)}, u32[]{:S(2)}, u32[]{:S(2)}) collective-permute-start(bf16[256,128]{1,0:T(8,128)(2,1)S(1)} %copy-done.64), channel_id=1, source_target_pairs={{0,2},{1,3},{2,0},{3,1},{4,6},{5,7},{6,4},{7,5},{8,10},{9,11},{10,... | collective-permute-start | bytes 196616 | tf_op jit(solution)/shard_map/ppermute | solution.py:53
  816.1 56.1 %collective-permute-start.35 = (bf16[256,128]{1,0:T(8,128)(2,1)S(1)}, bf16[256,128]{1,0:T(8,128)(2,1)}, u32[]{:S(2)}, u32[]{:S(2)}) collective-permute-start(bf16[256,128]{1,0:T(8,128)(2,1)S(1)} %copy-done.64), channel_id=1, source_target_pairs={{0,3},{1,0},{2,1},{3,2},{4,7},{5,4},{6,5},{7,6},{8,11},{9,8},{10,9... | collective-permute-start | bytes 196616 | tf_op jit(solution)/shard_map/ppermute | solution.py:53
  819.1 66.5 %collective-permute-start.37 = (bf16[4,256,512]{2,1,0:T(8,128)(2,1)}, bf16[4,256,512]{2,1,0:T(8,128)(2,1)}, u32[]{:S(2)}, u32[]{:S(2)}) collective-permute-start(bf16[4,256,512]{2,1,0:T(8,128)(2,1)} %dynamic-slice_bitcast_fusion.1), channel_id=1, source_target_pairs={{0,4},{4,0},{8,12},{12,8},{16,20},{20,16},{24,28},{28,24},{1,5},{5... | collective-permute-start | bytes 3145736 | tf_op jit(solution)/shard_map/ppermute | solution.py:850
  828.8 82.0 %all-to-all-start.13 = ((bf16[8,4,48,2048]{3,2,1,0:T(8,128)(2,1)}), bf16[8,4,48,2048]{3,2,1,0:T(8,128)(2,1)}, u32[]{:S(2)}, u32[]{:S(2)}) async-start(bf16[8,4,48,2048]{3,2,1,0:T(8,128)(2,1)} %expert_out.3), calls=%async_computation.13 | async-start | bytes 12582912 | tf_op jit(solution)/shard_map/all_to_all | solution.py:632
  843.4 39.6 %collective-permute-start.24 = (bf16[256,2048]{1,0:T(8,128)(2,1)}, bf16[256,2048]{1,0:T(8,128)(2,1)}, u32[]{:S(2)}, u32[]{:S(2)}) collective-permute-start(bf16[256,2048]{1,0:T(8,128)(2,1)} %fusion.67), channel_id=1, source_target_pairs={{0,1},{1,2},{2,3},{3,0},{4,5},{5,6},{6,7},{7,4},{8,9},{9,10},{10,1... | collective-permute-start | bytes 3145736 | tf_op jit(solution)/shard_map/ppermute | solution.py:53
  870.7 43.7 %collective-permute-start.36 = (bf16[4,256,1536]{2,1,0:T(8,128)(2,1)}, bf16[4,256,1536]{2,1,0:T(8,128)(2,1)}, u32[]{:S(2)}, u32[]{:S(2)}) collective-permute-start(bf16[4,256,1536]{2,1,0:T(8,128)(2,1)} %dynamic-slice_bitcast_fusion), channel_id=1, source_target_pairs={{0,4},{4,0},{8,12},{12,8},{16,20},{20,16},{24,28},{28,24},{1,5},{5... | collective-permute-start | bytes 9437192 | tf_op jit(solution)/shard_map/ppermute | solution.py:850
  885.6 51.7 %collective-permute-start.28 = (bf16[256,2048]{1,0:T(8,128)(2,1)}, bf16[256,2048]{1,0:T(8,128)(2,1)}, u32[]{:S(2)}, u32[]{:S(2)}) collective-permute-start(bf16[256,2048]{1,0:T(8,128)(2,1)} %add_convert_fusion.6), channel_id=1, source_target_pairs={{0,1},{1,2},{2,3},{3,0},{4,5},{5,6},{6,7},{7,4},{8,9},{9,10},{10,1... | collective-permute-start | bytes 3145736 | tf_op jit(solution)/shard_map/ppermute | solution.py:53
  910.8 43.4 %collective-permute-start.32 = (bf16[256,2048]{1,0:T(8,128)(2,1)S(1)}, bf16[256,2048]{1,0:T(8,128)(2,1)}, u32[]{:S(2)}, u32[]{:S(2)}) collective-permute-start(bf16[256,2048]{1,0:T(8,128)(2,1)S(1)} %add_convert_fusion.2), channel_id=1, source_target_pairs={{0,1},{1,2},{2,3},{3,0},{4,5},{5,6},{6,7},{7,4},{8,9},{9,10},{10,1... | collective-permute-start | bytes 3145736 | tf_op jit(solution)/shard_map/ppermute | solution.py:53
  926.9 53.6 %all-to-all-start.15 = ((bf16[4,256,2048]{2,1,0:T(8,128)(2,1)}), bf16[4,256,2048]{2,1,0:T(8,128)(2,1)}, u32[]{:S(2)}, u32[]{:S(2)}) async-start(bf16[4,256,2048]{2,1,0:T(8,128)(2,1)} %pad_maximum_fusion), calls=%async_computation.15 | async-start | bytes 8388608 | tf_op jit(solution)/shard_map/all_to_all | solution.py:860
  (140 other events, 2259.5 us)
Sparse Core Ops, SparseCore 0:
  10.5 72.5 all-gather.2
  85.0 31.9 all-gather.4

commit v2 on v1

--- a/solution.py
+++ b/solution.py
@@ -651,8 +651,8 @@
     squares = exchange_sum(
         jnp.stack([jnp.sum(query_raw * query_raw, -1), jnp.sum(key_raw * key_raw, -1)]), "col"
     )
+    squares = after(squares, g_blocks[1])
     g_blocks.append(shift(after(g_blocks[1], squares), "col"))
-    g_rows.append(to_experts(after(g_blocks[1], qkv), 1))
     inv_query = lax.rsqrt(squares[0] / width + EPSILON)[:, None]
     inv_key = lax.rsqrt(squares[1] / width + EPSILON)[:, None]
     cosines, sine_table = rope_tables(length, HEAD_DIM)
@@ -663,7 +663,7 @@
     *heads_out, attended, logs = attend(
         qkv, inv_query, inv_key, query_gain, key_gain, tables, doc_ids, block, factor
     )
-    attended = after(attended, g_blocks[2])
+    g_rows.append(to_experts(after(g_blocks[1], attended), 1))
     raw_grads = [down_t(rows, w_down, units) for rows in g_rows]
     g_rows.append(to_experts(g_blocks[2], 2))
     parts = [
@@ -674,7 +674,7 @@
         )
         for back in range(cols_total)
     ]
-    parts[2] = after(parts[2], raw_grads[0])
+    parts[2] = after(parts[2], raw_grads[0], g_blocks[2])
     parts[3] = after(parts[3], raw_grads[1])
     parts[0] = after(parts[0], g_rows[2])
     attn = ring_sum(parts, "col")
@@ -717,31 +717,39 @@
     grad_packed = share.astype(jnp.bfloat16)
     run_core()
     hiddens = [part[1] for part in core]
-    gate_grad = in_grads(b_rows, [part[2] for part in core], width)
-    up_grad = in_grads(b_rows, [part[3] for part in core], width)
-    down_grad = down_grads(hiddens, g_rows)
     order = list(range(1, cols_total)) + [0]
-    out_groups = [order[i : i + 2] for i in range(0, cols_total, 2)]
-    outs = [
-        expert_out([hiddens[back] for back in group], w_down, rows_total)
-        for group in out_groups
-    ]
-    totals = [None, None, grad_packed]
+    out_groups = [order[:2]] + [[back] for back in order[2:]]
+
+    def expert_outs(group, *earlier):
+        first = after(hiddens[group[0]], *earlier)
+        return expert_out([first] + [hiddens[b] for b in group[1:]], w_down, rows_total)
+
+    grad_gates = [after(core[0][2], grad_packed)] + [part[2] for part in core[1:]]
+    gate_grad = in_grads(b_rows, grad_gates, width)
+    outs = [expert_outs(out_groups[0], grad_packed)]
+    beside = [hiddens[last]]
     for back in range(2, cols_total):
-        beside = {2: [hiddens[last]], last: [gate_grad, outs[0]]}.get(back, [])
-        if totals[back - 1] is not None:
-            beside = beside + [totals[back - 1]]
         share = to_tokens(core[back][0], back, *beside)
         grad_packed = (shift(grad_packed, "col").astype(jnp.float32) + share).astype(
             jnp.bfloat16
         )
-        totals.append(grad_packed)
-    share = to_tokens(core[0][0], 0, up_grad, totals[-2], *outs[1:])
-    share = after(share, down_grad)
+        if back == 2:
+            grad_ups = [after(core[0][3], grad_packed)] + [part[3] for part in core[1:]]
+            up_grad = in_grads(b_rows, grad_ups, width)
+        if back < last:
+            outs.append(expert_outs(out_groups[back - 1], grad_packed))
+            beside = [gate_grad, outs[0]] if back == 2 else [outs[-2]]
+    share = to_tokens(core[0][0], 0, up_grad, outs[-1])
+    down_grad = down_grads([after(hiddens[0], grad_packed)] + hiddens[1:], g_rows)
+    outs += [expert_outs(group, grad_packed) for group in out_groups[len(outs) :]]
+    share = after(share, down_grad, *outs)
     grad_packed = shift(grad_packed, "col").astype(jnp.float32) + share
+
+    homes = []
 
     def outs_home(number):
         home = in_plane(outs[number])
+        homes.append(home)
         for slot, back in enumerate(out_groups[number]):
             rows = home[:, slot * owned : (slot + 1) * owned]
             rows = rows.reshape(rows_total * owned * capacity, width)
@@ -773,8 +781,7 @@
     incoming = after(natural(grad_blocks, place), out_shares[1])
     for number in range(1, len(outs)):
         outs_home(number)
-    moe = after(out_shares[1].astype(jnp.bfloat16), grad_blocks[-1])
-    moe = (shift(moe, "col").astype(jnp.float32) + out_shares[2]).astype(jnp.bfloat16)
+    moe = shift(after(out_shares[1].astype(jnp.bfloat16), grad_blocks[-1]), "col")
     wout_local = first_t(incoming, attended).astype(jnp.bfloat16)
     grad_out_heads = times_t(incoming, wo_full).astype(jnp.bfloat16)
     (
@@ -799,7 +806,9 @@
         block,
         factor,
     )
+    query_sum = after(query_sum, moe)
     sums = exchange_sum(jnp.stack([query_sum[:, 0], key_sum[:, 0]]), "col")
+    moe = (moe.astype(jnp.float32) + out_shares[2]).astype(jnp.bfloat16)
     small_blocks = hop_blocks(after(small, query_sum), "col")
     small_rows = natural(small_blocks, place)
     router_local = first_t(natural(b_blocks, place)[:, :width], small_rows[:, :expert_count])
@@ -815,12 +824,6 @@
         1,
     )
     early = jnp.sum(in_plane(early), 0)
-    moe = after(moe, sums)
-    for back in order[2:]:
-        moe = shift(moe, "col").astype(jnp.float32) + out_shares[back]
-        if back:
-            moe = moe.astype(jnp.bfloat16)
-    output = (residual + moe).astype(jnp.bfloat16)
     grad_query_b = (
         inv_query * query_scaled
         - query_raw * inv_query * inv_query * inv_query * (sums[0] / width)[:, None]
@@ -829,20 +832,37 @@
         inv_key * key_scaled - key_raw * inv_key * inv_key * inv_key * (sums[1] / width)[:, None]
     ).astype(jnp.bfloat16)
     grad_qkv = jnp.concatenate([grad_query_b, grad_key_b, grad_value_b], 1)
+    grad_qkv = after(grad_qkv, homes[1], *small_blocks[1:])
     da_parts = [
         times_t(block_of(grad_qkv, place - back, cols_total), wqkv) for back in range(cols_total)
     ]
     da_total = da_parts[1].astype(jnp.bfloat16)
     for back in range(2, cols_total):
         da_came = shift(da_total, "col")
+        da_total = (da_came.astype(jnp.float32) + da_parts[back]).astype(jnp.bfloat16)
         if back == 2:
-            first_came = da_came
-        da_total = (da_came.astype(jnp.float32) + da_parts[back]).astype(jnp.bfloat16)
+            da_second = da_total
+        if back == last:
+            da_total = after(da_total, early)
+    moe = after(moe, da_came)
+    for back in order[2:]:
+        moe = shift(moe, "col").astype(jnp.float32) + out_shares[back]
+        if back:
+            moe = moe.astype(jnp.bfloat16)
+    output = (residual + moe).astype(jnp.bfloat16)
     grad_normal_a = shift(da_total, "col").astype(jnp.float32) + da_parts[0]
-    wqkv_local = first_t(seq_rows, after(grad_qkv, first_came)).astype(jnp.bfloat16)
+    wqkv_local = first_t(seq_rows, after(grad_qkv, da_second, homes[-1])).astype(jnp.bfloat16)
     attn_gain_local = (
         jnp.sum(wqkv.astype(jnp.float32) * wqkv_local.astype(jnp.float32), -1) / attn_gain
     )
+    late = jnp.concatenate([attn_gain_local, query_gain_local[0], key_gain_local[0]])
+    late = jnp.concatenate([early.reshape(-1), late]).reshape(1, -1, 128)
+    spread = in_plane(jnp.broadcast_to(late, (rows_total,) + late.shape[1:]))
+    spread = spread.reshape(rows_total, -1)
+    late = jnp.sum(spread[:, early.size :], 0)
+    early = spread[:, : early.size].reshape((rows_total,) + early.shape)
+    attn_gain_grad = exchange_sum(late[:width], "col", place)
+
     core_place = row_place % 2
 
     def over_cores(value):
@@ -865,15 +885,6 @@
         tiled=True,
         axis_index_groups=[list(range(core, rows_total, 2)) for core in range(2)],
     )
-    queue.append(pair)
-    late = jnp.concatenate([attn_gain_local, query_gain_local[0], key_gain_local[0]])
-    late = jnp.concatenate([early.reshape(-1), late]).reshape(1, -1, 128)
-    spread = in_plane(jnp.broadcast_to(late, (rows_total,) + late.shape[1:]))
-    spread = spread.reshape(rows_total, -1)
-    late = jnp.sum(spread[:, early.size :], 0)
-    early = spread[:, : early.size].reshape((rows_total,) + early.shape)
-    attn_gain_grad = exchange_sum(late[:width], "col", place)
-
     weight_grads = jnp.sum(pair.astype(jnp.float32), 0)
     wqkv_grad = weight_grads[:, : 3 * head_cols]
     out_proj_grad = weight_grads[:, 3 * head_cols :].T

time: 1020 us -> 1000 us (0.980)
  waiting for transfers between devices: 414 us -> 386 us
  starting transfers between devices: 105 us -> 117 us
    ppermute x39, waiting for transfers between devices: 322 us -> 284 us  [shift(): lax.ppermute(value, axis, [(i, (i + step) % count) for i in range(count)])]
    all_to_all x16 -> x17, waiting for transfers between devices: 91.7 us -> 100 us  [in_plane(): lax.all_to_all(table, 'row', split_axis=0, concat_axis=0, tiled=True)]
    all_to_all x16 -> x17, starting transfers between devices: 71.1 us -> 77.2 us  [in_plane(): lax.all_to_all(table, 'row', split_axis=0, concat_axis=0, tiled=True)]
    pallas_call x2 -> x3, Pallas kernels: 30.2 us -> 30 us  [expert_out(): pl.pallas_call(expert_out_kernel, grid=(count, owned, width // tile), in_...]
  transfers between devices with their start and end apart: 60 -> 61, of which waited for: 30 -> 32; matrix products, arithmetic and copies ran while one was open for 18% -> 19% of each run, Pallas kernels for 23% -> 25%
where the time goes in v2:
time: 1000 us; the launch traced here: 995 us
  waiting for transfers between devices  386 us (39%)
  Pallas kernels  252 us (25%)
  matrix products  120 us (12%)
  starting transfers between devices  117 us (12%)
  local copies, waits for them, and re-layouts  60.5 us (6%)
  other arithmetic  44.4 us (4%)
  between operations  16.3 us (2%)
    ppermute x39, waiting for transfers between devices, shift(): lax.ppermute(value, axis, [(i, (i + step) % count) for i in range(count)])  284 us
    all_to_all x17, waiting for transfers between devices, in_plane(): lax.all_to_all(table, 'row', split_axis=0, concat_axis=0, tiled=True)  100 us
    pallas_call x4, Pallas kernels, expert_core(): pl.pallas_call(expert_kernel, grid=(owned, tiles), in_specs=[packed_spec,...  83.9 us
    all_to_all x17, starting transfers between devices, in_plane(): lax.all_to_all(table, 'row', split_axis=0, concat_axis=0, tiled=True)  77.2 us
    dot_general x11, matrix products, first_t(): lax.dot_general(left, right, (((0,), (0,)), ((), ())), preferred_element_...  46.6 us
    pallas_call x2, Pallas kernels, in_grads(): pl.pallas_call(functools.partial(in_grads_kernel, count), grid=(owned, wi...  46.5 us
    pallas_call x4, Pallas kernels, down_t(): pl.pallas_call(down_t_kernel, grid=(owned, tiles), in_specs=[pl.BlockSpec...  35.1 us
    ppermute x39, starting transfers between devices, shift(): lax.ppermute(value, axis, [(i, (i + step) % count) for i in range(count)])  34.8 us
  transfers between devices with their start and end apart: 61, of which 32 were waited for; matrix products, arithmetic and copies ran while one was open for 19% of the time, Pallas kernels for 25%

profile of v2, /device:TPU:0, one launch (start us, length us, event | category | flops | bytes accessed | tf_op | source)
XLA Modules:
  0.0 995.2 jit_solution(2495467600115824219)
XLA Ops:
  33.1 13.1 %collective-permute-done = bf16[256,2048]{1,0:T(8,128)(2,1)} collective-permute-done((bf16[256,2048]{1,0:T(8,128)(2,1)}, bf16[256,2048]{1,0:T(8,128)(2,1)}, u32[]{:S(2)}, u32[]{:S(2)}) %collective-permute-start) | collective-permute-done | bytes 1048608 | tf_op jit(solution)/shard_map/ppermute | solution.py:53
  47.7 23.7 %collective-permute-done.1 = bf16[256,2048]{1,0:T(8,128)(2,1)} collective-permute-done((bf16[256,2048]{1,0:T(8,128)(2,1)}, bf16[256,2048]{1,0:T(8,128)(2,1)}, u32[]{:S(2)}, u32[]{:S(2)}) %collective-permute-start.1) | collective-permute-done | bytes 1048608 | tf_op jit(solution)/shard_map/ppermute | solution.py:53
  79.2 16.6 %collective-permute-done.2 = bf16[256,2048]{1,0:T(8,128)(2,1)} collective-permute-done((bf16[256,2048]{1,0:T(8,128)(2,1)}, bf16[256,2048]{1,0:T(8,128)(2,1)}, u32[]{:S(2)}, u32[]{:S(2)}) %collective-permute-start.2) | collective-permute-done | bytes 1048608 | tf_op jit(solution)/shard_map/ppermute | solution.py:53
  122.5 13.3 %attend.1 = (bf16[1024,512]{1,0:T(8,128)(2,1)}, bf16[1024,512]{1,0:T(8,128)(2,1)}, bf16[1024,512]{1,0:T(8,128)(2,1)}, bf16[1024,512]{1,0:T(8,128)(2,1)}, f32[4,1,1024]{2,1,0:T(1,128)S(1)}) custom-call(f32[1024,1536]{1,0:T(8,128)} %copy-done.22, f32[1024,1536]{1,0:T(8,128)} %copy-done.22, f32[1024,1536]{1,0:T(8,128)} %copy-done.22, ...), custom_call_target="tpu_custom_call" | custom-call | flops 12884901888 | bytes 10485760 | tf_op jit(solution)/shard_map/attend/pallas_call | solution.py:394
  160.3 12.0 %collective-permute-done.8 = bf16[256,2048]{1,0:T(8,128)(2,1)} collective-permute-done((bf16[256,2048]{1,0:T(8,128)(2,1)}, bf16[256,2048]{1,0:T(8,128)(2,1)}, u32[]{:S(2)}, u32[]{:S(2)}) %collective-permute-start.8) | collective-permute-done | bytes 1048608 | tf_op jit(solution)/shard_map/ppermute | solution.py:53
  205.8 16.9 %collective-permute-done.9 = bf16[256,2048]{1,0:T(8,128)(2,1)S(1)} collective-permute-done((bf16[256,2048]{1,0:T(8,128)(2,1)S(1)}, bf16[256,2048]{1,0:T(8,128)(2,1)S(1)}, u32[]{:S(2)}, u32[]{:S(2)}) %collective-permute-start.9) | collective-permute-done | bytes 1048608 | tf_op jit(solution)/shard_map/ppermute | solution.py:53
  226.5 23.7 %collective-permute-done.11 = bf16[256,2048]{1,0:T(8,128)(2,1)} collective-permute-done((bf16[256,2048]{1,0:T(8,128)(2,1)}, bf16[256,2048]{1,0:T(8,128)(2,1)}, u32[]{:S(2)}, u32[]{:S(2)}) %collective-permute-start.11) | collective-permute-done | bytes 1048608 | tf_op jit(solution)/shard_map/ppermute | solution.py:53
  271.7 19.9 %collective-permute-done.13 = bf16[256,2176]{1,0:T(8,128)(2,1)S(1)} collective-permute-done((bf16[256,2176]{1,0:T(8,128)(2,1)S(1)}, bf16[256,2176]{1,0:T(8,128)(2,1)S(1)}, u32[]{:S(2)}, u32[]{:S(2)}) %collective-permute-start.13) | collective-permute-done | bytes 1114144 | tf_op jit(solution)/shard_map/ppermute | solution.py:53
  307.7 21.0 %expert_core.5 = (bf16[8,2,48,2176]{3,2,1,0:T(8,128)(2,1)}, bf16[2,384,1024]{2,1,0:T(8,128)(2,1)S(1)}, bf16[2,384,1024]{2,1,0:T(8,128)(2,1)}, bf16[2,384,1024]{2,1,0:T(8,128)(2,1)}) custom-call(bf16[8,2,48,2176]{3,2,1,0:T(8,128)(2,1)} %all-to-all-done.3.rows_ref.refs_0_, bf16[2048,2048]{1,0:T(8,128)(2,1)} %gate_ref.7, bf16[2048,2048]{1,0:T(8,128)(2,1)} %up_ref.7, ...), custom_call_target="tpu_custom_call" | custom-call | flops 12884901888 | bytes 39845888 | tf_op jit(solution)/shard_map/expert_core/pallas_call | solution.py:218
  352.1 20.9 %expert_core.4 = (bf16[8,2,48,2176]{3,2,1,0:T(8,128)(2,1)}, bf16[2,384,1024]{2,1,0:T(8,128)(2,1)S(1)}, bf16[2,384,1024]{2,1,0:T(8,128)(2,1)}, bf16[2,384,1024]{2,1,0:T(8,128)(2,1)}) custom-call(bf16[8,2,48,2176]{3,2,1,0:T(8,128)(2,1)} %all-to-all-done.4.rows_ref.refs_1_, bf16[2048,2048]{1,0:T(8,128)(2,1)} %gate_ref.7, bf16[2048,2048]{1,0:T(8,128)(2,1)} %up_ref.7, ...), custom_call_target="tpu_custom_call" | custom-call | flops 12884901888 | bytes 39845888 | tf_op jit(solution)/shard_map/expert_core/pallas_call | solution.py:218
  396.4 20.9 %expert_core.6 = (bf16[8,2,48,2176]{3,2,1,0:T(8,128)(2,1)}, bf16[2,384,1024]{2,1,0:T(8,128)(2,1)S(1)}, bf16[2,384,1024]{2,1,0:T(8,128)(2,1)}, bf16[2,384,1024]{2,1,0:T(8,128)(2,1)}) custom-call(bf16[8,2,48,2176]{3,2,1,0:T(8,128)(2,1)} %all-to-all-done.5.rows_ref.refs_2_, bf16[2048,2048]{1,0:T(8,128)(2,1)} %gate_ref.7, bf16[2048,2048]{1,0:T(8,128)(2,1)} %up_ref.7, ...), custom_call_target="tpu_custom_call" | custom-call | flops 12884901888 | bytes 39845888 | tf_op jit(solution)/shard_map/expert_core/pallas_call | solution.py:218
  447.4 31.2 %all-to-all-done.7.rows_ref.refs_3_ = bf16[8,2,48,2176]{3,2,1,0:T(8,128)(2,1)} async-done(((bf16[8,2,48,2176]{3,2,1,0:T(8,128)(2,1)}), bf16[8,2,48,2176]{3,2,1,0:T(8,128)(2,1)}, u32[]{:S(2)}, u32[]{:S(2)}) %all-to-all-start.7) | async-done | bytes 3342368 | tf_op jit(solution)/shard_map/all_to_all | solution.py:632
  483.4 21.0 %expert_core.7 = (bf16[8,2,48,2176]{3,2,1,0:T(8,128)(2,1)}, bf16[2,384,1024]{2,1,0:T(8,128)(2,1)S(1)}, bf16[2,384,1024]{2,1,0:T(8,128)(2,1)}, bf16[2,384,1024]{2,1,0:T(8,128)(2,1)}) custom-call(bf16[8,2,48,2176]{3,2,1,0:T(8,128)(2,1)} %all-to-all-done.7.rows_ref.refs_3_, bf16[2048,2048]{1,0:T(8,128)(2,1)} %gate_ref.7, bf16[2048,2048]{1,0:T(8,128)(2,1)} %up_ref.7, ...), custom_call_target="tpu_custom_call" | custom-call | flops 12884901888 | bytes 39845888 | tf_op jit(solution)/shard_map/expert_core/pallas_call | solution.py:218
  504.4 19.0 %all-to-all-done.8 = bf16[8,2,48,2176]{3,2,1,0:T(8,128)(2,1)} async-done(((bf16[8,2,48,2176]{3,2,1,0:T(8,128)(2,1)}), bf16[8,2,48,2176]{3,2,1,0:T(8,128)(2,1)}, u32[]{:S(2)}, u32[]{:S(2)}) %all-to-all-start.8) | async-done | bytes 3342368 | tf_op jit(solution)/shard_map/all_to_all | solution.py:632
  532.2 23.3 %in_grads.2 = f32[2048,2048]{1,0:T(8,128)} custom-call(bf16[8,2,48,2176]{3,2,1,0:T(8,128)(2,1)} %all-to-all-done.3.rows_ref.refs_0_, bf16[8,2,48,2176]{3,2,1,0:T(8,128)(2,1)} %all-to-all-done.4.rows_ref.refs_1_, bf16[8,2,48,2176]{3,2,1,0:T(8,128)(2,1)} %all-to-all-done.5.rows_ref.refs_2_, bf16[8,2,48,2176]{3,2,1,0:T(8,128)(2,1)} %all-to-all-done.7.rows_ref.refs_3_, ...), custom_call_target="tpu_custom_call" | custom-call | flops 12884901888 | bytes 16777216 | tf_op jit(solution)/shard_map/in_grads/pallas_call | solution.py:296
  555.6 15.0 %expert_out.3 = bf16[8,4,48,2048]{3,2,1,0:T(8,128)(2,1)} custom-call(bf16[2,384,1024]{2,1,0:T(8,128)(2,1)S(1)} %copy-done.13, bf16[2,384,1024]{2,1,0:T(8,128)(2,1)} %copy-done.14, bf16[2048,2048]{1,0:T(8,128)(2,1)} %refs_1_.3), custom_call_target="tpu_custom_call" | custom-call | flops 6442450944 | bytes 23068672 | tf_op jit(solution)/shard_map/expert_out/pallas_call | solution.py:264
  579.9 23.2 %in_grads.3 = f32[2048,2048]{1,0:T(8,128)} custom-call(bf16[8,2,48,2176]{3,2,1,0:T(8,128)(2,1)} %all-to-all-done.3.rows_ref.refs_0_, bf16[8,2,48,2176]{3,2,1,0:T(8,128)(2,1)} %all-to-all-done.4.rows_ref.refs_1_, bf16[8,2,48,2176]{3,2,1,0:T(8,128)(2,1)} %all-to-all-done.5.rows_ref.refs_2_, bf16[8,2,48,2176]{3,2,1,0:T(8,128)(2,1)} %all-to-all-done.7.rows_ref.refs_3_, ...), custom_call_target="tpu_custom_call" | custom-call | flops 12884901888 | bytes 16777216 | tf_op jit(solution)/shard_map/in_grads/pallas_call | solution.py:296
  625.1 26.0 %down_grads.1 = f32[2048,2048]{1,0:T(8,128)} custom-call(bf16[2,384,1024]{2,1,0:T(8,128)(2,1)S(1)} %get-tuple-element.134.refs_0_, bf16[2,384,1024]{2,1,0:T(8,128)(2,1)} %copy-done.12, bf16[2,384,1024]{2,1,0:T(8,128)(2,1)} %copy-done.14, bf16[2,384,1024]{2,1,0:T(8,128)(2,1)} %copy-done.1, bf16[8,2,48,2048]{3,2,1,0:T(8,128)(2,1)} %all-to-all-done.grad_ref.refs_4_, ...), custom_call_target="tpu_custom_call" | custom-call | flops 12884901888 | bytes 16777216 | tf_op jit(solution)/shard_map/down_grads/pallas_call | solution.py:328
  676.2 27.5 %collective-permute-done.21 = bf16[256,2048]{1,0:T(8,128)(2,1)S(1)} collective-permute-done((bf16[256,2048]{1,0:T(8,128)(2,1)S(1)}, bf16[256,2048]{1,0:T(8,128)(2,1)S(1)}, u32[]{:S(2)}, u32[]{:S(2)}) %collective-permute-start.21) | collective-permute-done | bytes 1048608 | tf_op jit(solution)/shard_map/ppermute | solution.py:53
  703.8 26.7 %collective-permute-done.22 = bf16[256,2048]{1,0:T(8,128)(2,1)} collective-permute-done((bf16[256,2048]{1,0:T(8,128)(2,1)S(1)}, bf16[256,2048]{1,0:T(8,128)(2,1)}, u32[]{:S(2)}, u32[]{:S(2)}) %collective-permute-start.22) | collective-permute-done | bytes 1048608 | tf_op jit(solution)/shard_map/ppermute | solution.py:53
  739.5 17.0 %collective-permute-done.23 = bf16[256,2048]{1,0:T(8,128)(2,1)} collective-permute-done((bf16[256,2048]{1,0:T(8,128)(2,1)}, bf16[256,2048]{1,0:T(8,128)(2,1)}, u32[]{:S(2)}, u32[]{:S(2)}) %collective-permute-start.23) | collective-permute-done | bytes 1048608 | tf_op jit(solution)/shard_map/ppermute | solution.py:53
  777.2 17.0 %attend_back.1 = (f32[1024,512]{1,0:T(8,128)}, f32[1024,512]{1,0:T(8,128)}, bf16[1024,512]{1,0:T(8,128)(2,1)}, f32[1024,1]{1,0:T(8,128)S(1)}, f32[1024,1]{1,0:T(...) custom-call(bf16[1024,512]{1,0:T(8,128)(2,1)} %get-tuple-element.137.query_ref, ...), custom_call_target="tpu_custom_call" | custom-call | flops 21474836480 | bytes 20971520 | tf_op jit(solution)/shard_map/attend_back/pallas_call | solution.py:498
  827.8 23.3 %collective-permute-done.31 = bf16[256,2048]{1,0:T(8,128)(2,1)S(1)} collective-permute-done((bf16[256,2048]{1,0:T(8,128)(2,1)S(1)}, bf16[256,2048]{1,0:T(8,128)(2,1)S(1)}, u32[]{:S(2)}, u32[]{:S(2)}) %collective-permute-start.31) | collective-permute-done | bytes 1048608 | tf_op jit(solution)/shard_map/ppermute | solution.py:53
  892.3 14.8 %collective-permute-done.33 = bf16[256,2048]{1,0:T(8,128)(2,1)} collective-permute-done((bf16[256,2048]{1,0:T(8,128)(2,1)}, bf16[256,2048]{1,0:T(8,128)(2,1)}, u32[]{:S(2)}, u32[]{:S(2)}) %collective-permute-start.33) | collective-permute-done | bytes 1048608 | tf_op jit(solution)/shard_map/ppermute | solution.py:53
  (466 shorter events, 491.6 us)
Async XLA Ops:
  7.2 90.9 %all-gather.3.cloned.1.call-start = ((), (), s32[]{:S(2)}) async-start(), calls=%async_computation.18 | async-start | bytes 7077888 | tf_op jit(solution)/shard_map/all_gather | solution.py:600
  28.6 69.5 %all-to-all-start = ((bf16[8,2,48,2048]{3,2,1,0:T(8,128)(2,1)}), bf16[8,2,48,2048]{3,2,1,0:T(8,128)(2,1)}, u32[]{:S(2)}, u32[]{:S(2)}) async-start(bf16[8,2,48,2048]{3,2,1,0:T(8,128)(2,1)} %bitcast.2), calls=%async_computation | async-start | bytes 6291456 | tf_op jit(solution)/shard_map/all_to_all | solution.py:632
  33.1 111.6 %all-gather.5.cloned.1.call-start = ((), (), s32[]{:S(2)}) async-start(), calls=%async_computation.19 | async-start | bytes 2359296 | tf_op jit(solution)/shard_map/all_gather | solution.py:603
  139.7 42.3 %all-to-all-start.1 = ((bf16[8,2,48,2048]{3,2,1,0:T(8,128)(2,1)}), bf16[8,2,48,2048]{3,2,1,0:T(8,128)(2,1)}, u32[]{:S(2)}, u32[]{:S(2)}) async-start(bf16[8,2,48,2048]{3,2,1,0:T(8,128)(2,1)} %bitcast.12), calls=%async_computation.1 | async-start | bytes 6291456 | tf_op jit(solution)/shard_map/all_to_all | solution.py:632
  148.1 46.1 %collective-permute-start.7 = (bf16[256,2048]{1,0:T(8,128)(2,1)}, bf16[256,2048]{1,0:T(8,128)(2,1)}, u32[]{:S(2)}, u32[]{:S(2)}) collective-permute-start(bf16[256,2048]{1,0:T(8,128)(2,1)} %convolution_convert_fusion.11), channel_id=1, source_target_pairs={{0,1},{1,2},{2,3},{3,0},{4,5},{5,6},{6,7},{7,4},{8,9},{9,10},{10,1... | collective-permute-start | bytes 3145736 | tf_op jit(solution)/shard_map/ppermute | solution.py:53
  182.1 44.4 %all-to-all-start.2 = ((bf16[8,2,48,2048]{3,2,1,0:T(8,128)(2,1)}), bf16[8,2,48,2048]{3,2,1,0:T(8,128)(2,1)}, u32[]{:S(2)}, u32[]{:S(2)}) async-start(bf16[8,2,48,2048]{3,2,1,0:T(8,128)(2,1)} %bitcast.159), calls=%async_computation.2 | async-start | bytes 6291456 | tf_op jit(solution)/shard_map/all_to_all | solution.py:632
  258.4 44.5 %all-to-all-start.3 = ((bf16[8,2,48,2176]{3,2,1,0:T(8,128)(2,1)}), bf16[8,2,48,2176]{3,2,1,0:T(8,128)(2,1)}, u32[]{:S(2)}, u32[]{:S(2)}) async-start(bf16[8,2,48,2176]{3,2,1,0:T(8,128)(2,1)} %bitcast.157), calls=%async_computation.3 | async-start | bytes 6684672 | tf_op jit(solution)/shard_map/all_to_all | solution.py:632
  302.9 44.5 %all-to-all-start.4 = ((bf16[8,2,48,2176]{3,2,1,0:T(8,128)(2,1)}), bf16[8,2,48,2176]{3,2,1,0:T(8,128)(2,1)}, u32[]{:S(2)}, u32[]{:S(2)}) async-start(bf16[8,2,48,2176]{3,2,1,0:T(8,128)(2,1)} %bitcast.155), calls=%async_computation.4 | async-start | bytes 6684672 | tf_op jit(solution)/shard_map/all_to_all | solution.py:632
  347.4 44.5 %all-to-all-start.5 = ((bf16[8,2,48,2176]{3,2,1,0:T(8,128)(2,1)}), bf16[8,2,48,2176]{3,2,1,0:T(8,128)(2,1)}, u32[]{:S(2)}, u32[]{:S(2)}) async-start(bf16[8,2,48,2176]{3,2,1,0:T(8,128)(2,1)} %bitcast.156), calls=%async_computation.5 | async-start | bytes 6684672 | tf_op jit(solution)/shard_map/all_to_all | solution.py:632
  391.8 42.3 %all-to-all-start.6 = ((bf16[8,2,48,2048]{3,2,1,0:T(8,128)(2,1)}), bf16[8,2,48,2048]{3,2,1,0:T(8,128)(2,1)}, u32[]{:S(2)}, u32[]{:S(2)}) async-start(bf16[8,2,48,2048]{3,2,1,0:T(8,128)(2,1)} %bitcast.160), calls=%async_computation.6 | async-start | bytes 6291456 | tf_op jit(solution)/shard_map/all_to_all | solution.py:632
  434.2 44.5 %all-to-all-start.7 = ((bf16[8,2,48,2176]{3,2,1,0:T(8,128)(2,1)}), bf16[8,2,48,2176]{3,2,1,0:T(8,128)(2,1)}, u32[]{:S(2)}, u32[]{:S(2)}) async-start(bf16[8,2,48,2176]{3,2,1,0:T(8,128)(2,1)} %bitcast.158), calls=%async_computation.7 | async-start | bytes 6684672 | tf_op jit(solution)/shard_map/all_to_all | solution.py:632
  478.6 44.7 %all-to-all-start.8 = ((bf16[8,2,48,2176]{3,2,1,0:T(8,128)(2,1)}), bf16[8,2,48,2176]{3,2,1,0:T(8,128)(2,1)}, u32[]{:S(2)}, u32[]{:S(2)}) async-start(bf16[8,2,48,2176]{3,2,1,0:T(8,128)(2,1)} %get-tuple-element.113), calls=%async_computation.8 | async-start | bytes 6684672 | tf_op jit(solution)/shard_map/all_to_all | solution.py:632
  523.4 47.1 %all-to-all-start.9 = ((bf16[8,2,48,2176]{3,2,1,0:T(8,128)(2,1)}), bf16[8,2,48,2176]{3,2,1,0:T(8,128)(2,1)}, u32[]{:S(2)}, u32[]{:S(2)}) async-start(bf16[8,2,48,2176]{3,2,1,0:T(8,128)(2,1)} %get-tuple-element.119), calls=%async_computation.9 | async-start | bytes 6684672 | tf_op jit(solution)/shard_map/all_to_all | solution.py:632
  532.2 43.2 %collective-permute-start.18 = (bf16[256,2176]{1,0:T(8,128)(2,1)}, bf16[256,2176]{1,0:T(8,128)(2,1)}, u32[]{:S(2)}, u32[]{:S(2)}) collective-permute-start(bf16[256,2176]{1,0:T(8,128)(2,1)} %convolution_convert_fusion.5), channel_id=1, source_target_pairs={{0,1},{1,2},{2,3},{3,0},{4,5},{5,6},{6,7},{7,4},{8,9},{9,10},{10,1... | collective-permute-start | bytes 3342344 | tf_op jit(solution)/shard_map/ppermute | solution.py:53
  570.5 44.7 %all-to-all-start.10 = ((bf16[8,2,48,2176]{3,2,1,0:T(8,128)(2,1)}), bf16[8,2,48,2176]{3,2,1,0:T(8,128)(2,1)}, u32[]{:S(2)}, u32[]{:S(2)}) async-start(bf16[8,2,48,2176]{3,2,1,0:T(8,128)(2,1)} %get-tuple-element.125), calls=%async_computation.10 | async-start | bytes 6684672 | tf_op jit(solution)/shard_map/all_to_all | solution.py:632
  579.9 40.7 %collective-permute-start.19 = (bf16[256,2176]{1,0:T(8,128)(2,1)}, bf16[256,2176]{1,0:T(8,128)(2,1)}, u32[]{:S(2)}, u32[]{:S(2)}) collective-permute-start(bf16[256,2176]{1,0:T(8,128)(2,1)} %add_convert_fusion.1), channel_id=1, source_target_pairs={{0,1},{1,2},{2,3},{3,0},{4,5},{5,6},{6,7},{7,4},{8,9},{9,10},{10,1... | collective-permute-start | bytes 3342344 | tf_op jit(solution)/shard_map/ppermute | solution.py:53
  615.2 45.0 %all-to-all-start.11 = ((bf16[8,2,48,2176]{3,2,1,0:T(8,128)(2,1)}), bf16[8,2,48,2176]{3,2,1,0:T(8,128)(2,1)}, u32[]{:S(2)}, u32[]{:S(2)}) async-start(bf16[8,2,48,2176]{3,2,1,0:T(8,128)(2,1)} %get-tuple-element.132), calls=%async_computation.11 | async-start | bytes 6684672 | tf_op jit(solution)/shard_map/all_to_all | solution.py:632
  625.1 43.1 %collective-permute-start.20 = (bf16[256,2176]{1,0:T(8,128)(2,1)}, bf16[256,2176]{1,0:T(8,128)(2,1)S(1)}, u32[]{:S(2)}, u32[]{:S(2)}) collective-permute-start(bf16[256,2176]{1,0:T(8,128)(2,1)} %add_convert_fusion), channel_id=1, source_target_pairs={{0,1},{1,2},{2,3},{3,0},{4,5},{5,6},{6,7},{7,4},{8,9},{9,10},{10,1... | collective-permute-start | bytes 3342344 | tf_op jit(solution)/shard_map/ppermute | solution.py:53
  660.2 98.6 %all-to-all-start.12 = ((bf16[8,4,48,2048]{3,2,1,0:T(8,128)(2,1)}), bf16[8,4,48,2048]{3,2,1,0:T(8,128)(2,1)}, u32[]{:S(2)}, u32[]{:S(2)}) async-start(bf16[8,4,48,2048]{3,2,1,0:T(8,128)(2,1)} %expert_out.3), calls=%async_computation.12 | async-start | bytes 12582912 | tf_op jit(solution)/shard_map/all_to_all | solution.py:632
  766.2 42.5 %all-to-all-start.13 = ((bf16[8,2,48,2048]{3,2,1,0:T(8,128)(2,1)}), bf16[8,2,48,2048]{3,2,1,0:T(8,128)(2,1)}, u32[]{:S(2)}, u32[]{:S(2)}) async-start(bf16[8,2,48,2048]{3,2,1,0:T(8,128)(2,1)} %expert_out.4), calls=%async_computation.13 | async-start | bytes 6291456 | tf_op jit(solution)/shard_map/all_to_all | solution.py:632
  808.7 45.4 %all-to-all-start.14 = ((bf16[8,2,48,2048]{3,2,1,0:T(8,128)(2,1)}), bf16[8,2,48,2048]{3,2,1,0:T(8,128)(2,1)}, u32[]{:S(2)}, u32[]{:S(2)}) async-start(bf16[8,2,48,2048]{3,2,1,0:T(8,128)(2,1)} %expert_out.5), calls=%async_computation.14 | async-start | bytes 6291456 | tf_op jit(solution)/shard_map/all_to_all | solution.py:632
  870.0 49.7 %collective-permute-start.39 = (bf16[4,256,1536]{2,1,0:T(8,128)(2,1)}, bf16[4,256,1536]{2,1,0:T(8,128)(2,1)}, u32[]{:S(2)}, u32[]{:S(2)}) collective-permute-start(bf16[4,256,1536]{2,1,0:T(8,128)(2,1)} %dynamic-slice_bitcast_fusion), channel_id=1, source_target_pairs={{0,4},{4,0},{8,12},{12,8},{16,20},{20,16},{24,28},{28,24},{1,5},{5... | collective-permute-start | bytes 9437192 | tf_op jit(solution)/shard_map/ppermute | solution.py:870
  911.3 56.2 %collective-permute-start.34 = (bf16[256,2048]{1,0:T(8,128)(2,1)}, bf16[256,2048]{1,0:T(8,128)(2,1)}, u32[]{:S(2)}, u32[]{:S(2)}) collective-permute-start(bf16[256,2048]{1,0:T(8,128)(2,1)} %add_convert_fusion.4), channel_id=1, source_target_pairs={{0,1},{1,2},{2,3},{3,0},{4,5},{5,6},{6,7},{7,4},{8,9},{9,10},{10,1... | collective-permute-start | bytes 3145736 | tf_op jit(solution)/shard_map/ppermute | solution.py:53
  930.9 51.6 %all-to-all-start.17 = ((bf16[4,256,2048]{2,1,0:T(8,128)(2,1)}), bf16[4,256,2048]{2,1,0:T(8,128)(2,1)}, u32[]{:S(2)}, u32[]{:S(2)}) async-start(bf16[4,256,2048]{2,1,0:T(8,128)(2,1)} %pad_maximum_fusion), calls=%async_computation.17 | async-start | bytes 8388608 | tf_op jit(solution)/shard_map/all_to_all | solution.py:880
  (133 other events, 2034.5 us)
Sparse Core Ops, SparseCore 0:
  10.5 69.6 all-gather.2
  82.1 33.8 all-gather.4

commit v3 on v2

--- a/solution.py
+++ b/solution.py
@@ -664,6 +664,7 @@
         qkv, inv_query, inv_key, query_gain, key_gain, tables, doc_ids, block, factor
     )
     g_rows.append(to_experts(after(g_blocks[1], attended), 1))
+    attended = after(attended, g_blocks[2])
     raw_grads = [down_t(rows, w_down, units) for rows in g_rows]
     g_rows.append(to_experts(g_blocks[2], 2))
     parts = [
@@ -674,7 +675,7 @@
         )
         for back in range(cols_total)
     ]
-    parts[2] = after(parts[2], raw_grads[0], g_blocks[2])
+    parts[2] = after(parts[2], raw_grads[0])
     parts[3] = after(parts[3], raw_grads[1])
     parts[0] = after(parts[0], g_rows[2])
     attn = ring_sum(parts, "col")
@@ -778,12 +779,13 @@
     )
 
     grad_blocks = ring_blocks(grad_attn, "col")
-    incoming = after(natural(grad_blocks, place), out_shares[1])
+    grad_out_heads = natural(
+        [times_t(block_grad, wo_full).astype(jnp.bfloat16) for block_grad in grad_blocks], place
+    )
+    grad_out_heads = after(grad_out_heads, out_shares[1])
     for number in range(1, len(outs)):
         outs_home(number)
     moe = shift(after(out_shares[1].astype(jnp.bfloat16), grad_blocks[-1]), "col")
-    wout_local = first_t(incoming, attended).astype(jnp.bfloat16)
-    grad_out_heads = times_t(incoming, wo_full).astype(jnp.bfloat16)
     (
         query_scaled,
         key_scaled,
@@ -806,6 +808,9 @@
         block,
         factor,
     )
+    wout_local = first_t(
+        after(natural(grad_blocks, place), query_sum), attended
+    ).astype(jnp.bfloat16)
     query_sum = after(query_sum, moe)
     sums = exchange_sum(jnp.stack([query_sum[:, 0], key_sum[:, 0]]), "col")
     moe = (moe.astype(jnp.float32) + out_shares[2]).astype(jnp.bfloat16)
@@ -823,6 +828,7 @@
         ],
         1,
     )
+    early_table = early
     early = jnp.sum(in_plane(early), 0)
     grad_query_b = (
         inv_query * query_scaled
@@ -837,21 +843,21 @@
         times_t(block_of(grad_qkv, place - back, cols_total), wqkv) for back in range(cols_total)
     ]
     da_total = da_parts[1].astype(jnp.bfloat16)
+    wqkv_local = first_t(seq_rows, after(grad_qkv, da_total)).astype(jnp.bfloat16)
+    moe = shift(after(moe, sums), "col")
     for back in range(2, cols_total):
         da_came = shift(da_total, "col")
+        if back == 2:
+            da_came = after(da_came, wqkv_local, early_table, moe)
         da_total = (da_came.astype(jnp.float32) + da_parts[back]).astype(jnp.bfloat16)
-        if back == 2:
-            da_second = da_total
         if back == last:
             da_total = after(da_total, early)
-    moe = after(moe, da_came)
+    grad_normal_a = shift(da_total, "col").astype(jnp.float32) + da_parts[0]
     for back in order[2:]:
-        moe = shift(moe, "col").astype(jnp.float32) + out_shares[back]
+        moe = moe.astype(jnp.float32) + out_shares[back]
         if back:
-            moe = moe.astype(jnp.bfloat16)
+            moe = shift(moe.astype(jnp.bfloat16), "col")
     output = (residual + moe).astype(jnp.bfloat16)
-    grad_normal_a = shift(da_total, "col").astype(jnp.float32) + da_parts[0]
-    wqkv_local = first_t(seq_rows, after(grad_qkv, da_second, homes[-1])).astype(jnp.bfloat16)
     attn_gain_local = (
         jnp.sum(wqkv.astype(jnp.float32) * wqkv_local.astype(jnp.float32), -1) / attn_gain
     )

time: 1000 us -> 1010 us (1.010)
    dot_general x6 -> x9, matrix products: 27.3 us -> 33.8 us  [times_t(): lax.dot_general(left, right, (((1,), (1,)), ((), ())), preferred_element_...]
  transfers between devices with their start and end apart: 61 -> 61, of which waited for: 32 -> 33; matrix products, arithmetic and copies ran while one was open for 19% -> 20% of each run, Pallas kernels for 25% -> 25%
where the time goes in v3:
time: 1010 us; the launch traced here: 1000 us
  waiting for transfers between devices  390 us (39%)
  Pallas kernels  252 us (25%)
  matrix products  127 us (13%)
  starting transfers between devices  111 us (11%)
  local copies, waits for them, and re-layouts  58.2 us (6%)
  other arithmetic  49.3 us (5%)
  between operations  16.3 us (2%)
    ppermute x39, waiting for transfers between devices, shift(): lax.ppermute(value, axis, [(i, (i + step) % count) for i in range(count)])  293 us
    all_to_all x17, waiting for transfers between devices, in_plane(): lax.all_to_all(table, 'row', split_axis=0, concat_axis=0, tiled=True)  97.1 us
    pallas_call x4, Pallas kernels, expert_core(): pl.pallas_call(expert_kernel, grid=(owned, tiles), in_specs=[packed_spec,...  83.8 us
    all_to_all x17, starting transfers between devices, in_plane(): lax.all_to_all(table, 'row', split_axis=0, concat_axis=0, tiled=True)  75.9 us
    dot_general x11, matrix products, first_t(): lax.dot_general(left, right, (((0,), (0,)), ((), ())), preferred_element_...  47.8 us
    pallas_call x2, Pallas kernels, in_grads(): pl.pallas_call(functools.partial(in_grads_kernel, count), grid=(owned, wi...  46.5 us
    pallas_call x4, Pallas kernels, down_t(): pl.pallas_call(down_t_kernel, grid=(owned, tiles), in_specs=[pl.BlockSpec...  35.1 us
    dot_general x9, matrix products, times_t(): lax.dot_general(left, right, (((1,), (1,)), ((), ())), preferred_element_...  33.8 us
  transfers between devices with their start and end apart: 61, of which 33 were waited for; matrix products, arithmetic and copies ran while one was open for 20% of the time, Pallas kernels for 25%

profile of v3, /device:TPU:0, one launch (start us, length us, event | category | flops | bytes accessed | tf_op | source)
XLA Modules:
  0.0 1004.3 jit_solution(15994233051140374311)
XLA Ops:
  31.4 15.8 %collective-permute-done = bf16[256,2048]{1,0:T(8,128)(2,1)} collective-permute-done((bf16[256,2048]{1,0:T(8,128)(2,1)}, bf16[256,2048]{1,0:T(8,128)(2,1)}, u32[]{:S(2)}, u32[]{:S(2)}) %collective-permute-start) | collective-permute-done | bytes 1048608 | tf_op jit(solution)/shard_map/ppermute | solution.py:53
  47.2 25.2 %collective-permute-done.1 = bf16[256,2048]{1,0:T(8,128)(2,1)} collective-permute-done((bf16[256,2048]{1,0:T(8,128)(2,1)}, bf16[256,2048]{1,0:T(8,128)(2,1)}, u32[]{:S(2)}, u32[]{:S(2)}) %collective-permute-start.1) | collective-permute-done | bytes 1048608 | tf_op jit(solution)/shard_map/ppermute | solution.py:53
  80.1 16.6 %collective-permute-done.2 = bf16[256,2048]{1,0:T(8,128)(2,1)} collective-permute-done((bf16[256,2048]{1,0:T(8,128)(2,1)}, bf16[256,2048]{1,0:T(8,128)(2,1)}, u32[]{:S(2)}, u32[]{:S(2)}) %collective-permute-start.2) | collective-permute-done | bytes 1048608 | tf_op jit(solution)/shard_map/ppermute | solution.py:53
  145.7 26.9 %collective-permute-done.7 = bf16[256,2048]{1,0:T(8,128)(2,1)} collective-permute-done((bf16[256,2048]{1,0:T(8,128)(2,1)}, bf16[256,2048]{1,0:T(8,128)(2,1)}, u32[]{:S(2)}, u32[]{:S(2)}) %collective-permute-start.7) | collective-permute-done | bytes 1048608 | tf_op jit(solution)/shard_map/ppermute | solution.py:53
  214.3 16.0 %collective-permute-done.9 = bf16[256,2048]{1,0:T(8,128)(2,1)S(1)} collective-permute-done((bf16[256,2048]{1,0:T(8,128)(2,1)S(1)}, bf16[256,2048]{1,0:T(8,128)(2,1)S(1)}, u32[]{:S(2)}, u32[]{:S(2)}) %collective-permute-start.9) | collective-permute-done | bytes 1048608 | tf_op jit(solution)/shard_map/ppermute | solution.py:53
  234.1 22.7 %collective-permute-done.11 = bf16[256,2048]{1,0:T(8,128)(2,1)} collective-permute-done((bf16[256,2048]{1,0:T(8,128)(2,1)}, bf16[256,2048]{1,0:T(8,128)(2,1)}, u32[]{:S(2)}, u32[]{:S(2)}) %collective-permute-start.11) | collective-permute-done | bytes 1048608 | tf_op jit(solution)/shard_map/ppermute | solution.py:53
  278.4 19.8 %collective-permute-done.13 = bf16[256,2176]{1,0:T(8,128)(2,1)S(1)} collective-permute-done((bf16[256,2176]{1,0:T(8,128)(2,1)S(1)}, bf16[256,2176]{1,0:T(8,128)(2,1)S(1)}, u32[]{:S(2)}, u32[]{:S(2)}) %collective-permute-start.13) | collective-permute-done | bytes 1114144 | tf_op jit(solution)/shard_map/ppermute | solution.py:53
  314.3 21.0 %expert_core.5 = (bf16[8,2,48,2176]{3,2,1,0:T(8,128)(2,1)}, bf16[2,384,1024]{2,1,0:T(8,128)(2,1)S(1)}, bf16[2,384,1024]{2,1,0:T(8,128)(2,1)}, bf16[2,384,1024]{2,1,0:T(8,128)(2,1)}) custom-call(bf16[8,2,48,2176]{3,2,1,0:T(8,128)(2,1)} %all-to-all-done.3.rows_ref.refs_0_, bf16[2048,2048]{1,0:T(8,128)(2,1)} %gate_ref.7, bf16[2048,2048]{1,0:T(8,128)(2,1)} %up_ref.7, ...), custom_call_target="tpu_custom_call" | custom-call | flops 12884901888 | bytes 39845888 | tf_op jit(solution)/shard_map/expert_core/pallas_call | solution.py:218
  358.7 20.9 %expert_core.4 = (bf16[8,2,48,2176]{3,2,1,0:T(8,128)(2,1)}, bf16[2,384,1024]{2,1,0:T(8,128)(2,1)S(1)}, bf16[2,384,1024]{2,1,0:T(8,128)(2,1)}, bf16[2,384,1024]{2,1,0:T(8,128)(2,1)}) custom-call(bf16[8,2,48,2176]{3,2,1,0:T(8,128)(2,1)} %all-to-all-done.4.rows_ref.refs_1_, bf16[2048,2048]{1,0:T(8,128)(2,1)} %gate_ref.7, bf16[2048,2048]{1,0:T(8,128)(2,1)} %up_ref.7, ...), custom_call_target="tpu_custom_call" | custom-call | flops 12884901888 | bytes 39845888 | tf_op jit(solution)/shard_map/expert_core/pallas_call | solution.py:218
  403.0 20.9 %expert_core.6 = (bf16[8,2,48,2176]{3,2,1,0:T(8,128)(2,1)}, bf16[2,384,1024]{2,1,0:T(8,128)(2,1)S(1)}, bf16[2,384,1024]{2,1,0:T(8,128)(2,1)}, bf16[2,384,1024]{2,1,0:T(8,128)(2,1)}) custom-call(bf16[8,2,48,2176]{3,2,1,0:T(8,128)(2,1)} %all-to-all-done.5.rows_ref.refs_2_, bf16[2048,2048]{1,0:T(8,128)(2,1)} %gate_ref.7, bf16[2048,2048]{1,0:T(8,128)(2,1)} %up_ref.7, ...), custom_call_target="tpu_custom_call" | custom-call | flops 12884901888 | bytes 39845888 | tf_op jit(solution)/shard_map/expert_core/pallas_call | solution.py:218
  454.0 31.3 %all-to-all-done.7.rows_ref.refs_3_ = bf16[8,2,48,2176]{3,2,1,0:T(8,128)(2,1)} async-done(((bf16[8,2,48,2176]{3,2,1,0:T(8,128)(2,1)}), bf16[8,2,48,2176]{3,2,1,0:T(8,128)(2,1)}, u32[]{:S(2)}, u32[]{:S(2)}) %all-to-all-start.7) | async-done | bytes 3342368 | tf_op jit(solution)/shard_map/all_to_all | solution.py:632
  490.0 20.9 %expert_core.7 = (bf16[8,2,48,2176]{3,2,1,0:T(8,128)(2,1)}, bf16[2,384,1024]{2,1,0:T(8,128)(2,1)S(1)}, bf16[2,384,1024]{2,1,0:T(8,128)(2,1)}, bf16[2,384,1024]{2,1,0:T(8,128)(2,1)}) custom-call(bf16[8,2,48,2176]{3,2,1,0:T(8,128)(2,1)} %all-to-all-done.7.rows_ref.refs_3_, bf16[2048,2048]{1,0:T(8,128)(2,1)} %gate_ref.7, bf16[2048,2048]{1,0:T(8,128)(2,1)} %up_ref.7, ...), custom_call_target="tpu_custom_call" | custom-call | flops 12884901888 | bytes 39845888 | tf_op jit(solution)/shard_map/expert_core/pallas_call | solution.py:218
  510.9 19.1 %all-to-all-done.8 = bf16[8,2,48,2176]{3,2,1,0:T(8,128)(2,1)} async-done(((bf16[8,2,48,2176]{3,2,1,0:T(8,128)(2,1)}), bf16[8,2,48,2176]{3,2,1,0:T(8,128)(2,1)}, u32[]{:S(2)}, u32[]{:S(2)}) %all-to-all-start.8) | async-done | bytes 3342368 | tf_op jit(solution)/shard_map/all_to_all | solution.py:632
  538.9 23.3 %in_grads.2 = f32[2048,2048]{1,0:T(8,128)} custom-call(bf16[8,2,48,2176]{3,2,1,0:T(8,128)(2,1)} %all-to-all-done.3.rows_ref.refs_0_, bf16[8,2,48,2176]{3,2,1,0:T(8,128)(2,1)} %all-to-all-done.4.rows_ref.refs_1_, bf16[8,2,48,2176]{3,2,1,0:T(8,128)(2,1)} %all-to-all-done.5.rows_ref.refs_2_, bf16[8,2,48,2176]{3,2,1,0:T(8,128)(2,1)} %all-to-all-done.7.rows_ref.refs_3_, ...), custom_call_target="tpu_custom_call" | custom-call | flops 12884901888 | bytes 16777216 | tf_op jit(solution)/shard_map/in_grads/pallas_call | solution.py:296
  562.2 15.0 %expert_out.3 = bf16[8,4,48,2048]{3,2,1,0:T(8,128)(2,1)} custom-call(bf16[2,384,1024]{2,1,0:T(8,128)(2,1)S(1)} %copy-done.13, bf16[2,384,1024]{2,1,0:T(8,128)(2,1)} %copy-done.14, bf16[2048,2048]{1,0:T(8,128)(2,1)} %refs_1_.3), custom_call_target="tpu_custom_call" | custom-call | flops 6442450944 | bytes 23068672 | tf_op jit(solution)/shard_map/expert_out/pallas_call | solution.py:264
  586.5 23.2 %in_grads.3 = f32[2048,2048]{1,0:T(8,128)} custom-call(bf16[8,2,48,2176]{3,2,1,0:T(8,128)(2,1)} %all-to-all-done.3.rows_ref.refs_0_, bf16[8,2,48,2176]{3,2,1,0:T(8,128)(2,1)} %all-to-all-done.4.rows_ref.refs_1_, bf16[8,2,48,2176]{3,2,1,0:T(8,128)(2,1)} %all-to-all-done.5.rows_ref.refs_2_, bf16[8,2,48,2176]{3,2,1,0:T(8,128)(2,1)} %all-to-all-done.7.rows_ref.refs_3_, ...), custom_call_target="tpu_custom_call" | custom-call | flops 12884901888 | bytes 16777216 | tf_op jit(solution)/shard_map/in_grads/pallas_call | solution.py:296
  632.3 26.0 %down_grads.1 = f32[2048,2048]{1,0:T(8,128)} custom-call(bf16[2,384,1024]{2,1,0:T(8,128)(2,1)S(1)} %get-tuple-element.138.refs_0_, bf16[2,384,1024]{2,1,0:T(8,128)(2,1)} %copy-done.12, bf16[2,384,1024]{2,1,0:T(8,128)(2,1)} %copy-done.14, bf16[2,384,1024]{2,1,0:T(8,128)(2,1)} %copy-done.1, bf16[8,2,48,2048]{3,2,1,0:T(8,128)(2,1)} %all-to-all-done.grad_ref.refs_4_, ...), custom_call_target="tpu_custom_call" | custom-call | flops 12884901888 | bytes 16777216 | tf_op jit(solution)/shard_map/down_grads/pallas_call | solution.py:328
  691.9 23.1 %collective-permute-done.21 = bf16[256,2048]{1,0:T(8,128)(2,1)S(1)} collective-permute-done((bf16[256,2048]{1,0:T(8,128)(2,1)S(1)}, bf16[256,2048]{1,0:T(8,128)(2,1)S(1)}, u32[]{:S(2)}, u32[]{:S(2)}) %collective-permute-start.21) | collective-permute-done | bytes 1048608 | tf_op jit(solution)/shard_map/ppermute | solution.py:53
  725.2 16.6 %collective-permute-done.22 = bf16[256,2048]{1,0:T(8,128)(2,1)} collective-permute-done((bf16[256,2048]{1,0:T(8,128)(2,1)S(1)}, bf16[256,2048]{1,0:T(8,128)(2,1)}, u32[]{:S(2)}, u32[]{:S(2)}) %collective-permute-start.22) | collective-permute-done | bytes 1048608 | tf_op jit(solution)/shard_map/ppermute | solution.py:53
  749.4 18.4 %collective-permute-done.23 = bf16[256,2048]{1,0:T(8,128)(2,1)S(1)} collective-permute-done((bf16[256,2048]{1,0:T(8,128)(2,1)}, bf16[256,2048]{1,0:T(8,128)(2,1)S(1)}, u32[]{:S(2)}, u32[]{:S(2)}) %collective-permute-start.23) | collective-permute-done | bytes 1048608 | tf_op jit(solution)/shard_map/ppermute | solution.py:53
  782.5 17.1 %attend_back.1 = (f32[1024,512]{1,0:T(8,128)}, f32[1024,512]{1,0:T(8,128)}, bf16[1024,512]{1,0:T(8,128)(2,1)}, f32[1024,1]{1,0:T(8,128)S(1)}, f32[1024,1]{1,0:T(...) custom-call(bf16[1024,512]{1,0:T(8,128)(2,1)} %get-tuple-element.141.query_ref, ...), custom_call_target="tpu_custom_call" | custom-call | flops 21474836480 | bytes 20971520 | tf_op jit(solution)/shard_map/attend_back/pallas_call | solution.py:498
  864.3 18.0 %collective-permute-done.28 = bf16[256,2048]{1,0:T(8,128)(2,1)} collective-permute-done((bf16[256,2048]{1,0:T(8,128)(2,1)}, bf16[256,2048]{1,0:T(8,128)(2,1)}, u32[]{:S(2)}, u32[]{:S(2)}) %collective-permute-start.28) | collective-permute-done | bytes 1048608 | tf_op jit(solution)/shard_map/ppermute | solution.py:53
  886.6 18.2 %collective-permute-done.33 = bf16[256,2048]{1,0:T(8,128)(2,1)} collective-permute-done((bf16[256,2048]{1,0:T(8,128)(2,1)}, bf16[256,2048]{1,0:T(8,128)(2,1)}, u32[]{:S(2)}, u32[]{:S(2)}) %collective-permute-start.33) | collective-permute-done | bytes 1048608 | tf_op jit(solution)/shard_map/ppermute | solution.py:53
  966.8 14.7 %collective-permute-done.36 = f32[2048]{0:T(1024)S(1)} collective-permute-done((f32[2048]{0:T(1024)S(1)}, f32[2048]{0:T(1024)S(1)}, u32[]{:S(2)}, u32[]{:S(2)}) %collective-permute-start.36) | collective-permute-done | bytes 8224 | tf_op jit(solution)/shard_map/ppermute | solution.py:53
  (483 shorter events, 497.1 us)
Async XLA Ops:
  7.2 91.9 %all-gather.3.cloned.1.call-start = ((), (), s32[]{:S(2)}) async-start(), calls=%async_computation.18 | async-start | bytes 7077888 | tf_op jit(solution)/shard_map/all_gather | solution.py:600
  26.8 72.2 %all-to-all-start = ((bf16[8,2,48,2048]{3,2,1,0:T(8,128)(2,1)}), bf16[8,2,48,2048]{3,2,1,0:T(8,128)(2,1)}, u32[]{:S(2)}, u32[]{:S(2)}) async-start(bf16[8,2,48,2048]{3,2,1,0:T(8,128)(2,1)} %bitcast.2), calls=%async_computation | async-start | bytes 6291456 | tf_op jit(solution)/shard_map/all_to_all | solution.py:632
  31.4 141.2 %all-gather.5.cloned.1.call-start = ((), (), s32[]{:S(2)}) async-start(), calls=%async_computation.19 | async-start | bytes 2359296 | tf_op jit(solution)/shard_map/all_gather | solution.py:603
  140.5 51.2 %all-to-all-start.1 = ((bf16[8,2,48,2048]{3,2,1,0:T(8,128)(2,1)}), bf16[8,2,48,2048]{3,2,1,0:T(8,128)(2,1)}, u32[]{:S(2)}, u32[]{:S(2)}) async-start(bf16[8,2,48,2048]{3,2,1,0:T(8,128)(2,1)} %bitcast.12), calls=%async_computation.1 | async-start | bytes 6291456 | tf_op jit(solution)/shard_map/all_to_all | solution.py:632
  191.7 42.3 %all-to-all-start.2 = ((bf16[8,2,48,2048]{3,2,1,0:T(8,128)(2,1)}), bf16[8,2,48,2048]{3,2,1,0:T(8,128)(2,1)}, u32[]{:S(2)}, u32[]{:S(2)}) async-start(bf16[8,2,48,2048]{3,2,1,0:T(8,128)(2,1)} %bitcast.165), calls=%async_computation.2 | async-start | bytes 6291456 | tf_op jit(solution)/shard_map/all_to_all | solution.py:632
  265.0 44.5 %all-to-all-start.3 = ((bf16[8,2,48,2176]{3,2,1,0:T(8,128)(2,1)}), bf16[8,2,48,2176]{3,2,1,0:T(8,128)(2,1)}, u32[]{:S(2)}, u32[]{:S(2)}) async-start(bf16[8,2,48,2176]{3,2,1,0:T(8,128)(2,1)} %bitcast.163), calls=%async_computation.3 | async-start | bytes 6684672 | tf_op jit(solution)/shard_map/all_to_all | solution.py:632
  309.5 44.5 %all-to-all-start.4 = ((bf16[8,2,48,2176]{3,2,1,0:T(8,128)(2,1)}), bf16[8,2,48,2176]{3,2,1,0:T(8,128)(2,1)}, u32[]{:S(2)}, u32[]{:S(2)}) async-start(bf16[8,2,48,2176]{3,2,1,0:T(8,128)(2,1)} %bitcast.161), calls=%async_computation.4 | async-start | bytes 6684672 | tf_op jit(solution)/shard_map/all_to_all | solution.py:632
  354.0 44.5 %all-to-all-start.5 = ((bf16[8,2,48,2176]{3,2,1,0:T(8,128)(2,1)}), bf16[8,2,48,2176]{3,2,1,0:T(8,128)(2,1)}, u32[]{:S(2)}, u32[]{:S(2)}) async-start(bf16[8,2,48,2176]{3,2,1,0:T(8,128)(2,1)} %bitcast.162), calls=%async_computation.5 | async-start | bytes 6684672 | tf_op jit(solution)/shard_map/all_to_all | solution.py:632
  398.4 42.4 %all-to-all-start.6 = ((bf16[8,2,48,2048]{3,2,1,0:T(8,128)(2,1)}), bf16[8,2,48,2048]{3,2,1,0:T(8,128)(2,1)}, u32[]{:S(2)}, u32[]{:S(2)}) async-start(bf16[8,2,48,2048]{3,2,1,0:T(8,128)(2,1)} %bitcast.166), calls=%async_computation.6 | async-start | bytes 6291456 | tf_op jit(solution)/shard_map/all_to_all | solution.py:632
  440.8 44.5 %all-to-all-start.7 = ((bf16[8,2,48,2176]{3,2,1,0:T(8,128)(2,1)}), bf16[8,2,48,2176]{3,2,1,0:T(8,128)(2,1)}, u32[]{:S(2)}, u32[]{:S(2)}) async-start(bf16[8,2,48,2176]{3,2,1,0:T(8,128)(2,1)} %bitcast.164), calls=%async_computation.7 | async-start | bytes 6684672 | tf_op jit(solution)/shard_map/all_to_all | solution.py:632
  485.3 44.7 %all-to-all-start.8 = ((bf16[8,2,48,2176]{3,2,1,0:T(8,128)(2,1)}), bf16[8,2,48,2176]{3,2,1,0:T(8,128)(2,1)}, u32[]{:S(2)}, u32[]{:S(2)}) async-start(bf16[8,2,48,2176]{3,2,1,0:T(8,128)(2,1)} %get-tuple-element.117), calls=%async_computation.8 | async-start | bytes 6684672 | tf_op jit(solution)/shard_map/all_to_all | solution.py:632
  530.0 47.2 %all-to-all-start.9 = ((bf16[8,2,48,2176]{3,2,1,0:T(8,128)(2,1)}), bf16[8,2,48,2176]{3,2,1,0:T(8,128)(2,1)}, u32[]{:S(2)}, u32[]{:S(2)}) async-start(bf16[8,2,48,2176]{3,2,1,0:T(8,128)(2,1)} %get-tuple-element.123), calls=%async_computation.9 | async-start | bytes 6684672 | tf_op jit(solution)/shard_map/all_to_all | solution.py:632
  538.8 43.1 %collective-permute-start.18 = (bf16[256,2176]{1,0:T(8,128)(2,1)}, bf16[256,2176]{1,0:T(8,128)(2,1)}, u32[]{:S(2)}, u32[]{:S(2)}) collective-permute-start(bf16[256,2176]{1,0:T(8,128)(2,1)} %convolution_convert_fusion.5), channel_id=1, source_target_pairs={{0,1},{1,2},{2,3},{3,0},{4,5},{5,6},{6,7},{7,4},{8,9},{9,10},{10,1... | collective-permute-start | bytes 3342344 | tf_op jit(solution)/shard_map/ppermute | solution.py:53
  577.2 44.6 %all-to-all-start.10 = ((bf16[8,2,48,2176]{3,2,1,0:T(8,128)(2,1)}), bf16[8,2,48,2176]{3,2,1,0:T(8,128)(2,1)}, u32[]{:S(2)}, u32[]{:S(2)}) async-start(bf16[8,2,48,2176]{3,2,1,0:T(8,128)(2,1)} %get-tuple-element.129), calls=%async_computation.10 | async-start | bytes 6684672 | tf_op jit(solution)/shard_map/all_to_all | solution.py:632
  586.5 41.3 %collective-permute-start.19 = (bf16[256,2176]{1,0:T(8,128)(2,1)}, bf16[256,2176]{1,0:T(8,128)(2,1)}, u32[]{:S(2)}, u32[]{:S(2)}) collective-permute-start(bf16[256,2176]{1,0:T(8,128)(2,1)} %add_convert_fusion.1), channel_id=1, source_target_pairs={{0,1},{1,2},{2,3},{3,0},{4,5},{5,6},{6,7},{7,4},{8,9},{9,10},{10,1... | collective-permute-start | bytes 3342344 | tf_op jit(solution)/shard_map/ppermute | solution.py:53
  621.8 45.0 %all-to-all-start.11 = ((bf16[8,2,48,2176]{3,2,1,0:T(8,128)(2,1)}), bf16[8,2,48,2176]{3,2,1,0:T(8,128)(2,1)}, u32[]{:S(2)}, u32[]{:S(2)}) async-start(bf16[8,2,48,2176]{3,2,1,0:T(8,128)(2,1)} %get-tuple-element.136), calls=%async_computation.11 | async-start | bytes 6684672 | tf_op jit(solution)/shard_map/all_to_all | solution.py:632
  632.3 37.7 %collective-permute-start.20 = (bf16[256,2176]{1,0:T(8,128)(2,1)}, bf16[256,2176]{1,0:T(8,128)(2,1)}, u32[]{:S(2)}, u32[]{:S(2)}) collective-permute-start(bf16[256,2176]{1,0:T(8,128)(2,1)} %add_convert_fusion), channel_id=1, source_target_pairs={{0,1},{1,2},{2,3},{3,0},{4,5},{5,6},{6,7},{7,4},{8,9},{9,10},{10,1... | collective-permute-start | bytes 3342344 | tf_op jit(solution)/shard_map/ppermute | solution.py:53
  673.3 97.1 %all-to-all-start.12 = ((bf16[8,4,48,2048]{3,2,1,0:T(8,128)(2,1)}), bf16[8,4,48,2048]{3,2,1,0:T(8,128)(2,1)}, u32[]{:S(2)}, u32[]{:S(2)}) async-start(bf16[8,4,48,2048]{3,2,1,0:T(8,128)(2,1)} %expert_out.3), calls=%async_computation.12 | async-start | bytes 12582912 | tf_op jit(solution)/shard_map/all_to_all | solution.py:632
  777.8 45.0 %all-to-all-start.13 = ((bf16[8,2,48,2048]{3,2,1,0:T(8,128)(2,1)}), bf16[8,2,48,2048]{3,2,1,0:T(8,128)(2,1)}, u32[]{:S(2)}, u32[]{:S(2)}) async-start(bf16[8,2,48,2048]{3,2,1,0:T(8,128)(2,1)} %expert_out.4), calls=%async_computation.13 | async-start | bytes 6291456 | tf_op jit(solution)/shard_map/all_to_all | solution.py:632
  828.4 76.4 %all-to-all-start.14 = ((bf16[8,2,48,2048]{3,2,1,0:T(8,128)(2,1)}), bf16[8,2,48,2048]{3,2,1,0:T(8,128)(2,1)S(1)}, u32[]{:S(2)}, u32[]{:S(2)}) async-start(bf16[8,2,48,2048]{3,2,1,0:T(8,128)(2,1)} %expert_out.5), calls=%async_computation.14 | async-start | bytes 6291456 | tf_op jit(solution)/shard_map/all_to_all | solution.py:632
  847.5 80.0 %collective-permute-start.39 = (bf16[4,256,1536]{2,1,0:T(8,128)(2,1)}, bf16[4,256,1536]{2,1,0:T(8,128)(2,1)}, u32[]{:S(2)}, u32[]{:S(2)}) collective-permute-start(bf16[4,256,1536]{2,1,0:T(8,128)(2,1)} %dynamic-slice_bitcast_fusion), channel_id=1, source_target_pairs={{0,4},{4,0},{8,12},{12,8},{16,20},{20,16},{24,28},{28,24},{1,5},{5... | collective-permute-start | bytes 9437192 | tf_op jit(solution)/shard_map/ppermute | solution.py:876
  856.0 48.8 %collective-permute-start.33 = (bf16[256,2048]{1,0:T(8,128)(2,1)}, bf16[256,2048]{1,0:T(8,128)(2,1)}, u32[]{:S(2)}, u32[]{:S(2)}) collective-permute-start(bf16[256,2048]{1,0:T(8,128)(2,1)} %convolution_convert_fusion.12), channel_id=1, source_target_pairs={{0,1},{1,2},{2,3},{3,0},{4,5},{5,6},{6,7},{7,4},{8,9},{9,10},{10,1... | collective-permute-start | bytes 3145736 | tf_op jit(solution)/shard_map/ppermute | solution.py:53
  886.6 68.2 %collective-permute-start.29 = (bf16[256,2048]{1,0:T(8,128)(2,1)}, bf16[256,2048]{1,0:T(8,128)(2,1)}, u32[]{:S(2)}, u32[]{:S(2)}) collective-permute-start(bf16[256,2048]{1,0:T(8,128)(2,1)} %add_convert_fusion.5), channel_id=1, source_target_pairs={{0,1},{1,2},{2,3},{3,0},{4,5},{5,6},{6,7},{7,4},{8,9},{9,10},{10,1... | collective-permute-start | bytes 3145736 | tf_op jit(solution)/shard_map/ppermute | solution.py:53
  938.6 53.0 %all-to-all-start.17 = ((bf16[4,256,2048]{2,1,0:T(8,128)(2,1)}), bf16[4,256,2048]{2,1,0:T(8,128)(2,1)}, u32[]{:S(2)}, u32[]{:S(2)}) async-start(bf16[4,256,2048]{2,1,0:T(8,128)(2,1)} %pad_maximum_fusion), calls=%async_computation.17 | async-start | bytes 8388608 | tf_op jit(solution)/shard_map/all_to_all | solution.py:886
  (140 other events, 2042.8 us)
Sparse Core Ops, SparseCore 0:
  10.5 72.6 all-gather.2
  85.1 31.7 all-gather.4

commit v4 on v2

--- a/solution.py
+++ b/solution.py
@@ -651,8 +651,8 @@
     squares = exchange_sum(
         jnp.stack([jnp.sum(query_raw * query_raw, -1), jnp.sum(key_raw * key_raw, -1)]), "col"
     )
-    squares = after(squares, g_blocks[1])
     g_blocks.append(shift(after(g_blocks[1], squares), "col"))
+    g_rows.append(to_experts(after(g_blocks[1], qkv), 1))
     inv_query = lax.rsqrt(squares[0] / width + EPSILON)[:, None]
     inv_key = lax.rsqrt(squares[1] / width + EPSILON)[:, None]
     cosines, sine_table = rope_tables(length, HEAD_DIM)
@@ -663,7 +663,7 @@
     *heads_out, attended, logs = attend(
         qkv, inv_query, inv_key, query_gain, key_gain, tables, doc_ids, block, factor
     )
-    g_rows.append(to_experts(after(g_blocks[1], attended), 1))
+    attended = after(attended, g_blocks[2])
     raw_grads = [down_t(rows, w_down, units) for rows in g_rows]
     g_rows.append(to_experts(g_blocks[2], 2))
     parts = [
@@ -674,7 +674,7 @@
         )
         for back in range(cols_total)
     ]
-    parts[2] = after(parts[2], raw_grads[0], g_blocks[2])
+    parts[2] = after(parts[2], raw_grads[0])
     parts[3] = after(parts[3], raw_grads[1])
     parts[0] = after(parts[0], g_rows[2])
     attn = ring_sum(parts, "col")
@@ -778,12 +778,13 @@
     )
 
     grad_blocks = ring_blocks(grad_attn, "col")
-    incoming = after(natural(grad_blocks, place), out_shares[1])
+    grad_out_heads = natural(
+        [times_t(block_grad, wo_full).astype(jnp.bfloat16) for block_grad in grad_blocks], place
+    )
+    grad_out_heads = after(grad_out_heads, out_shares[1])
     for number in range(1, len(outs)):
         outs_home(number)
     moe = shift(after(out_shares[1].astype(jnp.bfloat16), grad_blocks[-1]), "col")
-    wout_local = first_t(incoming, attended).astype(jnp.bfloat16)
-    grad_out_heads = times_t(incoming, wo_full).astype(jnp.bfloat16)
     (
         query_scaled,
         key_scaled,
@@ -823,6 +824,7 @@
         ],
         1,
     )
+    early_table = early
     early = jnp.sum(in_plane(early), 0)
     grad_query_b = (
         inv_query * query_scaled
@@ -837,13 +839,15 @@
         times_t(block_of(grad_qkv, place - back, cols_total), wqkv) for back in range(cols_total)
     ]
     da_total = da_parts[1].astype(jnp.bfloat16)
+    incoming = natural([after(grad_blocks[0], da_total)] + grad_blocks[1:], place)
+    wout_local = first_t(incoming, attended).astype(jnp.bfloat16)
     for back in range(2, cols_total):
         da_came = shift(da_total, "col")
+        if back == 2:
+            da_came = after(da_came, early_table, wout_local)
         da_total = (da_came.astype(jnp.float32) + da_parts[back]).astype(jnp.bfloat16)
         if back == 2:
             da_second = da_total
-        if back == last:
-            da_total = after(da_total, early)
     moe = after(moe, da_came)
     for back in order[2:]:
         moe = shift(moe, "col").astype(jnp.float32) + out_shares[back]
@@ -851,7 +855,7 @@
             moe = moe.astype(jnp.bfloat16)
     output = (residual + moe).astype(jnp.bfloat16)
     grad_normal_a = shift(da_total, "col").astype(jnp.float32) + da_parts[0]
-    wqkv_local = first_t(seq_rows, after(grad_qkv, da_second, homes[-1])).astype(jnp.bfloat16)
+    wqkv_local = first_t(seq_rows, after(grad_qkv, da_second, early)).astype(jnp.bfloat16)
     attn_gain_local = (
         jnp.sum(wqkv.astype(jnp.float32) * wqkv_local.astype(jnp.float32), -1) / attn_gain
     )

time: 1000 us -> 1010 us (1.010)
    dot_general x6 -> x9, matrix products: 27.3 us -> 31.1 us  [times_t(): lax.dot_general(left, right, (((1,), (1,)), ((), ())), preferred_element_...]
  transfers between devices with their start and end apart: 61 -> 61, of which waited for: 32 -> 35; matrix products, arithmetic and copies ran while one was open for 19% -> 18% of each run, Pallas kernels for 25% -> 25%
where the time goes in v4:
time: 1010 us; the launch traced here: 996 us
  waiting for transfers between devices  393 us (39%)
  Pallas kernels  252 us (25%)
  matrix products  125 us (12%)
  starting transfers between devices  110 us (11%)
  local copies, waits for them, and re-layouts  54.3 us (5%)
  other arithmetic  46.2 us (5%)
  between operations  16.3 us (2%)
    ppermute x39, waiting for transfers between devices, shift(): lax.ppermute(value, axis, [(i, (i + step) % count) for i in range(count)])  291 us
    all_to_all x17, waiting for transfers between devices, in_plane(): lax.all_to_all(table, 'row', split_axis=0, concat_axis=0, tiled=True)  99.5 us
    pallas_call x4, Pallas kernels, expert_core(): pl.pallas_call(expert_kernel, grid=(owned, tiles), in_specs=[packed_spec,...  83.8 us
    all_to_all x17, starting transfers between devices, in_plane(): lax.all_to_all(table, 'row', split_axis=0, concat_axis=0, tiled=True)  75.6 us
    dot_general x11, matrix products, first_t(): lax.dot_general(left, right, (((0,), (0,)), ((), ())), preferred_element_...  48.2 us
    pallas_call x2, Pallas kernels, in_grads(): pl.pallas_call(functools.partial(in_grads_kernel, count), grid=(owned, wi...  46.5 us
    pallas_call x4, Pallas kernels, down_t(): pl.pallas_call(down_t_kernel, grid=(owned, tiles), in_specs=[pl.BlockSpec...  35.1 us
    dot_general x9, matrix products, times_t(): lax.dot_general(left, right, (((1,), (1,)), ((), ())), preferred_element_...  31.1 us
  transfers between devices with their start and end apart: 61, of which 35 were waited for; matrix products, arithmetic and copies ran while one was open for 18% of the time, Pallas kernels for 25%

profile of v4, /device:TPU:0, one launch (start us, length us, event | category | flops | bytes accessed | tf_op | source)
XLA Modules:
  0.0 996.2 jit_solution(12825443327652632574)
XLA Ops:
  47.7 23.8 %collective-permute-done.1 = bf16[256,2048]{1,0:T(8,128)(2,1)} collective-permute-done((bf16[256,2048]{1,0:T(8,128)(2,1)}, bf16[256,2048]{1,0:T(8,128)(2,1)}, u32[]{:S(2)}, u32[]{:S(2)}) %collective-permute-start.1) | collective-permute-done | bytes 1048608 | tf_op jit(solution)/shard_map/ppermute | solution.py:53
  80.6 15.2 %collective-permute-done.2 = bf16[256,2048]{1,0:T(8,128)(2,1)} collective-permute-done((bf16[256,2048]{1,0:T(8,128)(2,1)}, bf16[256,2048]{1,0:T(8,128)(2,1)}, u32[]{:S(2)}, u32[]{:S(2)}) %collective-permute-start.2) | collective-permute-done | bytes 1048608 | tf_op jit(solution)/shard_map/ppermute | solution.py:53
  131.1 13.1 %attend.1 = (bf16[1024,512]{1,0:T(8,128)(2,1)}, bf16[1024,512]{1,0:T(8,128)(2,1)}, bf16[1024,512]{1,0:T(8,128)(2,1)}, bf16[1024,512]{1,0:T(8,128)(2,1)}, f32[4,1,1024]{2,1,0:T(1,128)S(1)}) custom-call(f32[1024,1536]{1,0:T(8,128)} %copy-done.25, f32[1024,1536]{1,0:T(8,128)} %copy-done.25, f32[1024,1536]{1,0:T(8,128)} %copy-done.25, ...), custom_call_target="tpu_custom_call" | custom-call | flops 12884901888 | bytes 10485760 | tf_op jit(solution)/shard_map/attend/pallas_call | solution.py:394
  144.2 14.3 %collective-permute-done.7 = bf16[256,2048]{1,0:T(8,128)(2,1)} collective-permute-done((bf16[256,2048]{1,0:T(8,128)(2,1)}, bf16[256,2048]{1,0:T(8,128)(2,1)}, u32[]{:S(2)}, u32[]{:S(2)}) %collective-permute-start.7) | collective-permute-done | bytes 1048608 | tf_op jit(solution)/shard_map/ppermute | solution.py:53
  200.3 16.1 %collective-permute-done.9 = bf16[256,2048]{1,0:T(8,128)(2,1)S(1)} collective-permute-done((bf16[256,2048]{1,0:T(8,128)(2,1)S(1)}, bf16[256,2048]{1,0:T(8,128)(2,1)S(1)}, u32[]{:S(2)}, u32[]{:S(2)}) %collective-permute-start.9) | collective-permute-done | bytes 1048608 | tf_op jit(solution)/shard_map/ppermute | solution.py:53
  220.1 22.5 %collective-permute-done.11 = bf16[256,2048]{1,0:T(8,128)(2,1)} collective-permute-done((bf16[256,2048]{1,0:T(8,128)(2,1)}, bf16[256,2048]{1,0:T(8,128)(2,1)}, u32[]{:S(2)}, u32[]{:S(2)}) %collective-permute-start.11) | collective-permute-done | bytes 1048608 | tf_op jit(solution)/shard_map/ppermute | solution.py:53
  264.5 19.8 %collective-permute-done.13 = bf16[256,2176]{1,0:T(8,128)(2,1)S(1)} collective-permute-done((bf16[256,2176]{1,0:T(8,128)(2,1)S(1)}, bf16[256,2176]{1,0:T(8,128)(2,1)S(1)}, u32[]{:S(2)}, u32[]{:S(2)}) %collective-permute-start.13) | collective-permute-done | bytes 1114144 | tf_op jit(solution)/shard_map/ppermute | solution.py:53
  300.1 21.0 %expert_core.5 = (bf16[8,2,48,2176]{3,2,1,0:T(8,128)(2,1)}, bf16[2,384,1024]{2,1,0:T(8,128)(2,1)S(1)}, bf16[2,384,1024]{2,1,0:T(8,128)(2,1)}, bf16[2,384,1024]{2,1,0:T(8,128)(2,1)}) custom-call(bf16[8,2,48,2176]{3,2,1,0:T(8,128)(2,1)} %all-to-all-done.3.rows_ref.refs_0_, bf16[2048,2048]{1,0:T(8,128)(2,1)} %gate_ref.7, bf16[2048,2048]{1,0:T(8,128)(2,1)} %up_ref.7, ...), custom_call_target="tpu_custom_call" | custom-call | flops 12884901888 | bytes 39845888 | tf_op jit(solution)/shard_map/expert_core/pallas_call | solution.py:218
  344.3 21.0 %expert_core.4 = (bf16[8,2,48,2176]{3,2,1,0:T(8,128)(2,1)}, bf16[2,384,1024]{2,1,0:T(8,128)(2,1)S(1)}, bf16[2,384,1024]{2,1,0:T(8,128)(2,1)}, bf16[2,384,1024]{2,1,0:T(8,128)(2,1)}) custom-call(bf16[8,2,48,2176]{3,2,1,0:T(8,128)(2,1)} %all-to-all-done.4.rows_ref.refs_1_, bf16[2048,2048]{1,0:T(8,128)(2,1)} %gate_ref.7, bf16[2048,2048]{1,0:T(8,128)(2,1)} %up_ref.7, ...), custom_call_target="tpu_custom_call" | custom-call | flops 12884901888 | bytes 39845888 | tf_op jit(solution)/shard_map/expert_core/pallas_call | solution.py:218
  388.9 21.0 %expert_core.6 = (bf16[8,2,48,2176]{3,2,1,0:T(8,128)(2,1)}, bf16[2,384,1024]{2,1,0:T(8,128)(2,1)S(1)}, bf16[2,384,1024]{2,1,0:T(8,128)(2,1)}, bf16[2,384,1024]{2,1,0:T(8,128)(2,1)}) custom-call(bf16[8,2,48,2176]{3,2,1,0:T(8,128)(2,1)} %all-to-all-done.5.rows_ref.refs_2_, bf16[2048,2048]{1,0:T(8,128)(2,1)} %gate_ref.7, bf16[2048,2048]{1,0:T(8,128)(2,1)} %up_ref.7, ...), custom_call_target="tpu_custom_call" | custom-call | flops 12884901888 | bytes 39845888 | tf_op jit(solution)/shard_map/expert_core/pallas_call | solution.py:218
  439.7 31.3 %all-to-all-done.7.rows_ref.refs_3_ = bf16[8,2,48,2176]{3,2,1,0:T(8,128)(2,1)} async-done(((bf16[8,2,48,2176]{3,2,1,0:T(8,128)(2,1)}), bf16[8,2,48,2176]{3,2,1,0:T(8,128)(2,1)}, u32[]{:S(2)}, u32[]{:S(2)}) %all-to-all-start.7) | async-done | bytes 3342368 | tf_op jit(solution)/shard_map/all_to_all | solution.py:632
  475.5 20.9 %expert_core.7 = (bf16[8,2,48,2176]{3,2,1,0:T(8,128)(2,1)}, bf16[2,384,1024]{2,1,0:T(8,128)(2,1)S(1)}, bf16[2,384,1024]{2,1,0:T(8,128)(2,1)}, bf16[2,384,1024]{2,1,0:T(8,128)(2,1)}) custom-call(bf16[8,2,48,2176]{3,2,1,0:T(8,128)(2,1)} %all-to-all-done.7.rows_ref.refs_3_, bf16[2048,2048]{1,0:T(8,128)(2,1)} %gate_ref.7, bf16[2048,2048]{1,0:T(8,128)(2,1)} %up_ref.7, ...), custom_call_target="tpu_custom_call" | custom-call | flops 12884901888 | bytes 39845888 | tf_op jit(solution)/shard_map/expert_core/pallas_call | solution.py:218
  496.5 19.0 %all-to-all-done.8 = bf16[8,2,48,2176]{3,2,1,0:T(8,128)(2,1)} async-done(((bf16[8,2,48,2176]{3,2,1,0:T(8,128)(2,1)}), bf16[8,2,48,2176]{3,2,1,0:T(8,128)(2,1)}, u32[]{:S(2)}, u32[]{:S(2)}) %all-to-all-start.8) | async-done | bytes 3342368 | tf_op jit(solution)/shard_map/all_to_all | solution.py:632
  524.6 23.3 %in_grads.2 = f32[2048,2048]{1,0:T(8,128)} custom-call(bf16[8,2,48,2176]{3,2,1,0:T(8,128)(2,1)} %all-to-all-done.3.rows_ref.refs_0_, bf16[8,2,48,2176]{3,2,1,0:T(8,128)(2,1)} %all-to-all-done.4.rows_ref.refs_1_, bf16[8,2,48,2176]{3,2,1,0:T(8,128)(2,1)} %all-to-all-done.5.rows_ref.refs_2_, bf16[8,2,48,2176]{3,2,1,0:T(8,128)(2,1)} %all-to-all-done.7.rows_ref.refs_3_, ...), custom_call_target="tpu_custom_call" | custom-call | flops 12884901888 | bytes 16777216 | tf_op jit(solution)/shard_map/in_grads/pallas_call | solution.py:296
  547.9 15.0 %expert_out.3 = bf16[8,4,48,2048]{3,2,1,0:T(8,128)(2,1)} custom-call(bf16[2,384,1024]{2,1,0:T(8,128)(2,1)S(1)} %copy-done.13, bf16[2,384,1024]{2,1,0:T(8,128)(2,1)} %copy-done.14, bf16[2048,2048]{1,0:T(8,128)(2,1)} %refs_1_.3), custom_call_target="tpu_custom_call" | custom-call | flops 6442450944 | bytes 23068672 | tf_op jit(solution)/shard_map/expert_out/pallas_call | solution.py:264
  572.2 23.2 %in_grads.3 = f32[2048,2048]{1,0:T(8,128)} custom-call(bf16[8,2,48,2176]{3,2,1,0:T(8,128)(2,1)} %all-to-all-done.3.rows_ref.refs_0_, bf16[8,2,48,2176]{3,2,1,0:T(8,128)(2,1)} %all-to-all-done.4.rows_ref.refs_1_, bf16[8,2,48,2176]{3,2,1,0:T(8,128)(2,1)} %all-to-all-done.5.rows_ref.refs_2_, bf16[8,2,48,2176]{3,2,1,0:T(8,128)(2,1)} %all-to-all-done.7.rows_ref.refs_3_, ...), custom_call_target="tpu_custom_call" | custom-call | flops 12884901888 | bytes 16777216 | tf_op jit(solution)/shard_map/in_grads/pallas_call | solution.py:296
  617.0 26.0 %down_grads.1 = f32[2048,2048]{1,0:T(8,128)} custom-call(bf16[2,384,1024]{2,1,0:T(8,128)(2,1)S(1)} %get-tuple-element.135.refs_0_, bf16[2,384,1024]{2,1,0:T(8,128)(2,1)} %copy-done.12, bf16[2,384,1024]{2,1,0:T(8,128)(2,1)} %copy-done.14, bf16[2,384,1024]{2,1,0:T(8,128)(2,1)} %copy-done.1, bf16[8,2,48,2048]{3,2,1,0:T(8,128)(2,1)} %all-to-all-done.grad_ref.refs_4_, ...), custom_call_target="tpu_custom_call" | custom-call | flops 12884901888 | bytes 16777216 | tf_op jit(solution)/shard_map/down_grads/pallas_call | solution.py:328
  667.7 25.6 %collective-permute-done.21 = bf16[256,2048]{1,0:T(8,128)(2,1)} collective-permute-done((bf16[256,2048]{1,0:T(8,128)(2,1)S(1)}, bf16[256,2048]{1,0:T(8,128)(2,1)}, u32[]{:S(2)}, u32[]{:S(2)}) %collective-permute-start.21) | collective-permute-done | bytes 1048608 | tf_op jit(solution)/shard_map/ppermute | solution.py:53
  700.3 20.0 %collective-permute-done.22 = bf16[256,2048]{1,0:T(8,128)(2,1)} collective-permute-done((bf16[256,2048]{1,0:T(8,128)(2,1)}, bf16[256,2048]{1,0:T(8,128)(2,1)}, u32[]{:S(2)}, u32[]{:S(2)}) %collective-permute-start.22) | collective-permute-done | bytes 1048608 | tf_op jit(solution)/shard_map/ppermute | solution.py:53
  729.1 17.2 %collective-permute-done.23 = bf16[256,2048]{1,0:T(8,128)(2,1)S(1)} collective-permute-done((bf16[256,2048]{1,0:T(8,128)(2,1)}, bf16[256,2048]{1,0:T(8,128)(2,1)S(1)}, u32[]{:S(2)}, u32[]{:S(2)}) %collective-permute-start.23) | collective-permute-done | bytes 1048608 | tf_op jit(solution)/shard_map/ppermute | solution.py:53
  761.1 17.1 %attend_back.1 = (f32[1024,512]{1,0:T(8,128)}, f32[1024,512]{1,0:T(8,128)}, bf16[1024,512]{1,0:T(8,128)(2,1)}, f32[1024,1]{1,0:T(8,128)S(1)}, f32[1024,1]{1,0:T(...) custom-call(bf16[1024,512]{1,0:T(8,128)(2,1)} %get-tuple-element.138.query_ref, ...), custom_call_target="tpu_custom_call" | custom-call | flops 21474836480 | bytes 20971520 | tf_op jit(solution)/shard_map/attend_back/pallas_call | solution.py:498
  824.3 19.5 %collective-permute-done.31 = bf16[256,2048]{1,0:T(8,128)(2,1)} collective-permute-done((bf16[256,2048]{1,0:T(8,128)(2,1)S(1)}, bf16[256,2048]{1,0:T(8,128)(2,1)}, u32[]{:S(2)}, u32[]{:S(2)}) %collective-permute-start.31) | collective-permute-done | bytes 1048608 | tf_op jit(solution)/shard_map/ppermute | solution.py:53
  886.9 19.7 %collective-permute-done.32 = bf16[256,2048]{1,0:T(8,128)(2,1)} collective-permute-done((bf16[256,2048]{1,0:T(8,128)(2,1)}, bf16[256,2048]{1,0:T(8,128)(2,1)}, u32[]{:S(2)}, u32[]{:S(2)}) %collective-permute-start.32) | collective-permute-done | bytes 1048608 | tf_op jit(solution)/shard_map/ppermute | solution.py:53
  939.3 17.9 %collective-permute-done.35 = bf16[256,2048]{1,0:T(8,128)(2,1)S(1)} collective-permute-done((bf16[256,2048]{1,0:T(8,128)(2,1)}, bf16[256,2048]{1,0:T(8,128)(2,1)S(1)}, u32[]{:S(2)}, u32[]{:S(2)}) %collective-permute-start.35) | collective-permute-done | bytes 1048608 | tf_op jit(solution)/shard_map/ppermute | solution.py:53
  (467 shorter events, 496.4 us)
Async XLA Ops:
  7.2 90.9 %all-gather.3.cloned.1.call-start = ((), (), s32[]{:S(2)}) async-start(), calls=%async_computation.18 | async-start | bytes 7077888 | tf_op jit(solution)/shard_map/all_gather | solution.py:600
  28.6 69.5 %all-to-all-start = ((bf16[8,2,48,2048]{3,2,1,0:T(8,128)(2,1)}), bf16[8,2,48,2048]{3,2,1,0:T(8,128)(2,1)}, u32[]{:S(2)}, u32[]{:S(2)}) async-start(bf16[8,2,48,2048]{3,2,1,0:T(8,128)(2,1)} %bitcast.2), calls=%async_computation | async-start | bytes 6291456 | tf_op jit(solution)/shard_map/all_to_all | solution.py:632
  33.1 125.5 %all-gather.5.cloned.1.call-start = ((), (), s32[]{:S(2)}) async-start(), calls=%async_computation.19 | async-start | bytes 2359296 | tf_op jit(solution)/shard_map/all_gather | solution.py:603
  125.6 52.1 %all-to-all-start.1 = ((bf16[8,2,48,2048]{3,2,1,0:T(8,128)(2,1)}), bf16[8,2,48,2048]{3,2,1,0:T(8,128)(2,1)}, u32[]{:S(2)}, u32[]{:S(2)}) async-start(bf16[8,2,48,2048]{3,2,1,0:T(8,128)(2,1)} %bitcast.165), calls=%async_computation.1 | async-start | bytes 6291456 | tf_op jit(solution)/shard_map/all_to_all | solution.py:632
  177.7 42.3 %all-to-all-start.2 = ((bf16[8,2,48,2048]{3,2,1,0:T(8,128)(2,1)}), bf16[8,2,48,2048]{3,2,1,0:T(8,128)(2,1)}, u32[]{:S(2)}, u32[]{:S(2)}) async-start(bf16[8,2,48,2048]{3,2,1,0:T(8,128)(2,1)} %bitcast.166), calls=%async_computation.2 | async-start | bytes 6291456 | tf_op jit(solution)/shard_map/all_to_all | solution.py:632
  250.7 44.5 %all-to-all-start.3 = ((bf16[8,2,48,2176]{3,2,1,0:T(8,128)(2,1)}), bf16[8,2,48,2176]{3,2,1,0:T(8,128)(2,1)}, u32[]{:S(2)}, u32[]{:S(2)}) async-start(bf16[8,2,48,2176]{3,2,1,0:T(8,128)(2,1)} %bitcast.163), calls=%async_computation.3 | async-start | bytes 6684672 | tf_op jit(solution)/shard_map/all_to_all | solution.py:632
  295.2 44.5 %all-to-all-start.4 = ((bf16[8,2,48,2176]{3,2,1,0:T(8,128)(2,1)}), bf16[8,2,48,2176]{3,2,1,0:T(8,128)(2,1)}, u32[]{:S(2)}, u32[]{:S(2)}) async-start(bf16[8,2,48,2176]{3,2,1,0:T(8,128)(2,1)} %bitcast.161), calls=%async_computation.4 | async-start | bytes 6684672 | tf_op jit(solution)/shard_map/all_to_all | solution.py:632
  339.7 44.5 %all-to-all-start.5 = ((bf16[8,2,48,2176]{3,2,1,0:T(8,128)(2,1)}), bf16[8,2,48,2176]{3,2,1,0:T(8,128)(2,1)}, u32[]{:S(2)}, u32[]{:S(2)}) async-start(bf16[8,2,48,2176]{3,2,1,0:T(8,128)(2,1)} %bitcast.162), calls=%async_computation.5 | async-start | bytes 6684672 | tf_op jit(solution)/shard_map/all_to_all | solution.py:632
  384.2 42.3 %all-to-all-start.6 = ((bf16[8,2,48,2048]{3,2,1,0:T(8,128)(2,1)}), bf16[8,2,48,2048]{3,2,1,0:T(8,128)(2,1)}, u32[]{:S(2)}, u32[]{:S(2)}) async-start(bf16[8,2,48,2048]{3,2,1,0:T(8,128)(2,1)} %bitcast.167), calls=%async_computation.6 | async-start | bytes 6291456 | tf_op jit(solution)/shard_map/all_to_all | solution.py:632
  426.5 44.5 %all-to-all-start.7 = ((bf16[8,2,48,2176]{3,2,1,0:T(8,128)(2,1)}), bf16[8,2,48,2176]{3,2,1,0:T(8,128)(2,1)}, u32[]{:S(2)}, u32[]{:S(2)}) async-start(bf16[8,2,48,2176]{3,2,1,0:T(8,128)(2,1)} %bitcast.164), calls=%async_computation.7 | async-start | bytes 6684672 | tf_op jit(solution)/shard_map/all_to_all | solution.py:632
  471.0 44.5 %all-to-all-start.8 = ((bf16[8,2,48,2176]{3,2,1,0:T(8,128)(2,1)}), bf16[8,2,48,2176]{3,2,1,0:T(8,128)(2,1)}, u32[]{:S(2)}, u32[]{:S(2)}) async-start(bf16[8,2,48,2176]{3,2,1,0:T(8,128)(2,1)} %get-tuple-element.114), calls=%async_computation.8 | async-start | bytes 6684672 | tf_op jit(solution)/shard_map/all_to_all | solution.py:632
  515.5 47.4 %all-to-all-start.9 = ((bf16[8,2,48,2176]{3,2,1,0:T(8,128)(2,1)}), bf16[8,2,48,2176]{3,2,1,0:T(8,128)(2,1)}, u32[]{:S(2)}, u32[]{:S(2)}) async-start(bf16[8,2,48,2176]{3,2,1,0:T(8,128)(2,1)} %get-tuple-element.120), calls=%async_computation.9 | async-start | bytes 6684672 | tf_op jit(solution)/shard_map/all_to_all | solution.py:632
  524.4 43.3 %collective-permute-start.18 = (bf16[256,2176]{1,0:T(8,128)(2,1)}, bf16[256,2176]{1,0:T(8,128)(2,1)}, u32[]{:S(2)}, u32[]{:S(2)}) collective-permute-start(bf16[256,2176]{1,0:T(8,128)(2,1)} %convolution_convert_fusion.5), channel_id=1, source_target_pairs={{0,1},{1,2},{2,3},{3,0},{4,5},{5,6},{6,7},{7,4},{8,9},{9,10},{10,1... | collective-permute-start | bytes 3342344 | tf_op jit(solution)/shard_map/ppermute | solution.py:53
  562.9 44.6 %all-to-all-start.10 = ((bf16[8,2,48,2176]{3,2,1,0:T(8,128)(2,1)}), bf16[8,2,48,2176]{3,2,1,0:T(8,128)(2,1)}, u32[]{:S(2)}, u32[]{:S(2)}) async-start(bf16[8,2,48,2176]{3,2,1,0:T(8,128)(2,1)} %get-tuple-element.126), calls=%async_computation.10 | async-start | bytes 6684672 | tf_op jit(solution)/shard_map/all_to_all | solution.py:632
  572.2 40.3 %collective-permute-start.19 = (bf16[256,2176]{1,0:T(8,128)(2,1)}, bf16[256,2176]{1,0:T(8,128)(2,1)}, u32[]{:S(2)}, u32[]{:S(2)}) collective-permute-start(bf16[256,2176]{1,0:T(8,128)(2,1)} %add_convert_fusion.1), channel_id=1, source_target_pairs={{0,1},{1,2},{2,3},{3,0},{4,5},{5,6},{6,7},{7,4},{8,9},{9,10},{10,1... | collective-permute-start | bytes 3342344 | tf_op jit(solution)/shard_map/ppermute | solution.py:53
  607.5 44.6 %all-to-all-start.11 = ((bf16[8,2,48,2176]{3,2,1,0:T(8,128)(2,1)}), bf16[8,2,48,2176]{3,2,1,0:T(8,128)(2,1)}, u32[]{:S(2)}, u32[]{:S(2)}) async-start(bf16[8,2,48,2176]{3,2,1,0:T(8,128)(2,1)} %get-tuple-element.133), calls=%async_computation.11 | async-start | bytes 6684672 | tf_op jit(solution)/shard_map/all_to_all | solution.py:632
  617.0 43.5 %collective-permute-start.20 = (bf16[256,2176]{1,0:T(8,128)(2,1)}, bf16[256,2176]{1,0:T(8,128)(2,1)S(1)}, u32[]{:S(2)}, u32[]{:S(2)}) collective-permute-start(bf16[256,2176]{1,0:T(8,128)(2,1)} %add_convert_fusion), channel_id=1, source_target_pairs={{0,1},{1,2},{2,3},{3,0},{4,5},{5,6},{6,7},{7,4},{8,9},{9,10},{10,1... | collective-permute-start | bytes 3342344 | tf_op jit(solution)/shard_map/ppermute | solution.py:53
  652.1 96.7 %all-to-all-start.12 = ((bf16[8,4,48,2048]{3,2,1,0:T(8,128)(2,1)}), bf16[8,4,48,2048]{3,2,1,0:T(8,128)(2,1)}, u32[]{:S(2)}, u32[]{:S(2)}) async-start(bf16[8,4,48,2048]{3,2,1,0:T(8,128)(2,1)} %expert_out.3), calls=%async_computation.12 | async-start | bytes 12582912 | tf_op jit(solution)/shard_map/all_to_all | solution.py:632
  756.3 42.7 %all-to-all-start.13 = ((bf16[8,2,48,2048]{3,2,1,0:T(8,128)(2,1)}), bf16[8,2,48,2048]{3,2,1,0:T(8,128)(2,1)}, u32[]{:S(2)}, u32[]{:S(2)}) async-start(bf16[8,2,48,2048]{3,2,1,0:T(8,128)(2,1)} %expert_out.4), calls=%async_computation.13 | async-start | bytes 6291456 | tf_op jit(solution)/shard_map/all_to_all | solution.py:632
  798.9 44.8 %all-to-all-start.14 = ((bf16[8,2,48,2048]{3,2,1,0:T(8,128)(2,1)}), bf16[8,2,48,2048]{3,2,1,0:T(8,128)(2,1)S(1)}, u32[]{:S(2)}, u32[]{:S(2)}) async-start(bf16[8,2,48,2048]{3,2,1,0:T(8,128)(2,1)} %expert_out.5), calls=%async_computation.14 | async-start | bytes 6291456 | tf_op jit(solution)/shard_map/all_to_all | solution.py:632
  877.9 39.5 %collective-permute-start.39 = (bf16[4,256,1536]{2,1,0:T(8,128)(2,1)}, bf16[4,256,1536]{2,1,0:T(8,128)(2,1)}, u32[]{:S(2)}, u32[]{:S(2)}) collective-permute-start(bf16[4,256,1536]{2,1,0:T(8,128)(2,1)} %dynamic-slice_bitcast_fusion), channel_id=1, source_target_pairs={{0,4},{4,0},{8,12},{12,8},{16,20},{20,16},{24,28},{28,24},{1,5},{5... | collective-permute-start | bytes 9437192 | tf_op jit(solution)/shard_map/ppermute | solution.py:874
  912.7 44.5 %collective-permute-start.35 = (bf16[256,2048]{1,0:T(8,128)(2,1)}, bf16[256,2048]{1,0:T(8,128)(2,1)S(1)}, u32[]{:S(2)}, u32[]{:S(2)}) collective-permute-start(bf16[256,2048]{1,0:T(8,128)(2,1)} %add_convert_fusion.2), channel_id=1, source_target_pairs={{0,1},{1,2},{2,3},{3,0},{4,5},{5,6},{6,7},{7,4},{8,9},{9,10},{10,1... | collective-permute-start | bytes 3145736 | tf_op jit(solution)/shard_map/ppermute | solution.py:53
  928.4 55.1 %all-to-all-start.17 = ((bf16[4,256,2048]{2,1,0:T(8,128)(2,1)}), bf16[4,256,2048]{2,1,0:T(8,128)(2,1)}, u32[]{:S(2)}, u32[]{:S(2)}) async-start(bf16[4,256,2048]{2,1,0:T(8,128)(2,1)} %pad_maximum_fusion), calls=%async_computation.17 | async-start | bytes 8388608 | tf_op jit(solution)/shard_map/all_to_all | solution.py:884
  939.1 40.2 %collective-permute-start.34 = (bf16[256,2048]{1,0:T(8,128)(2,1)}, bf16[256,2048]{1,0:T(8,128)(2,1)}, u32[]{:S(2)}, u32[]{:S(2)}) collective-permute-start(bf16[256,2048]{1,0:T(8,128)(2,1)} %add_convert_fusion.4), channel_id=1, source_target_pairs={{0,1},{1,2},{2,3},{3,0},{4,5},{5,6},{6,7},{7,4},{8,9},{9,10},{10,1... | collective-permute-start | bytes 3145736 | tf_op jit(solution)/shard_map/ppermute | solution.py:53
  (132 other events, 2139.5 us)
Sparse Core Ops, SparseCore 0:
  10.5 69.6 all-gather.2
  82.1 33.8 all-gather.4

commit v5 on v4

--- a/solution.py
+++ b/solution.py
@@ -848,6 +848,8 @@
         da_total = (da_came.astype(jnp.float32) + da_parts[back]).astype(jnp.bfloat16)
         if back == 2:
             da_second = da_total
+        if back == last:
+            da_total = after(da_total, early)
     moe = after(moe, da_came)
     for back in order[2:]:
         moe = shift(moe, "col").astype(jnp.float32) + out_shares[back]
@@ -855,7 +857,7 @@
             moe = moe.astype(jnp.bfloat16)
     output = (residual + moe).astype(jnp.bfloat16)
     grad_normal_a = shift(da_total, "col").astype(jnp.float32) + da_parts[0]
-    wqkv_local = first_t(seq_rows, after(grad_qkv, da_second, early)).astype(jnp.bfloat16)
+    wqkv_local = first_t(seq_rows, after(grad_qkv, da_second, homes[-1])).astype(jnp.bfloat16)
     attn_gain_local = (
         jnp.sum(wqkv.astype(jnp.float32) * wqkv_local.astype(jnp.float32), -1) / attn_gain
     )

time: 1010 us -> 1010 us (level)
    ppermute x39, waiting for transfers between devices: 291 us -> 304 us  [shift(): lax.ppermute(value, axis, [(i, (i + step) % count) for i in range(count)])]
  transfers between devices with their start and end apart: 61 -> 61, of which waited for: 35 -> 31; matrix products, arithmetic and copies ran while one was open for 18% -> 17% of each run, Pallas kernels for 25% -> 25%
where the time goes in v5:
time: 1010 us; the launch traced here: 1000 us
  waiting for transfers between devices  397 us (39%)
  Pallas kernels  252 us (25%)
  matrix products  123 us (12%)
  starting transfers between devices  114 us (11%)
  local copies, waits for them, and re-layouts  53.2 us (5%)
  other arithmetic  44.6 us (4%)
  between operations  16.3 us (2%)
    ppermute x39, waiting for transfers between devices, shift(): lax.ppermute(value, axis, [(i, (i + step) % count) for i in range(count)])  304 us
    all_to_all x17, waiting for transfers between devices, in_plane(): lax.all_to_all(table, 'row', split_axis=0, concat_axis=0, tiled=True)  91.3 us
    pallas_call x4, Pallas kernels, expert_core(): pl.pallas_call(expert_kernel, grid=(owned, tiles), in_specs=[packed_spec,...  83.9 us
    all_to_all x17, starting transfers between devices, in_plane(): lax.all_to_all(table, 'row', split_axis=0, concat_axis=0, tiled=True)  75.8 us
    dot_general x11, matrix products, first_t(): lax.dot_general(left, right, (((0,), (0,)), ((), ())), preferred_element_...  47.9 us
    pallas_call x2, Pallas kernels, in_grads(): pl.pallas_call(functools.partial(in_grads_kernel, count), grid=(owned, wi...  46.5 us
    pallas_call x4, Pallas kernels, down_t(): pl.pallas_call(down_t_kernel, grid=(owned, tiles), in_specs=[pl.BlockSpec...  35.1 us
    ppermute x39, starting transfers between devices, shift(): lax.ppermute(value, axis, [(i, (i + step) % count) for i in range(count)])  32.4 us
  transfers between devices with their start and end apart: 61, of which 31 were waited for; matrix products, arithmetic and copies ran while one was open for 17% of the time, Pallas kernels for 25%

profile of v5, /device:TPU:0, one launch (start us, length us, event | category | flops | bytes accessed | tf_op | source)
XLA Modules:
  0.0 999.9 jit_solution(4495120185782254189)
XLA Ops:
  47.8 23.7 %collective-permute-done.1 = bf16[256,2048]{1,0:T(8,128)(2,1)} collective-permute-done((bf16[256,2048]{1,0:T(8,128)(2,1)}, bf16[256,2048]{1,0:T(8,128)(2,1)}, u32[]{:S(2)}, u32[]{:S(2)}) %collective-permute-start.1) | collective-permute-done | bytes 1048608 | tf_op jit(solution)/shard_map/ppermute | solution.py:53
  80.6 15.3 %collective-permute-done.2 = bf16[256,2048]{1,0:T(8,128)(2,1)} collective-permute-done((bf16[256,2048]{1,0:T(8,128)(2,1)}, bf16[256,2048]{1,0:T(8,128)(2,1)}, u32[]{:S(2)}, u32[]{:S(2)}) %collective-permute-start.2) | collective-permute-done | bytes 1048608 | tf_op jit(solution)/shard_map/ppermute | solution.py:53
  131.1 13.1 %attend.1 = (bf16[1024,512]{1,0:T(8,128)(2,1)}, bf16[1024,512]{1,0:T(8,128)(2,1)}, bf16[1024,512]{1,0:T(8,128)(2,1)}, bf16[1024,512]{1,0:T(8,128)(2,1)}, f32[4,1,1024]{2,1,0:T(1,128)S(1)}) custom-call(f32[1024,1536]{1,0:T(8,128)} %copy-done.25, f32[1024,1536]{1,0:T(8,128)} %copy-done.25, f32[1024,1536]{1,0:T(8,128)} %copy-done.25, ...), custom_call_target="tpu_custom_call" | custom-call | flops 12884901888 | bytes 10485760 | tf_op jit(solution)/shard_map/attend/pallas_call | solution.py:394
  144.2 14.4 %collective-permute-done.7 = bf16[256,2048]{1,0:T(8,128)(2,1)} collective-permute-done((bf16[256,2048]{1,0:T(8,128)(2,1)}, bf16[256,2048]{1,0:T(8,128)(2,1)}, u32[]{:S(2)}, u32[]{:S(2)}) %collective-permute-start.7) | collective-permute-done | bytes 1048608 | tf_op jit(solution)/shard_map/ppermute | solution.py:53
  200.3 16.1 %collective-permute-done.9 = bf16[256,2048]{1,0:T(8,128)(2,1)S(1)} collective-permute-done((bf16[256,2048]{1,0:T(8,128)(2,1)S(1)}, bf16[256,2048]{1,0:T(8,128)(2,1)S(1)}, u32[]{:S(2)}, u32[]{:S(2)}) %collective-permute-start.9) | collective-permute-done | bytes 1048608 | tf_op jit(solution)/shard_map/ppermute | solution.py:53
  220.1 22.4 %collective-permute-done.11 = bf16[256,2048]{1,0:T(8,128)(2,1)} collective-permute-done((bf16[256,2048]{1,0:T(8,128)(2,1)}, bf16[256,2048]{1,0:T(8,128)(2,1)}, u32[]{:S(2)}, u32[]{:S(2)}) %collective-permute-start.11) | collective-permute-done | bytes 1048608 | tf_op jit(solution)/shard_map/ppermute | solution.py:53
  264.5 19.8 %collective-permute-done.13 = bf16[256,2176]{1,0:T(8,128)(2,1)S(1)} collective-permute-done((bf16[256,2176]{1,0:T(8,128)(2,1)S(1)}, bf16[256,2176]{1,0:T(8,128)(2,1)S(1)}, u32[]{:S(2)}, u32[]{:S(2)}) %collective-permute-start.13) | collective-permute-done | bytes 1114144 | tf_op jit(solution)/shard_map/ppermute | solution.py:53
  300.1 21.0 %expert_core.5 = (bf16[8,2,48,2176]{3,2,1,0:T(8,128)(2,1)}, bf16[2,384,1024]{2,1,0:T(8,128)(2,1)S(1)}, bf16[2,384,1024]{2,1,0:T(8,128)(2,1)}, bf16[2,384,1024]{2,1,0:T(8,128)(2,1)}) custom-call(bf16[8,2,48,2176]{3,2,1,0:T(8,128)(2,1)} %all-to-all-done.3.rows_ref.refs_0_, bf16[2048,2048]{1,0:T(8,128)(2,1)} %gate_ref.7, bf16[2048,2048]{1,0:T(8,128)(2,1)} %up_ref.7, ...), custom_call_target="tpu_custom_call" | custom-call | flops 12884901888 | bytes 39845888 | tf_op jit(solution)/shard_map/expert_core/pallas_call | solution.py:218
  344.3 21.0 %expert_core.4 = (bf16[8,2,48,2176]{3,2,1,0:T(8,128)(2,1)}, bf16[2,384,1024]{2,1,0:T(8,128)(2,1)S(1)}, bf16[2,384,1024]{2,1,0:T(8,128)(2,1)}, bf16[2,384,1024]{2,1,0:T(8,128)(2,1)}) custom-call(bf16[8,2,48,2176]{3,2,1,0:T(8,128)(2,1)} %all-to-all-done.4.rows_ref.refs_1_, bf16[2048,2048]{1,0:T(8,128)(2,1)} %gate_ref.7, bf16[2048,2048]{1,0:T(8,128)(2,1)} %up_ref.7, ...), custom_call_target="tpu_custom_call" | custom-call | flops 12884901888 | bytes 39845888 | tf_op jit(solution)/shard_map/expert_core/pallas_call | solution.py:218
  388.9 20.9 %expert_core.6 = (bf16[8,2,48,2176]{3,2,1,0:T(8,128)(2,1)}, bf16[2,384,1024]{2,1,0:T(8,128)(2,1)S(1)}, bf16[2,384,1024]{2,1,0:T(8,128)(2,1)}, bf16[2,384,1024]{2,1,0:T(8,128)(2,1)}) custom-call(bf16[8,2,48,2176]{3,2,1,0:T(8,128)(2,1)} %all-to-all-done.5.rows_ref.refs_2_, bf16[2048,2048]{1,0:T(8,128)(2,1)} %gate_ref.7, bf16[2048,2048]{1,0:T(8,128)(2,1)} %up_ref.7, ...), custom_call_target="tpu_custom_call" | custom-call | flops 12884901888 | bytes 39845888 | tf_op jit(solution)/shard_map/expert_core/pallas_call | solution.py:218
  439.7 31.3 %all-to-all-done.7.rows_ref.refs_3_ = bf16[8,2,48,2176]{3,2,1,0:T(8,128)(2,1)} async-done(((bf16[8,2,48,2176]{3,2,1,0:T(8,128)(2,1)}), bf16[8,2,48,2176]{3,2,1,0:T(8,128)(2,1)}, u32[]{:S(2)}, u32[]{:S(2)}) %all-to-all-start.7) | async-done | bytes 3342368 | tf_op jit(solution)/shard_map/all_to_all | solution.py:632
  475.5 21.0 %expert_core.7 = (bf16[8,2,48,2176]{3,2,1,0:T(8,128)(2,1)}, bf16[2,384,1024]{2,1,0:T(8,128)(2,1)S(1)}, bf16[2,384,1024]{2,1,0:T(8,128)(2,1)}, bf16[2,384,1024]{2,1,0:T(8,128)(2,1)}) custom-call(bf16[8,2,48,2176]{3,2,1,0:T(8,128)(2,1)} %all-to-all-done.7.rows_ref.refs_3_, bf16[2048,2048]{1,0:T(8,128)(2,1)} %gate_ref.7, bf16[2048,2048]{1,0:T(8,128)(2,1)} %up_ref.7, ...), custom_call_target="tpu_custom_call" | custom-call | flops 12884901888 | bytes 39845888 | tf_op jit(solution)/shard_map/expert_core/pallas_call | solution.py:218
  496.5 19.0 %all-to-all-done.8 = bf16[8,2,48,2176]{3,2,1,0:T(8,128)(2,1)} async-done(((bf16[8,2,48,2176]{3,2,1,0:T(8,128)(2,1)}), bf16[8,2,48,2176]{3,2,1,0:T(8,128)(2,1)}, u32[]{:S(2)}, u32[]{:S(2)}) %all-to-all-start.8) | async-done | bytes 3342368 | tf_op jit(solution)/shard_map/all_to_all | solution.py:632
  524.6 23.3 %in_grads.2 = f32[2048,2048]{1,0:T(8,128)} custom-call(bf16[8,2,48,2176]{3,2,1,0:T(8,128)(2,1)} %all-to-all-done.3.rows_ref.refs_0_, bf16[8,2,48,2176]{3,2,1,0:T(8,128)(2,1)} %all-to-all-done.4.rows_ref.refs_1_, bf16[8,2,48,2176]{3,2,1,0:T(8,128)(2,1)} %all-to-all-done.5.rows_ref.refs_2_, bf16[8,2,48,2176]{3,2,1,0:T(8,128)(2,1)} %all-to-all-done.7.rows_ref.refs_3_, ...), custom_call_target="tpu_custom_call" | custom-call | flops 12884901888 | bytes 16777216 | tf_op jit(solution)/shard_map/in_grads/pallas_call | solution.py:296
  547.9 15.0 %expert_out.3 = bf16[8,4,48,2048]{3,2,1,0:T(8,128)(2,1)} custom-call(bf16[2,384,1024]{2,1,0:T(8,128)(2,1)S(1)} %copy-done.13, bf16[2,384,1024]{2,1,0:T(8,128)(2,1)} %copy-done.14, bf16[2048,2048]{1,0:T(8,128)(2,1)} %refs_1_.3), custom_call_target="tpu_custom_call" | custom-call | flops 6442450944 | bytes 23068672 | tf_op jit(solution)/shard_map/expert_out/pallas_call | solution.py:264
  572.3 23.2 %in_grads.3 = f32[2048,2048]{1,0:T(8,128)} custom-call(bf16[8,2,48,2176]{3,2,1,0:T(8,128)(2,1)} %all-to-all-done.3.rows_ref.refs_0_, bf16[8,2,48,2176]{3,2,1,0:T(8,128)(2,1)} %all-to-all-done.4.rows_ref.refs_1_, bf16[8,2,48,2176]{3,2,1,0:T(8,128)(2,1)} %all-to-all-done.5.rows_ref.refs_2_, bf16[8,2,48,2176]{3,2,1,0:T(8,128)(2,1)} %all-to-all-done.7.rows_ref.refs_3_, ...), custom_call_target="tpu_custom_call" | custom-call | flops 12884901888 | bytes 16777216 | tf_op jit(solution)/shard_map/in_grads/pallas_call | solution.py:296
  617.0 26.0 %down_grads.1 = f32[2048,2048]{1,0:T(8,128)} custom-call(bf16[2,384,1024]{2,1,0:T(8,128)(2,1)S(1)} %get-tuple-element.136.refs_0_, bf16[2,384,1024]{2,1,0:T(8,128)(2,1)} %copy-done.12, bf16[2,384,1024]{2,1,0:T(8,128)(2,1)} %copy-done.14, bf16[2,384,1024]{2,1,0:T(8,128)(2,1)} %copy-done.1, bf16[8,2,48,2048]{3,2,1,0:T(8,128)(2,1)} %all-to-all-done.grad_ref.refs_4_, ...), custom_call_target="tpu_custom_call" | custom-call | flops 12884901888 | bytes 16777216 | tf_op jit(solution)/shard_map/down_grads/pallas_call | solution.py:328
  667.8 25.6 %collective-permute-done.21 = bf16[256,2048]{1,0:T(8,128)(2,1)} collective-permute-done((bf16[256,2048]{1,0:T(8,128)(2,1)S(1)}, bf16[256,2048]{1,0:T(8,128)(2,1)}, u32[]{:S(2)}, u32[]{:S(2)}) %collective-permute-start.21) | collective-permute-done | bytes 1048608 | tf_op jit(solution)/shard_map/ppermute | solution.py:53
  700.5 20.0 %collective-permute-done.22 = bf16[256,2048]{1,0:T(8,128)(2,1)} collective-permute-done((bf16[256,2048]{1,0:T(8,128)(2,1)}, bf16[256,2048]{1,0:T(8,128)(2,1)}, u32[]{:S(2)}, u32[]{:S(2)}) %collective-permute-start.22) | collective-permute-done | bytes 1048608 | tf_op jit(solution)/shard_map/ppermute | solution.py:53
  729.3 17.2 %collective-permute-done.23 = bf16[256,2048]{1,0:T(8,128)(2,1)S(1)} collective-permute-done((bf16[256,2048]{1,0:T(8,128)(2,1)}, bf16[256,2048]{1,0:T(8,128)(2,1)S(1)}, u32[]{:S(2)}, u32[]{:S(2)}) %collective-permute-start.23) | collective-permute-done | bytes 1048608 | tf_op jit(solution)/shard_map/ppermute | solution.py:53
  761.2 17.1 %attend_back.1 = (f32[1024,512]{1,0:T(8,128)}, f32[1024,512]{1,0:T(8,128)}, bf16[1024,512]{1,0:T(8,128)(2,1)}, f32[1024,1]{1,0:T(8,128)S(1)}, f32[1024,1]{1,0:T(...) custom-call(bf16[1024,512]{1,0:T(8,128)(2,1)} %get-tuple-element.139.query_ref, ...), custom_call_target="tpu_custom_call" | custom-call | flops 21474836480 | bytes 20971520 | tf_op jit(solution)/shard_map/attend_back/pallas_call | solution.py:498
  820.3 19.3 %collective-permute-done.31 = bf16[256,2048]{1,0:T(8,128)(2,1)S(1)} collective-permute-done((bf16[256,2048]{1,0:T(8,128)(2,1)S(1)}, bf16[256,2048]{1,0:T(8,128)(2,1)S(1)}, u32[]{:S(2)}, u32[]{:S(2)}) %collective-permute-start.31) | collective-permute-done | bytes 1048608 | tf_op jit(solution)/shard_map/ppermute | solution.py:53
  864.1 24.0 %collective-permute-done.32 = bf16[256,2048]{1,0:T(8,128)(2,1)} collective-permute-done((bf16[256,2048]{1,0:T(8,128)(2,1)S(1)}, bf16[256,2048]{1,0:T(8,128)(2,1)}, u32[]{:S(2)}, u32[]{:S(2)}) %collective-permute-start.32) | collective-permute-done | bytes 1048608 | tf_op jit(solution)/shard_map/ppermute | solution.py:53
  893.6 21.4 %collective-permute-done.33 = bf16[256,2048]{1,0:T(8,128)(2,1)} collective-permute-done((bf16[256,2048]{1,0:T(8,128)(2,1)}, bf16[256,2048]{1,0:T(8,128)(2,1)}, u32[]{:S(2)}, u32[]{:S(2)}) %collective-permute-start.33) | collective-permute-done | bytes 1048608 | tf_op jit(solution)/shard_map/ppermute | solution.py:53
  (472 shorter events, 492.6 us)
Async XLA Ops:
  7.2 91.0 %all-gather.3.cloned.1.call-start = ((), (), s32[]{:S(2)}) async-start(), calls=%async_computation.18 | async-start | bytes 7077888 | tf_op jit(solution)/shard_map/all_gather | solution.py:600
  28.6 69.5 %all-to-all-start = ((bf16[8,2,48,2048]{3,2,1,0:T(8,128)(2,1)}), bf16[8,2,48,2048]{3,2,1,0:T(8,128)(2,1)}, u32[]{:S(2)}, u32[]{:S(2)}) async-start(bf16[8,2,48,2048]{3,2,1,0:T(8,128)(2,1)} %bitcast.2), calls=%async_computation | async-start | bytes 6291456 | tf_op jit(solution)/shard_map/all_to_all | solution.py:632
  33.1 125.5 %all-gather.5.cloned.1.call-start = ((), (), s32[]{:S(2)}) async-start(), calls=%async_computation.19 | async-start | bytes 2359296 | tf_op jit(solution)/shard_map/all_gather | solution.py:603
  125.6 52.2 %all-to-all-start.1 = ((bf16[8,2,48,2048]{3,2,1,0:T(8,128)(2,1)}), bf16[8,2,48,2048]{3,2,1,0:T(8,128)(2,1)}, u32[]{:S(2)}, u32[]{:S(2)}) async-start(bf16[8,2,48,2048]{3,2,1,0:T(8,128)(2,1)} %bitcast.165), calls=%async_computation.1 | async-start | bytes 6291456 | tf_op jit(solution)/shard_map/all_to_all | solution.py:632
  177.8 42.4 %all-to-all-start.2 = ((bf16[8,2,48,2048]{3,2,1,0:T(8,128)(2,1)}), bf16[8,2,48,2048]{3,2,1,0:T(8,128)(2,1)}, u32[]{:S(2)}, u32[]{:S(2)}) async-start(bf16[8,2,48,2048]{3,2,1,0:T(8,128)(2,1)} %bitcast.166), calls=%async_computation.2 | async-start | bytes 6291456 | tf_op jit(solution)/shard_map/all_to_all | solution.py:632
  250.8 44.5 %all-to-all-start.3 = ((bf16[8,2,48,2176]{3,2,1,0:T(8,128)(2,1)}), bf16[8,2,48,2176]{3,2,1,0:T(8,128)(2,1)}, u32[]{:S(2)}, u32[]{:S(2)}) async-start(bf16[8,2,48,2176]{3,2,1,0:T(8,128)(2,1)} %bitcast.163), calls=%async_computation.3 | async-start | bytes 6684672 | tf_op jit(solution)/shard_map/all_to_all | solution.py:632
  295.2 44.5 %all-to-all-start.4 = ((bf16[8,2,48,2176]{3,2,1,0:T(8,128)(2,1)}), bf16[8,2,48,2176]{3,2,1,0:T(8,128)(2,1)}, u32[]{:S(2)}, u32[]{:S(2)}) async-start(bf16[8,2,48,2176]{3,2,1,0:T(8,128)(2,1)} %bitcast.161), calls=%async_computation.4 | async-start | bytes 6684672 | tf_op jit(solution)/shard_map/all_to_all | solution.py:632
  339.7 44.5 %all-to-all-start.5 = ((bf16[8,2,48,2176]{3,2,1,0:T(8,128)(2,1)}), bf16[8,2,48,2176]{3,2,1,0:T(8,128)(2,1)}, u32[]{:S(2)}, u32[]{:S(2)}) async-start(bf16[8,2,48,2176]{3,2,1,0:T(8,128)(2,1)} %bitcast.162), calls=%async_computation.5 | async-start | bytes 6684672 | tf_op jit(solution)/shard_map/all_to_all | solution.py:632
  384.2 42.3 %all-to-all-start.6 = ((bf16[8,2,48,2048]{3,2,1,0:T(8,128)(2,1)}), bf16[8,2,48,2048]{3,2,1,0:T(8,128)(2,1)}, u32[]{:S(2)}, u32[]{:S(2)}) async-start(bf16[8,2,48,2048]{3,2,1,0:T(8,128)(2,1)} %bitcast.167), calls=%async_computation.6 | async-start | bytes 6291456 | tf_op jit(solution)/shard_map/all_to_all | solution.py:632
  426.5 44.5 %all-to-all-start.7 = ((bf16[8,2,48,2176]{3,2,1,0:T(8,128)(2,1)}), bf16[8,2,48,2176]{3,2,1,0:T(8,128)(2,1)}, u32[]{:S(2)}, u32[]{:S(2)}) async-start(bf16[8,2,48,2176]{3,2,1,0:T(8,128)(2,1)} %bitcast.164), calls=%async_computation.7 | async-start | bytes 6684672 | tf_op jit(solution)/shard_map/all_to_all | solution.py:632
  471.0 44.5 %all-to-all-start.8 = ((bf16[8,2,48,2176]{3,2,1,0:T(8,128)(2,1)}), bf16[8,2,48,2176]{3,2,1,0:T(8,128)(2,1)}, u32[]{:S(2)}, u32[]{:S(2)}) async-start(bf16[8,2,48,2176]{3,2,1,0:T(8,128)(2,1)} %get-tuple-element.115), calls=%async_computation.8 | async-start | bytes 6684672 | tf_op jit(solution)/shard_map/all_to_all | solution.py:632
  515.5 47.4 %all-to-all-start.9 = ((bf16[8,2,48,2176]{3,2,1,0:T(8,128)(2,1)}), bf16[8,2,48,2176]{3,2,1,0:T(8,128)(2,1)}, u32[]{:S(2)}, u32[]{:S(2)}) async-start(bf16[8,2,48,2176]{3,2,1,0:T(8,128)(2,1)} %get-tuple-element.121), calls=%async_computation.9 | async-start | bytes 6684672 | tf_op jit(solution)/shard_map/all_to_all | solution.py:632
  524.4 43.4 %collective-permute-start.18 = (bf16[256,2176]{1,0:T(8,128)(2,1)}, bf16[256,2176]{1,0:T(8,128)(2,1)}, u32[]{:S(2)}, u32[]{:S(2)}) collective-permute-start(bf16[256,2176]{1,0:T(8,128)(2,1)} %convolution_convert_fusion.5), channel_id=1, source_target_pairs={{0,1},{1,2},{2,3},{3,0},{4,5},{5,6},{6,7},{7,4},{8,9},{9,10},{10,1... | collective-permute-start | bytes 3342344 | tf_op jit(solution)/shard_map/ppermute | solution.py:53
  562.9 44.7 %all-to-all-start.10 = ((bf16[8,2,48,2176]{3,2,1,0:T(8,128)(2,1)}), bf16[8,2,48,2176]{3,2,1,0:T(8,128)(2,1)}, u32[]{:S(2)}, u32[]{:S(2)}) async-start(bf16[8,2,48,2176]{3,2,1,0:T(8,128)(2,1)} %get-tuple-element.127), calls=%async_computation.10 | async-start | bytes 6684672 | tf_op jit(solution)/shard_map/all_to_all | solution.py:632
  572.3 40.3 %collective-permute-start.19 = (bf16[256,2176]{1,0:T(8,128)(2,1)}, bf16[256,2176]{1,0:T(8,128)(2,1)}, u32[]{:S(2)}, u32[]{:S(2)}) collective-permute-start(bf16[256,2176]{1,0:T(8,128)(2,1)} %add_convert_fusion.1), channel_id=1, source_target_pairs={{0,1},{1,2},{2,3},{3,0},{4,5},{5,6},{6,7},{7,4},{8,9},{9,10},{10,1... | collective-permute-start | bytes 3342344 | tf_op jit(solution)/shard_map/ppermute | solution.py:53
  607.6 44.6 %all-to-all-start.11 = ((bf16[8,2,48,2176]{3,2,1,0:T(8,128)(2,1)}), bf16[8,2,48,2176]{3,2,1,0:T(8,128)(2,1)}, u32[]{:S(2)}, u32[]{:S(2)}) async-start(bf16[8,2,48,2176]{3,2,1,0:T(8,128)(2,1)} %get-tuple-element.134), calls=%async_computation.11 | async-start | bytes 6684672 | tf_op jit(solution)/shard_map/all_to_all | solution.py:632
  617.0 43.5 %collective-permute-start.20 = (bf16[256,2176]{1,0:T(8,128)(2,1)}, bf16[256,2176]{1,0:T(8,128)(2,1)S(1)}, u32[]{:S(2)}, u32[]{:S(2)}) collective-permute-start(bf16[256,2176]{1,0:T(8,128)(2,1)} %add_convert_fusion), channel_id=1, source_target_pairs={{0,1},{1,2},{2,3},{3,0},{4,5},{5,6},{6,7},{7,4},{8,9},{9,10},{10,1... | collective-permute-start | bytes 3342344 | tf_op jit(solution)/shard_map/ppermute | solution.py:53
  652.2 96.7 %all-to-all-start.12 = ((bf16[8,4,48,2048]{3,2,1,0:T(8,128)(2,1)}), bf16[8,4,48,2048]{3,2,1,0:T(8,128)(2,1)}, u32[]{:S(2)}, u32[]{:S(2)}) async-start(bf16[8,4,48,2048]{3,2,1,0:T(8,128)(2,1)} %expert_out.3), calls=%async_computation.12 | async-start | bytes 12582912 | tf_op jit(solution)/shard_map/all_to_all | solution.py:632
  756.4 45.1 %all-to-all-start.13 = ((bf16[8,2,48,2048]{3,2,1,0:T(8,128)(2,1)}), bf16[8,2,48,2048]{3,2,1,0:T(8,128)(2,1)}, u32[]{:S(2)}, u32[]{:S(2)}) async-start(bf16[8,2,48,2048]{3,2,1,0:T(8,128)(2,1)} %expert_out.4), calls=%async_computation.13 | async-start | bytes 6291456 | tf_op jit(solution)/shard_map/all_to_all | solution.py:632
  801.5 42.1 %all-to-all-start.14 = ((bf16[8,2,48,2048]{3,2,1,0:T(8,128)(2,1)}), bf16[8,2,48,2048]{3,2,1,0:T(8,128)(2,1)S(1)}, u32[]{:S(2)}, u32[]{:S(2)}) async-start(bf16[8,2,48,2048]{3,2,1,0:T(8,128)(2,1)} %expert_out.5), calls=%async_computation.14 | async-start | bytes 6291456 | tf_op jit(solution)/shard_map/all_to_all | solution.py:632
  860.6 63.9 %collective-permute-start.39 = (bf16[4,256,1536]{2,1,0:T(8,128)(2,1)}, bf16[4,256,1536]{2,1,0:T(8,128)(2,1)}, u32[]{:S(2)}, u32[]{:S(2)}) collective-permute-start(bf16[4,256,1536]{2,1,0:T(8,128)(2,1)} %dynamic-slice_bitcast_fusion), channel_id=1, source_target_pairs={{0,4},{4,0},{8,12},{12,8},{16,20},{20,16},{24,28},{28,24},{1,5},{5... | collective-permute-start | bytes 9437192 | tf_op jit(solution)/shard_map/ppermute | solution.py:876
  860.7 31.4 %collective-permute-start.40 = (bf16[4,256,512]{2,1,0:T(8,128)(2,1)S(1)}, bf16[4,256,512]{2,1,0:T(8,128)(2,1)S(1)}, u32[]{:S(2)}, u32[]{:S(2)}) collective-permute-start(bf16[4,256,512]{2,1,0:T(8,128)(2,1)S(1)} %dynamic-slice_bitcast_fusion.1), channel_id=1, source_target_pairs={{0,4},{4,0},{8,12},{12,8},{16,20},{20,16},{24,28},{28,24},{1,5},{5... | collective-permute-start | bytes 3145736 | tf_op jit(solution)/shard_map/ppermute | solution.py:876
  919.1 53.3 %collective-permute-start.34 = (bf16[256,2048]{1,0:T(8,128)(2,1)}, bf16[256,2048]{1,0:T(8,128)(2,1)}, u32[]{:S(2)}, u32[]{:S(2)}) collective-permute-start(bf16[256,2048]{1,0:T(8,128)(2,1)} %add_convert_fusion.4), channel_id=1, source_target_pairs={{0,1},{1,2},{2,3},{3,0},{4,5},{5,6},{6,7},{7,4},{8,9},{9,10},{10,1... | collective-permute-start | bytes 3145736 | tf_op jit(solution)/shard_map/ppermute | solution.py:53
  935.6 51.6 %all-to-all-start.17 = ((bf16[4,256,2048]{2,1,0:T(8,128)(2,1)}), bf16[4,256,2048]{2,1,0:T(8,128)(2,1)}, u32[]{:S(2)}, u32[]{:S(2)}) async-start(bf16[4,256,2048]{2,1,0:T(8,128)(2,1)} %pad_maximum_fusion), calls=%async_computation.17 | async-start | bytes 8388608 | tf_op jit(solution)/shard_map/all_to_all | solution.py:886
  (134 other events, 2226.7 us)
Sparse Core Ops, SparseCore 0:
  10.5 69.7 all-gather.2
  82.1 33.8 all-gather.4
